TPU v7x, 32 devices: a whole 2x2x4 slice. The times are simulated.
32 devices in a mesh: row: 4 (over y, x), seq: 8 (over z, core).
Axes of the slice: x: 2, y: 2, z: 4, core: 2. Of those that a mesh axis runs over, the one named last changes fastest.
Arguments:
- tokens: bfloat16 [4, 1024, 2048], P('row', 'seq'), may hold values from -6 to 6
- cotangent: bfloat16 [4, 1024, 2048], P('row', 'seq'), may hold values from -6 to 6
- modality: int32 [4, 1024], P(None, 'seq'), may hold values from 0 to 2
- starts: int32 [4, 1024], P(None, 'seq'), may hold values from 0 to 1, as said below
- row_lengths: int32 [4], replicated, may hold values from 960 to 1024
- norm_gain: bfloat16 [2048], P('seq'), may hold values from 0.5 to 1.5
- in_x_weight: bfloat16 [2048, 3, 4096], P('seq', None, 'row'), may hold values from -0.125 to 0.125
- in_z_weight: bfloat16 [2048, 3, 4096], P('seq', None, 'row'), may hold values from -0.125 to 0.125
- xdt_weight: bfloat16 [4096, 3, 128], P(('row', 'seq')), may hold values from -0.09375 to 0.09375
- xbc_weight: bfloat16 [32, 3, 4096], P(None, None, ('row', 'seq')), may hold values from -0.09375 to 0.09375
- dt_weight: bfloat16 [128, 3, 4096], P(None, None, ('row', 'seq')), may hold values from -0.5 to 0.5
- dt_bias: bfloat16 [3, 4096], P(None, ('row', 'seq')), may hold values from -11 to -2
- conv_weight: bfloat16 [4, 4096], P(None, ('row', 'seq')), may hold values from -3 to 3
- conv_bias: bfloat16 [4096], P(('row', 'seq')), may hold values from -3 to 3
- log_rates: bfloat16 [16, 4096], P(None, ('row', 'seq')), may hold values from 0 to 2.765625
- skip_gain: bfloat16 [4096], P(('row', 'seq')), may hold values from 0.5 to 1.5
- out_weight: bfloat16 [2048, 3, 4096], P('seq', None, 'row'), may hold values from -0.1875 to 0.1875
Outputs:
- block_out: bfloat16 [4, 1024, 2048], P('row', 'seq')
- tokens_grad: bfloat16 [4, 1024, 2048], P('row', 'seq')
- norm_gain_grad: float32 [2048], P('seq')
- in_x_grad: float32 [2048, 3, 4096], P('seq', None, 'row')
- in_z_grad: float32 [2048, 3, 4096], P('seq', None, 'row')
- xdt_grad: float32 [4096, 3, 128], P(('row', 'seq'))
- xbc_grad: float32 [32, 3, 4096], P(None, None, ('row', 'seq'))
- dt_weight_grad: float32 [128, 3, 4096], P(None, None, ('row', 'seq'))
- dt_bias_grad: float32 [3, 4096], P(None, ('row', 'seq'))
- conv_weight_grad: float32 [4, 4096], P(None, ('row', 'seq'))
- conv_bias_grad: float32 [4096], P(('row', 'seq'))
- log_rates_grad: float32 [16, 4096], P(None, ('row', 'seq'))
- skip_gain_grad: float32 [4096], P(('row', 'seq'))
- out_weight_grad: float32 [2048, 3, 4096], P('seq', None, 'row')
Inputs may be any that keep to these rules, and one draw needn't show every extreme that they name: `starts`: the first position of every row is 1.
All inputs are finite; a program needn't handle non-finite values.
Results may differ from a plain program's by a relative error of at most 0.013.
Values may be sent and summed in bfloat16 or wider, within the bound.
No kernel may reach another device: no remote copies, remote signals or barrier semaphores. Data moves between devices by JAX's collectives and lax.ppermute only.
A program may use at most 320 MiB of HBM per device.

v0:
```python
import functools
import math

import jax
import jax.numpy as jnp
from jax import lax
from jax.experimental import pallas as pl
from jax.experimental.pallas import tpu as pltpu
from jax.sharding import Mesh
from jax.sharding import PartitionSpec as P

epsilon = 1e-05
row_axes = ("y", "x")
group_axes = ("z", "c")
seq_axes = ("o", "z", "c")
team_axes = ("y", "x", "z", "c")
bf16 = jnp.bfloat16
f32 = jnp.float32
lanes = 128
huge_step = 1e6
vmem_bytes = 48 * 1024 * 1024


def apply_silu(values):
    return values * jax.nn.sigmoid(values)


def silu_slope(values):
    sigmoid_of = jax.nn.sigmoid(values)
    return sigmoid_of * (1.0 + values * (1.0 - sigmoid_of))


def softplus(values):
    tail = jnp.exp(-jnp.abs(values))
    series = tail * (1.0 + tail * (-1 / 2 + tail * (1 / 3 + tail * (-1 / 4 + tail * (1 / 5 - tail * (1 / 6))))))
    return jnp.maximum(values, 0.0) + jnp.where(tail < 0.05, series, jnp.log(1.0 + tail))


def dot(a, b, contract):
    return lax.dot_general(a, b, (contract, ((), ())), preferred_element_type=f32)


def chosen(values, label, mods, axis=1):
    wide = values.shape[axis] // mods
    parts = [lax.slice_in_dim(values, m * wide, (m + 1) * wide, axis=axis) for m in range(mods)]
    picked = parts[0]
    for m in range(1, mods):
        picked = jnp.where(label == m, parts[m], picked)
    return picked


def placed(values, label, mods, axis=1):
    wide = values.astype(f32)
    return jnp.concatenate([jnp.where(label == m, wide, 0.0) for m in range(mods)], axis=axis).astype(values.dtype)


start_column, label_column, fact_columns = 3, 4, 8


def columns_of(facts):
    missing = facts.shape[1] - facts.shape[0]
    return jnp.transpose(jnp.concatenate([facts, jnp.zeros((missing, facts.shape[1]), f32)], axis=0))


def label_column_of(facts_ref):
    return jnp.concatenate(
        [columns_of(facts_ref[j])[:, label_column : label_column + 1] for j in range(facts_ref.shape[0])], axis=0
    )


params = functools.partial(pltpu.CompilerParams, vmem_limit_bytes=vmem_bytes)


def everything(array):
    return pl.BlockSpec(array.shape, lambda i, rank=len(array.shape): (0,) * rank)


def scalars():
    return pl.BlockSpec(memory_space=pltpu.SMEM)


def shape(dims, dtype):
    return jax.ShapeDtypeStruct(dims, dtype)


def cost(flops, nbytes):
    return pl.CostEstimate(flops=int(flops), bytes_accessed=int(nbytes), transcendentals=0)


def assemble(weight_ref, whole):
    pieces, mods, some, wide = weight_ref.shape
    for i in range(pieces):
        for m in range(mods):
            whole[i * some : (i + 1) * some, m * wide : (m + 1) * wide] = weight_ref[i, m]


def lead_kernel(mods, places, x_ref, facts_ref, weight_ref, out_ref, whole):
    @pl.when(pl.program_id(0) == 0)
    def _():
        assemble(weight_ref, whole)

    some, here, wide = x_ref.shape
    label = label_column_of(facts_ref)
    picked = chosen(dot(x_ref[...].reshape(some * here, wide), whole[...], ((1,), (0,))), label, mods)
    for j in range(some):
        out_ref[places[pl.program_id(0) * some + j]] = picked[j * here : (j + 1) * here].astype(out_ref.dtype)


def lead_product(places, x, facts, weight, dtype):
    pieces, here, wide = x.shape
    groups, mods, some, mine = weight.shape
    outs = [shape((pieces, here, mine), dtype), shape((groups * some, mods * mine), bf16)]
    return pl.pallas_call(
        functools.partial(lead_kernel, mods),
        grid=(pieces // 4,),
        in_specs=[
            scalars(),
            pl.BlockSpec((4, here, wide), lambda i: (i, 0, 0)),
            pl.BlockSpec((4, fact_columns, here), lambda i: (i, 0, 0)),
            everything(weight),
        ],
        out_specs=[everything(out) for out in outs],
        out_shape=outs,
        compiler_params=params(),
        cost_estimate=cost(2 * pieces * here * wide * mods * mine, 2 * pieces * here * wide),
        name="lead_product",
    )(places, x, facts, weight)


def lead_pieces_kernel(mods, count, places, facts_ref, weight_ref, *refs):
    pieces = refs[:count]
    out_ref, whole, all_ref, buffer, in_sems, out_sems = refs[count:]
    _, some, here, wide = buffer.shape
    assemble(weight_ref, whole)

    def fetch(i):
        return [
            pltpu.make_async_copy(pieces[i * some + j], buffer.at[i % 2, j], in_sems.at[i % 2, j]) for j in range(some)
        ]

    def store(i):
        return pltpu.make_async_copy(buffer.at[i % 2], all_ref.at[pl.ds(i * some, some)], out_sems.at[i % 2])

    steps = count // some
    for copy in fetch(0):
        copy.start()
    for i in range(steps):
        if i + 1 < steps:
            if i:
                store(i - 1).wait()
            for copy in fetch(i + 1):
                copy.start()
        for copy in fetch(i):
            copy.wait()
        store(i).start()
        label = label_column_of(facts_ref.at[i * some : (i + 1) * some])
        picked = chosen(dot(buffer[i % 2].reshape(some * here, wide), whole[...], ((1,), (0,))), label, mods)
        for j in range(some):
            out_ref[places[i * some + j]] = picked[j * here : (j + 1) * here].astype(out_ref.dtype)
    for i in range(max(steps - 2, 0), steps):
        store(i).wait()


def lead_pieces(places, pieces, facts, weight, dtype):
    here, wide = pieces[0].shape
    count, some = len(pieces), 4
    groups, mods, features, mine = weight.shape
    outs = [
        shape((count, here, mine), dtype),
        shape((groups * features, mods * mine), bf16),
        shape((count, here, wide), bf16),
    ]
    vmem, there = pl.BlockSpec(memory_space=pltpu.VMEM), pl.BlockSpec(memory_space=pl.ANY)
    return pl.pallas_call(
        functools.partial(lead_pieces_kernel, mods, count),
        in_specs=[scalars(), vmem, vmem] + [there] * count,
        out_specs=[vmem, vmem, there],
        out_shape=outs,
        scratch_shapes=[
            pltpu.VMEM((2, some, here, wide), bf16),
            pltpu.SemaphoreType.DMA((2, some)),
            pltpu.SemaphoreType.DMA((2,)),
        ],
        compiler_params=params(),
        cost_estimate=cost(2 * count * here * wide * mods * mine, 4 * count * here * wide),
        name="lead_pieces",
    )(places, facts, weight, *pieces)


def trail_kernel(mods, count, first, *refs):
    lefts, facts_ref, weights = refs[:count], refs[count], refs[count + 1 : 2 * count + 1]
    outs = refs[2 * count + 1 :]
    some, here, mine = lefts[0].shape
    label = label_column_of(facts_ref)
    total = None
    for left, weight in zip(lefts, weights):
        term = dot(placed(left[...].reshape(some * here, mine), label, mods), weight[...], ((1,), (1,)))
        total = term if total is None else total + term
    total = total.astype(bf16).reshape(some, here, -1)
    if len(outs) == 1:
        outs[0][...] = total
    else:
        for i, out in enumerate(outs):

            @pl.when(pl.program_id(0) == i)
            def _():
                out[...] = total


def trail_product(lefts, facts, weights, mods, k=None):
    pieces, here, mine = lefts[0].shape
    features = weights[0].shape[0]
    if k is None:
        steps, outs = pieces // 4, [shape((pieces, here, features), bf16)]
        out_specs = [pl.BlockSpec((4, here, features), lambda i: (i, 0, 0))]

        def block(i):
            return (i, 0, 0)
    else:
        steps, outs = 2, [shape((4, here, features), bf16)] * 2
        out_specs = [everything(out) for out in outs]

        def block(i):
            return (2 * k + 1 - i, 0, 0)

    return pl.pallas_call(
        functools.partial(trail_kernel, mods, len(lefts), k),
        grid=(steps,),
        in_specs=[pl.BlockSpec((4, here, mine), block) for _ in lefts]
        + [pl.BlockSpec((4, fact_columns, here), block)]
        + [everything(weight) for weight in weights],
        out_specs=out_specs,
        out_shape=outs,
        compiler_params=params(),
        cost_estimate=cost(
            8 * steps * here * features * mods * mine * len(lefts), 8 * steps * here * features
        ),
        name="trail_product",
    )(*lefts, facts, *weights)


def grad_kernel(mods, x_ref, d_ref, facts_ref, out_ref, spread):
    pieces, here, mine = d_ref.shape

    @pl.when(pl.program_id(0) == 0)
    def _():
        for i in range(pieces):
            label = columns_of(facts_ref[i])[:, label_column : label_column + 1]
            spread[i * here : (i + 1) * here] = placed(d_ref[i], label, mods)

    out_ref[0] = dot(x_ref[...], spread[...], ((0,), (0,))).astype(out_ref.dtype)


def feature_grad(x, d, facts, mods, groups, dtype):
    pieces, here, wide = x.shape
    mine = d.shape[2]
    some = min(256, wide)
    out = shape((wide // some, some, mods * mine), dtype)
    grad = pl.pallas_call(
        functools.partial(grad_kernel, mods),
        grid=(wide // some,),
        in_specs=[
            pl.BlockSpec((pieces * here, some), lambda i: (0, i)),
            everything(d),
            everything(facts),
        ],
        out_specs=pl.BlockSpec((1, some, mods * mine), lambda i: (i, 0, 0)),
        out_shape=out,
        scratch_shapes=[pltpu.VMEM((pieces * here, mods * mine), bf16)],
        compiler_params=params(),
        cost_estimate=cost(6 * pieces * here * wide * mods * mine, 2 * pieces * here * wide),
        name="feature_grad",
    )(x.reshape(pieces * here, wide), d, facts)
    return grad.reshape(groups, wide // groups, mods * mine)


def settle_kernel(got_ref, weight_ref, out_ref, sum_ref):
    mods, _, mine = out_ref.shape

    @pl.when(pl.program_id(0) == 0)
    def _():
        sum_ref[...] = jnp.zeros_like(sum_ref)

    for m in range(mods):
        grad = got_ref[0, :, m * mine : (m + 1) * mine].astype(f32)
        out_ref[m] = grad
        sum_ref[...] += grad * weight_ref[m].astype(f32)


def settle(got, weight):
    sources, some, columns = got.shape
    mods, _, wide = weight.shape
    mine = wide // sources
    item = pl.BlockSpec((mods, some, mine), lambda i: (0, 0, i))
    outs = [shape(weight.shape, f32), shape((some, mine), f32)]
    return pl.pallas_call(
        settle_kernel,
        grid=(sources,),
        in_specs=[pl.BlockSpec((1, some, columns), lambda i: (i, 0, 0)), item],
        out_specs=[item, everything(outs[1])],
        out_shape=outs,
        compiler_params=params(),
        cost_estimate=cost(0, 8 * mods * some * wide),
        name="settle",
    )(got, weight)


def conv_kernel(mods, conv_ref, before_ref, facts_ref, row_label_ref, taps_ref, bias_ref, xdt_ref, xbc_ref, pre_ref, proj_ref, carried, line):
    rows, here, mine = conv_ref.shape

    @pl.when(pl.program_id(0) == 0)
    def _():
        carried[...] = before_ref[...]

    for r in range(rows):
        block = conv_ref[r].astype(f32)
        line[:8] = carried[r]
        line[8:] = block
        facts = columns_of(facts_ref[r, 0])
        pre = bias_ref[...] + taps_ref[0:1] * block
        for lag in range(1, taps_ref.shape[0]):
            pre = pre + taps_ref[lag : lag + 1] * (facts[:, lag - 1 : lag] * line[8 - lag : 8 - lag + here])
        carried[r] = block[here - 8 :]
        pre_ref[r] = pre
        low = apply_silu(pre).astype(bf16)
        wide = chosen(dot(low, xdt_ref[...], ((1,), (0,))), facts[:, label_column : label_column + 1], mods)
        small = chosen(dot(xbc_ref[...], low, ((1,), (1,))), row_label_ref[0, r : r + 1], mods, 0)
        proj_ref[r, 0, :here] = wide.astype(bf16)
        proj_ref[r, 0, here:] = small.astype(bf16)


def conv_block(conv_in, before, facts, row_label, taps, bias, xdt, xbc):
    rows, length, mine = conv_in.shape
    blocks, _, here = row_label.shape
    mods = xdt.shape[1] // here
    narrow = xbc.shape[0] // mods
    item = pl.BlockSpec((rows, here, mine), lambda i: (0, i, 0))
    return pl.pallas_call(
        functools.partial(conv_kernel, mods),
        grid=(blocks,),
        in_specs=[
            item,
            everything(before),
            pl.BlockSpec((rows, 1, fact_columns, here), lambda i: (0, i, 0, 0)),
            pl.BlockSpec((1, rows, here), lambda i: (i, 0, 0)),
        ]
        + [everything(array) for array in (taps, bias, xdt, xbc)],
        out_specs=[item, pl.BlockSpec((rows, 1, here + narrow, here), lambda i: (0, i, 0, 0))],
        out_shape=[shape(conv_in.shape, f32), shape((rows, blocks, here + narrow, here), bf16)],
        scratch_shapes=[pltpu.VMEM((rows, 8, mine), f32), pltpu.VMEM((8 + here, mine), f32)],
        compiler_params=params(),
        cost_estimate=cost(20000 * rows * length * mine, 10 * rows * length * mine),
        name="conv_block",
    )(conv_in, before, facts, row_label, taps, bias, xdt, xbc)


def coefficient_lines(proj_ref, rows, here, line):
    narrow = proj_ref.shape[2] - here
    for r in range(rows):
        small = proj_ref[r, 0, here:].astype(f32)
        small = jnp.concatenate([small, jnp.zeros((here - narrow, here), f32)], axis=0)
        turned = jnp.transpose(small)
        line[r * here : (r + 1) * here] = turned
        line[(rows + r) * here : (rows + r + 1) * here] = pltpu.roll(turned, here - narrow // 2, 1)


def scan_lines(r, rows, here, value, line):
    line[r * here : (r + 1) * here] = value
    line[(rows + r) * here : (rows + r + 1) * here] = value


def forward_kernel(
    mods, proj_ref, pre_ref, facts_ref, gate_ref, dtw_ref, dtb_ref, rate_ref, skip_ref, start_ref,
    gated_ref, scanned_ref, dt_ref, kept_ref, end_ref, held, step_line, drive_line, coef_line, out_line,
):
    rows, here, mine = pre_ref.shape
    pieces, subl, _ = rate_ref.shape

    @pl.when(pl.program_id(0) == 0)
    def _():
        held[...] = start_ref[...]

    coefficient_lines(proj_ref, rows, here, coef_line)
    for r in range(rows):
        facts = columns_of(facts_ref[r, 0])
        label = facts[:, label_column : label_column + 1]
        dt_pre = chosen(dot(proj_ref[r, 0, :here], dtw_ref[...], ((1,), (0,))) + dtb_ref[...], label, mods)
        dt_ref[r] = dt_pre
        step = softplus(dt_pre)
        scan_lines(r, rows, here, step * apply_silu(pre_ref[r]), drive_line)
        scan_lines(r, rows, here, jnp.where(facts[:, start_column : start_column + 1] > 0, huge_step, step), step_line)

    def one(t, state):
        lines = pl.ds(t, subl, stride=here)
        step, drive, coefs = step_line[lines, :], drive_line[lines, :], coef_line[lines, :]
        emitted = None
        following = []
        for j in range(pieces):
            kept_ref[t, j] = state[j]
            decay = jnp.exp2(step * rate_ref[j])
            now = decay * state[j] + drive * jnp.broadcast_to(coefs[:, j : j + 1], step.shape)
            term = now * jnp.broadcast_to(coefs[:, pieces + j : pieces + j + 1], step.shape)
            emitted = term if emitted is None else emitted + term
            following.append(now)
        out_line[lines, :] = emitted
        return tuple(following)

    def eight(block, state):
        for i in range(8):
            state = one(block * 8 + i, state)
        return state

    state = lax.fori_loop(0, here // 8, eight, tuple(held[j] for j in range(pieces)))
    for j in range(pieces):
        held[j] = state[j]
        end_ref[j] = state[j]
    for r in range(rows):
        emitted = out_line[r * here : (r + 1) * here] + out_line[(rows + r) * here : (rows + r + 1) * here]
        scanned = emitted + skip_ref[...] * apply_silu(pre_ref[r])
        scanned_ref[r] = scanned
        gated_ref[r] = (scanned * apply_silu(gate_ref[r])).astype(bf16)


def scan_forward(proj, pre, facts, gate, dtw, dtb, rates2, skip, start):
    rows, length, mine = pre.shape
    _, blocks, deep, here = proj.shape
    pieces, subl, _ = rates2.shape
    item = pl.BlockSpec((rows, here, mine), lambda i: (0, i, 0))
    line = pltpu.VMEM((subl * here, mine), f32)
    return pl.pallas_call(
        functools.partial(forward_kernel, dtw.shape[1] // mine),
        grid=(blocks,),
        in_specs=[
            pl.BlockSpec((rows, 1, deep, here), lambda i: (0, i, 0, 0)),
            item,
            pl.BlockSpec((rows, 1, fact_columns, here), lambda i: (0, i, 0, 0)),
            item,
        ]
        + [everything(array) for array in (dtw, dtb, rates2, skip, start)],
        out_specs=[
            item,
            item,
            item,
            pl.BlockSpec((here, pieces, subl, mine), lambda i: (i, 0, 0, 0)),
            everything(start),
        ],
        out_shape=[
            shape(pre.shape, bf16),
            shape(pre.shape, f32),
            shape(pre.shape, f32),
            shape((length, pieces, subl, mine), f32),
            shape(start.shape, f32),
        ],
        scratch_shapes=[pltpu.VMEM(start.shape, f32), line, line, line, line],
        compiler_params=params(),
        cost_estimate=cost(5500 * length * pieces * subl * mine, 5 * length * pieces * subl * mine),
        name="scan_forward",
    )(proj, pre, facts, gate, dtw, dtb, rates2, skip, start)


def backward_kernel(
    mods, tables, proj_ref, pre_ref, facts_ref, gate_ref, scanned_ref, dt_ref, d_gated_ref, kept_ref, dtw_ref, rate2_ref,
    rate_ref, skip_ref, last_ref, carry_ref, sum_ref, d_gate_ref, d_proj_ref, d_act_ref, dtw_grad_ref, dtb_grad_ref,
    skip_grad_ref, rate_sum_ref, carry_out_ref, carried, later, products, step_line, drive_line, coef_line, back_line,
    pulled_line, weighted_line, small_line,
):
    rows, here, mine = pre_ref.shape
    blocks = tables.shape[0] // rows
    narrow = proj_ref.shape[2] - here
    pieces, subl, _ = rate_ref.shape
    place = blocks - 1 - pl.program_id(0)

    @pl.when(pl.program_id(0) == 0)
    def _():
        carried[...] = carry_ref[...]
        later[...] = last_ref[...]
        for ref in (rate_sum_ref, dtw_grad_ref, dtb_grad_ref, skip_grad_ref):
            ref[...] = jnp.zeros_like(ref)

    coefficient_lines(proj_ref, rows, here, coef_line)
    for r in range(rows):
        facts = columns_of(facts_ref[r, 0])
        step, activated = softplus(dt_ref[r]), apply_silu(pre_ref[r])
        gate, d_gated = gate_ref[r], d_gated_ref[r]
        d_scan = d_gated * apply_silu(gate)
        d_gate_ref[tables[r * blocks + place]] = (d_gated * scanned_ref[r] * silu_slope(gate)).astype(bf16)
        skip_grad_ref[...] += jnp.sum(d_scan * activated, axis=0, keepdims=True)
        scan_lines(r, rows, here, d_scan, back_line)
        scan_lines(r, rows, here, step * activated, drive_line)
        scan_lines(r, rows, here, jnp.where(facts[:, start_column : start_column + 1] > 0, huge_step, step), step_line)

    def one(t, carry, state):
        lines = pl.ds(t, subl, stride=here)
        step, drive, coefs, back = step_line[lines, :], drive_line[lines, :], coef_line[lines, :], back_line[lines, :]
        pulled_sum, weighted_sum = None, None
        new_carry, new_state, terms, sums = [], [], [], []
        for j in range(pieces):
            before = kept_ref[t, j]
            decay = jnp.exp2(step * rate2_ref[j])
            adjoint = back * jnp.broadcast_to(coefs[:, pieces + j : pieces + j + 1], step.shape) + carry[j]
            passed = decay * adjoint
            pulled = passed * before
            weighted = adjoint * jnp.broadcast_to(coefs[:, j : j + 1], step.shape)
            first = pulled * rate_ref[j]
            pulled_sum = first if pulled_sum is None else pulled_sum + first
            weighted_sum = weighted if weighted_sum is None else weighted_sum + weighted
            terms.append((adjoint * drive, back * state[j]))
            sums.append(pulled * step)
            new_carry.append(passed)
            new_state.append(before)
        pulled_line[lines, :] = pulled_sum
        weighted_line[lines, :] = weighted_sum
        return new_carry, new_state, terms, sums

    def eight(k, loop):
        carry, state, rates = loop
        block = here // 8 - 1 - k
        rates = list(rates)
        for i in (6, 4, 2, 0):
            t = block * 8 + i
            carry, state, terms_b, sums_b = one(t + 1, carry, state)
            carry, state, terms_a, sums_a = one(t, carry, state)
            spot = pl.ds(pl.multiple_of(t * subl, 16), 16)
            for j in range(pieces):
                rates[j] = rates[j] + (sums_a[j] + sums_b[j])
                for part in range(2):
                    column = (part * pieces + j) * mine
                    products[spot, column : column + mine] = jnp.concatenate(
                        [terms_a[j][part], terms_b[j][part]], axis=0
                    ).astype(bf16)
        return tuple(carry), tuple(state), tuple(rates)

    begin = tuple(tuple(ref[j] for j in range(pieces)) for ref in (carried, later, rate_sum_ref))
    carry, state, rates = lax.fori_loop(0, here // 8, eight, begin)
    for j in range(pieces):
        carried[j] = carry[j]
        later[j] = state[j]
        rate_sum_ref[j] = rates[j]
        carry_out_ref[j] = carry[j]
    small_line[...] = dot(products[...], sum_ref[...], ((1,), (0,)))
    for r in range(rows):
        label = columns_of(facts_ref[r, 0])[:, label_column : label_column + 1]
        dt_pre, activated = dt_ref[r], apply_silu(pre_ref[r])
        near, far = slice(r * here, (r + 1) * here), slice((rows + r) * here, (rows + r + 1) * here)
        weighted = weighted_line[near] + weighted_line[far]
        d_step = pulled_line[near] + pulled_line[far] + activated * weighted
        d_act_ref[r] = back_line[near] * skip_ref[...] + softplus(dt_pre) * weighted
        d_dt = placed((d_step * jax.nn.sigmoid(dt_pre)).astype(bf16), label, mods)
        dtw_grad_ref[...] += dot(proj_ref[r, 0, :here], d_dt, ((0,), (0,)))
        dtb_grad_ref[...] += jnp.sum(d_dt.astype(f32), axis=0, keepdims=True)
        d_proj_ref[r, 0, :here] = dot(d_dt, dtw_ref[...], ((1,), (1,))).astype(bf16)
        one_half = small_line[pl.ds(r, here, stride=subl), :]
        other_half = small_line[pl.ds(rows + r, here, stride=subl), :]
        small = jnp.transpose(one_half + pltpu.roll(other_half, narrow // 2, 1))
        d_proj_ref[r, 0, here:] = small[:narrow].astype(bf16)


def scan_backward(tables, proj, pre, facts, gate, scanned, dt_pre, d_gated, kept, dtw, rates2, rates, skip, last, carry):
    rows, length, mine = pre.shape
    _, blocks, deep, here = proj.shape
    pieces, subl, _ = rates2.shape
    item = pl.BlockSpec((rows, here, mine), lambda i: (0, blocks - 1 - i, 0))
    proj_item = pl.BlockSpec((rows, 1, deep, here), lambda i: (0, blocks - 1 - i, 0, 0))
    columns = 2 * pieces * mine
    summing = (jnp.arange(columns)[:, None] // mine == jnp.arange(lanes)[None, :]).astype(bf16)
    d_gate = shape((rows * blocks, here, mine), bf16)
    line = pltpu.VMEM((subl * here, mine), f32)
    small = [shape((here, dtw.shape[1]), f32), shape((1, dtw.shape[1]), f32), shape((1, mine), f32), shape(carry.shape, f32)]
    return pl.pallas_call(
        functools.partial(backward_kernel, dtw.shape[1] // mine),
        grid=(blocks,),
        in_specs=[
            scalars(),
            proj_item,
            item,
            pl.BlockSpec((rows, 1, fact_columns, here), lambda i: (0, blocks - 1 - i, 0, 0)),
            item,
            item,
            item,
            item,
            pl.BlockSpec((here, pieces, subl, mine), lambda i: (blocks - 1 - i, 0, 0, 0)),
        ]
        + [everything(array) for array in (dtw, rates2, rates, skip, last, carry, summing)],
        out_specs=[everything(d_gate), proj_item, item] + [everything(array) for array in small + [carry]],
        out_shape=[d_gate, shape(proj.shape, bf16), shape(pre.shape, f32)] + small + [shape(carry.shape, f32)],
        scratch_shapes=[pltpu.VMEM(carry.shape, f32)] * 2 + [pltpu.VMEM((subl * here, columns), bf16)] + [line] * 7,
        compiler_params=params(),
        cost_estimate=cost(7500 * length * pieces * subl * mine, 5 * length * pieces * subl * mine),
        name="scan_backward",
    )(tables, proj, pre, facts, gate, scanned, dt_pre, d_gated, kept, dtw, rates2, rates, skip, last, carry, summing)


def deconv_kernel(
    mods, tables, d_proj_ref, conv_ref, pre_ref, d_act_ref, facts_ref, row_label_ref, taps_ref, xdt_ref, xbc_ref,
    d_conv_ref, xdt_grad_ref, xbc_grad_ref, taps_grad_ref, bias_grad_ref, head_ref, tail_ref, carried, line,
):
    rows, here, mine = pre_ref.shape
    blocks = tables.shape[0] // rows
    taps = taps_ref.shape[0]
    place = blocks - 1 - pl.program_id(0)

    @pl.when(pl.program_id(0) == 0)
    def _():
        carried[...] = jnp.zeros_like(carried)
        for ref in (xdt_grad_ref, xbc_grad_ref, taps_grad_ref, bias_grad_ref):
            ref[...] = jnp.zeros_like(ref)

    for r in range(rows):
        facts = columns_of(facts_ref[r, 0])
        pre = pre_ref[r]
        low = apply_silu(pre).astype(bf16)
        d_rank = placed(d_proj_ref[r, 0, :here], facts[:, label_column : label_column + 1], mods)
        d_small = placed(d_proj_ref[r, 0, here:], row_label_ref[0, r : r + 1], mods, 0)
        xdt_grad_ref[...] += dot(low, d_rank, ((0,), (0,)))
        xbc_grad_ref[...] += dot(d_small, low, ((1,), (0,)))
        d_act = d_act_ref[r] + dot(d_rank, xdt_ref[...], ((1,), (1,))) + dot(d_small, xbc_ref[...], ((0,), (0,)))
        d_pre = d_act * silu_slope(pre)
        source = conv_ref[r].astype(f32)
        total = taps_ref[0:1] * d_pre
        bias_grad_ref[...] += jnp.sum(d_pre, axis=0, keepdims=True)
        taps_grad_ref[0:1] += jnp.sum(source * d_pre, axis=0, keepdims=True)
        for lag in range(1, taps):
            kept = facts[:, lag - 1 : lag] * d_pre
            line[:here] = kept
            line[here:] = carried[r, lag - 1]
            carried[r, lag - 1] = kept[:8]
            moved = line[lag : lag + here]
            total = total + taps_ref[lag : lag + 1] * moved
            taps_grad_ref[lag : lag + 1] += jnp.sum(source * moved, axis=0, keepdims=True)
        d_conv_ref[tables[r * blocks + place]] = total.astype(bf16)

        @pl.when(pl.program_id(0) == 0)
        def _():
            tail_ref[r] = total[here - 8 :]

    head_ref[...] = carried[...]


def deconv_block(tables, d_proj, conv_in, pre, d_act, facts, row_label, taps, xdt, xbc):
    rows, length, mine = pre.shape
    _, blocks, deep, here = d_proj.shape
    item = pl.BlockSpec((rows, here, mine), lambda i: (0, blocks - 1 - i, 0))
    outs = [
        shape((rows * blocks, here, mine), bf16),
        shape(xdt.shape, f32),
        shape(xbc.shape, f32),
        shape(taps.shape, f32),
        shape((1, mine), f32),
        shape((rows, taps.shape[0] - 1, 8, mine), f32),
        shape((rows, 8, mine), f32),
    ]
    return pl.pallas_call(
        functools.partial(deconv_kernel, xdt.shape[1] // here),
        grid=(blocks,),
        in_specs=[
            scalars(),
            pl.BlockSpec((rows, 1, deep, here), lambda i: (0, blocks - 1 - i, 0, 0)),
            item,
            item,
            item,
            pl.BlockSpec((rows, 1, fact_columns, here), lambda i: (0, blocks - 1 - i, 0, 0)),
            pl.BlockSpec((1, rows, here), lambda i: (blocks - 1 - i, 0, 0)),
        ]
        + [everything(array) for array in (taps, xdt, xbc)],
        out_specs=[everything(array) for array in outs],
        out_shape=outs,
        scratch_shapes=[pltpu.VMEM(outs[5].shape, f32), pltpu.VMEM((here + 8, mine), f32)],
        compiler_params=params(),
        cost_estimate=cost(30000 * rows * length * mine, 14 * rows * length * mine),
        name="deconv_block",
    )(tables, d_proj, conv_in, pre, d_act, facts, row_label, taps, xdt, xbc)


def passed_along(value, axis, by):
    size = lax.axis_size(axis)
    return lax.ppermute(value, axis, [(i, i + by) for i in range(size) if 0 <= i + by < size])


def shifted(value, by):
    size = lax.axis_size("z")
    return value if by % size == 0 else lax.ppermute(value, "z", [(i, (i + by) % size) for i in range(size)])


def swapped(value):
    return lax.ppermute(value, "c", [(0, 1), (1, 0)])


def hop(value, second):
    depth = lax.axis_size("z")

    def place(y, x, z, c):
        return ((y * 2 + x) * depth + z) * 2 + c

    pairs = [
        (place(y, x, z, c), place(y, 1 - x, z, c) if (c == 1) == second else place(1 - y, x, z, c))
        for y in range(2)
        for x in range(2)
        for z in range(depth)
        for c in range(2)
    ]
    return lax.ppermute(value, team_axes, pairs)


def relative_places():
    depth = lax.axis_size("z")
    y, x, z, c = (lax.axis_index(name) for name in team_axes)
    n = jnp.arange(4)[None, None, :]
    core = (c + jnp.arange(2)[None, :, None]) % 2
    back = (z - jnp.arange(depth)[:, None, None]) % depth
    one, two = n % 2, n // 2
    flip_x = jnp.where(core == 0, one, two)
    flip_y = jnp.where(core == 0, two, one)
    return (((((y + flip_y) % 2) * 2 + (x + flip_x) % 2) * depth + back) * 2 + core).reshape(-1)


def team_gather(value):
    parts = []
    for k in range(lax.axis_size("z")):
        near = shifted(value, k)
        first, second = hop(near, False), hop(near, True)
        pieces = [near, first, second, hop(first, True)]
        parts += pieces + [swapped(piece) for piece in pieces]
    return parts


def team_scatter(made):
    total = None
    depth = lax.axis_size("z")

    def added(*terms):
        return sum(term.astype(f32) for term in terms)

    for k in list(range(1, depth)) + [0]:
        far, near = made(k)
        far = swapped(far)
        come = hop(added(near[2:], far[2:]).astype(bf16), True)
        last = hop(added(near[1], far[1], come[1]).astype(bf16), False)
        held = added(near[0], far[0], come[0], last)
        if k:
            held = shifted(held.astype(bf16), -k).astype(f32)
        total = held if total is None else total + held
    return total


def exchanged(parts):
    return lax.all_to_all(parts, group_axes, 0, 0, tiled=True)


def spread_weight(weight):
    outer, group = lax.axis_size("o"), lax.axis_size(group_axes)
    mods, here, wide = weight.shape
    each = wide // (outer * group)
    parts = weight.reshape(mods, here, outer, group, each)
    parts = jnp.transpose(parts, (3, 0, 1, 2, 4)).reshape(group, mods, here, outer * each)
    return parts


def spread_done(parts):
    got = exchanged(parts)
    return got if lax.axis_size("o") == 1 else lax.all_gather(got, "o", axis=0, tiled=True)


def collect_grad(parts, weight):
    outer, group = lax.axis_size("o"), lax.axis_size(group_axes)
    mods, here, wide = weight.shape
    if outer > 1:
        parts = lax.psum_scatter(parts, "o", scatter_dimension=0, tiled=True)
    got = exchanged(parts.astype(bf16))
    if outer == 1:
        grad, sums = settle(got, weight)
        return grad, jnp.sum(sums, axis=1)
    got = got.astype(f32).reshape(group, here, mods, outer, wide // (outer * group))
    grad = jnp.transpose(got, (2, 1, 3, 0, 4)).reshape(weight.shape)
    return grad, jnp.sum(grad * weight.astype(f32), axis=(0, 2))


def outer_gathered(value, axis):
    return value if lax.axis_size("o") == 1 else lax.all_gather(value, "o", axis=axis, tiled=True)


def outer_summed(value, axis):
    if lax.axis_size("o") == 1:
        return value
    return lax.psum_scatter(value, "o", scatter_dimension=axis, tiled=True)


def half_of(value, axis, name, other):
    return lax.dynamic_index_in_dim(value, (lax.axis_index(name) + other) % 2, axis, False)


def team_sum(value):
    depth = lax.axis_size("z")
    z = lax.axis_index("z")

    def halved(value, axis, name, pairs):
        sent = lax.ppermute(half_of(value, axis, name, 1).astype(bf16), name, pairs)
        return half_of(value, axis, name, 0).astype(f32) + sent.astype(f32)

    swap = [(0, 1), (1, 0)]
    held = halved(value, 3, "c", swap)
    held = halved(held, 0, "y", swap)
    held = halved(held, 0, "x", swap)
    own = lax.dynamic_index_in_dim(held, z, 0, False)
    for k in range(1, depth):
        own = own + shifted(lax.dynamic_index_in_dim(held, (z + k) % depth, 0, False).astype(bf16), k).astype(f32)
    own = own.astype(bf16)
    back = jnp.stack([own] + [shifted(own, k) for k in range(1, depth)])
    rolled = back[(z - jnp.arange(depth)) % depth]

    def doubled(value, axis, name):
        other = lax.ppermute(value, name, swap)
        flag = lax.axis_index(name) == 0
        return jnp.stack([jnp.where(flag, value, other), jnp.where(flag, other, value)], axis=axis)

    return doubled(doubled(doubled(rolled, 0, "x"), 0, "y"), 3, "c")


def entering_state(passing, local_end, backward):
    count, place = lax.axis_size("o"), lax.axis_index("o")
    decays = lax.all_gather(passing.astype(bf16), "o")
    ends = lax.all_gather(local_end.astype(bf16), "o")
    state = jnp.zeros_like(local_end)
    for i in range(count):
        source = count - 1 - i if backward else i
        ahead = source > place if backward else source < place
        state = jnp.where(ahead, decays[source].astype(f32) * state + ends[source].astype(f32), state)
    return state


def on_device(
    tokens,
    cotangent,
    modality,
    starts,
    row_lengths,
    norm_gain,
    in_x_weight,
    in_z_weight,
    xdt_weight,
    xbc_weight,
    dt_weight,
    dt_bias,
    conv_weight,
    conv_bias,
    log_rates,
    skip_gain,
    out_weight,
):
    outer, group = lax.axis_size("o"), lax.axis_size(group_axes)
    rows, here = modality.shape
    width = tokens.shape[-1]
    mods = in_x_weight.shape[1]
    taps, states, rank = conv_weight.shape[0], log_rates.shape[0], dt_weight.shape[0]
    margin = taps - 1
    local_len = group * here
    own_row = lax.axis_index(row_axes)
    count = rows * local_len

    depth = lax.axis_size("z")
    place_z = lax.axis_index("z")

    def lead(weight):
        return jnp.transpose(weight, (1, 0, 2))

    features = norm_gain.shape[0]
    packed = jnp.concatenate(
        [modality.astype(f32).reshape(-1), starts.astype(f32).reshape(-1), norm_gain.astype(f32)]
    )
    packed = jnp.stack([packed] + [shifted(packed, k) for k in range(1, depth)])
    packed = packed[(place_z - jnp.arange(depth)) % depth]
    others, first_core = swapped(packed), lax.axis_index("c") == 0
    packed = jnp.stack([jnp.where(first_core, packed, others), jnp.where(first_core, others, packed)], axis=1)
    labels = packed[:, :, : 2 * rows * here].astype(jnp.int32).reshape(depth, 2, 2, rows, here)
    labels = jnp.transpose(labels, (2, 3, 0, 1, 4)).reshape(2, rows, local_len)
    modality, starts = labels[0], labels[1]
    gain = outer_gathered(packed[:, :, 2 * rows * here :].reshape(-1, features), 0).reshape(width)

    inputs = tokens[0].astype(f32)
    inv_rms = lax.rsqrt(jnp.mean(inputs * inputs, axis=-1, keepdims=True) + epsilon)
    scaled = inputs * inv_rms
    normed_pieces = team_gather((scaled * gain).astype(bf16))
    wx = spread_done(spread_weight(lead(in_x_weight)))
    wz_parts, wo_parts = in_z_weight, out_weight
    wz_parts, wx = lax.optimization_barrier((wz_parts, wx))
    wz = spread_done(spread_weight(lead(wz_parts)))
    wo_parts, wz = lax.optimization_barrier((wo_parts, wz))
    wo = spread_done(spread_weight(lead(wo_parts)))
    position = lax.axis_index(seq_axes) * here + jnp.arange(here, dtype=jnp.int32)
    own_valid = (position < lax.dynamic_index_in_dim(row_lengths, own_row, 0, False)).astype(f32)[:, None]
    upstream = cotangent[0].astype(f32)
    own_back = (upstream * own_valid).astype(bf16)
    own_back, normed_pieces[-1] = lax.optimization_barrier((own_back, normed_pieces[-1]))
    d_branch = lax.all_gather(own_back, team_axes)
    xdt = outer_gathered(xdt_weight, 0)
    xbc = outer_gathered(xbc_weight, 2)
    dtw = outer_gathered(dt_weight, 2)
    dtb = outer_gathered(dt_bias, 1).astype(f32)
    conv_w = outer_gathered(conv_weight, 1).astype(f32)
    conv_b = outer_gathered(conv_bias, 0).astype(f32)
    log_r = outer_gathered(log_rates, 1).astype(f32)
    skip = outer_gathered(skip_gain, 0).astype(f32)
    mine = skip.shape[0]
    places = relative_places()
    pieces_of = lax.axis_size(team_axes)
    relative = jnp.zeros((pieces_of,), jnp.int32).at[places].set(jnp.arange(pieces_of, dtype=jnp.int32))

    counted = jnp.cumsum(starts, axis=1)
    send_keep = counted[:, -1:] - counted[:, local_len - margin :] == 0
    counted_ext = jnp.concatenate([jnp.zeros((rows, margin), jnp.int32), counted], axis=1)
    facts = [counted - counted_ext[:, margin - lag : margin - lag + local_len] == 0 for lag in range(1, taps)]
    facts = [f.astype(f32) for f in facts] + [starts.astype(f32), modality.astype(f32)]
    facts += [jnp.zeros_like(facts[0])] * (fact_columns - len(facts))
    facts = jnp.stack([f.reshape(rows, group, here) for f in facts], axis=2)
    row_label = jnp.transpose(modality.reshape(rows, group, here), (1, 0, 2)).astype(f32)
    facts_flat = facts.reshape(pieces_of, fact_columns, here)
    facts_there = facts_flat[places]
    in_order = jnp.arange(pieces_of, dtype=jnp.int32)

    conv_in, wx_f, normed = lead_pieces(places, normed_pieces, facts_there, wx, bf16)
    conv_in = conv_in.reshape(rows, local_len, mine)
    gate_in, wz_f = lead_product(places, normed, facts_there, wz, f32)
    gate_in = gate_in.reshape(rows, local_len, mine)
    d_gated, wo_f = lead_product(in_order, d_branch, facts_flat, wo, f32)
    d_gated = d_gated.reshape(rows, local_len, mine)

    before = jnp.zeros((rows, 8, mine), f32)
    if outer > 1:
        outgoing = jnp.where(send_keep[:, :, None], conv_in[:, local_len - margin :, :], jnp.zeros((), bf16))
        incoming = passed_along(outgoing, "o", 1).astype(f32)
        before = jnp.pad(incoming, ((0, 0), (8 - margin, 0), (0, 0)))
    halves = 2
    pieces = states // halves
    narrow = 2 * states
    xdt_f = xdt.reshape(mine, mods * rank)
    xbc_f = jnp.transpose(xbc.reshape(2, halves, pieces, mods, mine), (3, 1, 0, 2, 4)).reshape(mods * narrow, mine)
    dt_f = dtw.reshape(rank, mods * mine)
    pre, proj_part = conv_block(conv_in, before, facts, row_label, conv_w, conv_b[None], xdt_f, xbc_f)

    def summed(part):
        return team_sum(part.reshape((2, 2, depth, 2) + part.shape[2:])).reshape(part.shape)

    proj = summed(proj_part)
    decay_coef = -jnp.exp(log_r)

    def per_state(values):
        split = jnp.transpose(values.reshape(halves, pieces, mine), (1, 0, 2))
        return jnp.repeat(split, rows, axis=1)

    rates = per_state(decay_coef)
    rates2 = rates * (1.0 / math.log(2.0))
    zero_state = jnp.zeros((pieces, halves * rows, mine), f32)
    skip_row = skip[None]
    dtb_row = dtb.reshape(1, mods * mine)

    def ahead(start):
        return scan_forward(proj, pre, facts, gate_in, dt_f, dtb_row, rates2, skip_row, start)

    gated, scanned, dt_pre, kept, last_state = ahead(zero_state)
    if outer > 1:
        steps = jnp.sum(jax.nn.softplus(dt_pre), axis=1)
        unbroken = (jnp.sum(starts, axis=1) == 0).astype(f32)[:, None]
        passing = jnp.exp2(jnp.concatenate([steps] * halves, axis=0)[None] * rates2)
        passing = passing * jnp.concatenate([unbroken] * halves, axis=0)[None]
        gated, scanned, dt_pre, kept, last_state = ahead(entering_state(passing, last_state, False))
    gated = gated.reshape(pieces_of, here, mine)
    branch = trail_product([gated], facts_flat, [wo_f], mods)[0].reshape(count, width)
    own_branch = lax.psum_scatter(branch, team_axes, scatter_dimension=0, tiled=True).astype(f32)
    block_out = (inputs + own_valid * own_branch).astype(bf16)[None]
    grad_type = f32 if outer > 1 else bf16

    def weight_grad(x, d, there, weight):
        return collect_grad(feature_grad(x, d, there, mods, outer * group, grad_type), lead(weight))

    out_weight_grad = lead(weight_grad(d_branch, gated, facts_flat, out_weight)[0])

    def back(carry):
        return scan_backward(
            relative, proj, pre, facts, gate_in, scanned, dt_pre, d_gated, kept, dt_f, rates2, rates, skip_row, last_state,
            carry,
        )

    results = back(zero_state)
    if outer > 1:
        results = back(entering_state(passing, results[-1], True))
    d_gate, d_proj_part, d_act, dtw_grad, dtb_grad, skip_grad, rate_total, _ = results
    in_z_grad, gain_z = weight_grad(normed, d_gate, facts_there, in_z_weight)
    d_proj = summed(d_proj_part)
    rate_total = jnp.sum(rate_total.reshape(pieces, halves, rows, mine), axis=2)
    rate_total = jnp.transpose(rate_total, (1, 0, 2)).reshape(states, mine)
    log_rates_grad = outer_summed(decay_coef * rate_total, 1)
    skip_gain_grad = outer_summed(skip_grad[0], 0)
    dt_weight_grad = outer_summed(dtw_grad.reshape(rank, mods, mine), 2)
    dt_bias_grad = outer_summed(dtb_grad.reshape(mods, mine), 1)
    d_conv, xdt_grad, xbc_grad, taps_grad, bias_grad, head, tail = deconv_block(
        relative, d_proj, conv_in, pre, d_act, facts, row_label, conv_w, xdt_f, xbc_f
    )
    if outer > 1:
        early = jnp.stack(
            [jnp.pad(head[:, lag - 1, :lag], ((0, 0), (margin - lag, 0), (0, 0))) for lag in range(1, taps)], axis=1
        )
        taps_grad = taps_grad.at[1:].add(jnp.sum(early * incoming[:, None], axis=(0, 2)))
        returned = jnp.sum(early * conv_w[None, 1:, None, :], axis=1)
        returned = passed_along(returned.astype(bf16), "o", -1).astype(f32)
        returned = jnp.where(send_keep[:, :, None], returned, 0.0)
        fixed = (tail[:, 8 - margin :] + returned).astype(bf16)
        spots = relative[jnp.arange(rows) * group + group - 1]
        d_conv = d_conv.at[spots, here - margin :].set(fixed)
    xdt_grad = outer_summed(xdt_grad.reshape(mine, mods, rank), 0)
    xbc_grad = jnp.transpose(xbc_grad.reshape(mods, halves, 2, pieces, mine), (2, 1, 3, 0, 4)).reshape(narrow, mods, mine)
    xbc_grad = outer_summed(xbc_grad, 2)
    conv_weight_grad = outer_summed(taps_grad, 1)
    conv_bias_grad = outer_summed(bias_grad[0], 0)
    d_scaled = team_scatter(lambda k: trail_product([d_conv, d_gate], facts_there, [wx_f, wz_f], mods, k)) * gain
    in_x_grad, gain_x = weight_grad(normed, d_conv, facts_there, in_x_weight)
    d_inputs = inv_rms * (d_scaled - scaled * jnp.mean(d_scaled * scaled, axis=-1, keepdims=True))
    tokens_grad = (upstream + d_inputs).astype(bf16)[None]
    gain_part = gain_x + gain_z
    for name in row_axes:
        gain_part = gain_part + lax.ppermute(gain_part, name, [(0, 1), (1, 0)])
    norm_gain_grad = gain_part / norm_gain.astype(f32)
    in_x_grad, in_z_grad = lead(in_x_grad), lead(in_z_grad)
    return (
        block_out,
        tokens_grad,
        norm_gain_grad,
        in_x_grad,
        in_z_grad,
        xdt_grad,
        xbc_grad,
        dt_weight_grad,
        dt_bias_grad,
        conv_weight_grad,
        conv_bias_grad,
        log_rates_grad,
        skip_gain_grad,
        out_weight_grad,
    )


def solution(mesh):
    rows, seq = mesh.shape["row"], mesh.shape["seq"]
    across = 2 if rows % 2 == 0 else 1
    cores = 2 if seq % 2 == 0 else 1
    along = next(n for n in (4, 3, 2, 1) if (seq // cores) % n == 0)
    fine = Mesh(
        mesh.devices.reshape(rows // across, across, seq // (along * cores), along, cores), ("y", "x", "o", "z", "c")
    )
    row, seq, both = row_axes, seq_axes, row_axes + seq_axes
    in_specs = (
        P(row, seq, None),
        P(row, seq, None),
        P(None, seq),
        P(None, seq),
        P(),
        P(seq),
        P(seq, None, row),
        P(seq, None, row),
        P(both, None, None),
        P(None, None, both),
        P(None, None, both),
        P(None, both),
        P(None, both),
        P(both),
        P(None, both),
        P(both),
        P(seq, None, row),
    )
    out_specs = (
        P(row, seq, None),
        P(row, seq, None),
        P(seq),
        P(seq, None, row),
        P(seq, None, row),
        P(both, None, None),
        P(None, None, both),
        P(None, None, both),
        P(None, both),
        P(None, both),
        P(both),
        P(None, both),
        P(both),
        P(seq, None, row),
    )
    return jax.shard_map(on_device, mesh=fine, in_specs=in_specs, out_specs=out_specs, check_vma=False)
```

profile of v0, /device:TPU:8, one launch (start us, length us, event | category | flops | bytes accessed | tf_op | source)
XLA Modules:
  0.0 783.3 jit_solution(9375253455505048637)
XLA Ops:
  8.8 3.0 collective-permute-start.1
  11.8 2.5 collective-permute-start
  18.9 2.7 collective-permute-start.27
  21.5 11.9 %collective-permute-done.27.refs_24_ = bf16[128,2048]{1,0:T(8,128)(2,1)S(1)} collective-permute-done((bf16[128,2048]{1,0:T(8,128)(2,1)S(1)}, bf16[128,2048]{1,0:T(8,128)(2,1)S(1)}, u32[]{:S(2)}, u32[]{:S(2)}) %collective-permute-start.27) | collective-permute-done | bytes 524320 | tf_op jit(solution)/shard_map/ppermute | solution.py:681
  34.9 7.8 collective-permute-done.28.refs_25_
  44.8 7.4 collective-permute-done.30.refs_27_
  54.5 3.0 collective-permute-start.19
  61.1 28.3 %collective-permute-done.19.refs_16_ = bf16[128,2048]{1,0:T(8,128)(2,1)} collective-permute-done((bf16[128,2048]{1,0:T(8,128)(2,1)S(1)}, bf16[128,2048]{1,0:T(8,128)(2,1)}, u32[]{:S(2)}, u32[]{:S(2)}) %collective-permute-start.19) | collective-permute-done | bytes 524320 | tf_op jit(solution)/shard_map/ppermute | solution.py:681
  89.4 12.9 %collective-permute-done.11.refs_8_ = bf16[128,2048]{1,0:T(8,128)(2,1)S(1)} collective-permute-done((bf16[128,2048]{1,0:T(8,128)(2,1)S(1)}, bf16[128,2048]{1,0:T(8,128)(2,1)S(1)}, u32[]{:S(2)}, u32[]{:S(2)}) %collective-permute-start.11) | collective-permute-done | bytes 524320 | tf_op jit(solution)/shard_map/ppermute | solution.py:681
  105.9 7.3 all-to-all-start
  115.4 3.6 collective-permute-done.29.refs_26_
  119.8 2.5 collective-permute-start.12
  122.2 7.9 %collective-permute-done.21.refs_18_ = bf16[128,2048]{1,0:T(8,128)(2,1)S(1)} collective-permute-done((bf16[128,2048]{1,0:T(8,128)(2,1)}, bf16[128,2048]{1,0:T(8,128)(2,1)S(1)}, u32[]{:S(2)}, u32[]{:S(2)}) %collective-permute-start.21) | collective-permute-done | bytes 524320 | tf_op jit(solution)/shard_map/ppermute | solution.py:701
  130.1 8.4 %collective-permute-start.8 = (bf16[128,2048]{1,0:T(8,128)(2,1)}, bf16[128,2048]{1,0:T(8,128)(2,1)}, u32[]{:S(2)}, u32[]{:S(2)}) collective-permute-start(bf16[128,2048]{1,0:T(8,128)(2,1)} %collective-permute-done.4.refs_1_), channel_id=1, source_target_pairs={{0,1},{1,0},{2,3},{3,2},{4,5},{5,4},{6,7},{7,6},{8,9},{9,8},{10,11... | collective-permute-start | bytes 1572872 | tf_op jit(solution)/shard_map/ppermute | solution.py:685
  140.9 7.5 collective-permute-start.33
  151.2 2.9 collective-permute-start.25
  159.7 12.3 %collective-permute-done.14.refs_11_ = bf16[128,2048]{1,0:T(8,128)(2,1)} collective-permute-done((bf16[128,2048]{1,0:T(8,128)(2,1)S(1)}, bf16[128,2048]{1,0:T(8,128)(2,1)}, u32[]{:S(2)}, u32[]{:S(2)}) %collective-permute-start.14) | collective-permute-done | bytes 524320 | tf_op jit(solution)/shard_map/ppermute | solution.py:701
  178.3 18.4 %lead_pieces.1 = (bf16[32,128,128]{2,1,0:T(8,128)(2,1)}, bf16[2048,384]{1,0:T(8,128)(2,1)}, bf16[32,128,2048]{2,1,0:T(8,128)(2,1)}) custom-call(s32[32]{0:T(128)S(1)} %add.518.places, f32[32,8,128]{2,1,0:T(8,128)S(1)} %gather_fusion.1, bf16[8,3,256,128]{3,2,1,0:T(8,128)(2,1)} %all-to-all-done.weight_ref, bf16[128,2048]{1,0:T(8,128)(2,1)S(1)} %fusion.5.refs_0_, ...), custom_call_target="tpu_custom_call" | custom-call | flops 6442450944 | bytes 33554432 | tf_op jit(solution)/shard_map/lead_pieces/pallas_call | solution.py:174
  198.0 6.4 conv_block.1
  213.7 8.1 %collective-permute-done.36 = bf16[2,4,160,128]{3,2,1,0:T(8,128)(2,1)S(1)} collective-permute-done((bf16[2,4,160,128]{3,2,1,0:T(8,128)(2,1)S(1)}, bf16[2,4,160,128]{3,2,1,0:T(8,128)(2,1)S(1)}, u32[]{:S(2)}, u32[]{:S(2)}) %collective-permute-start.36) | collective-permute-done | bytes 327712 | tf_op jit(solution)/shard_map/ppermute | solution.py:796
  226.3 5.7 all-to-all-start.1
  237.9 31.1 %collective-permute-done.38 = bf16[160,128]{1,0:T(8,128)(2,1)S(1)} collective-permute-done((bf16[160,128]{1,0:T(8,128)(2,1)S(1)}, bf16[160,128]{1,0:T(8,128)(2,1)S(1)}, u32[]{:S(2)}, u32[]{:S(2)}) %collective-permute-start.38) | collective-permute-done | bytes 40992 | tf_op jit(solution)/shard_map/ppermute | solution.py:681
  268.9 2.5 collective-permute-done.40
  273.5 2.7 collective-permute-start.41
  281.0 3.4 collective-permute-done.44
  286.3 5.6 collective-permute-done.45
  299.9 2.7 copy.103
  302.6 5.7 all-to-all-start.2
  308.3 13.9 %lead_product.2 = (f32[32,128,128]{2,1,0:T(8,128)S(1)}, bf16[2048,384]{1,0:T(8,128)(2,1)S(1)}) custom-call(s32[32]{0:T(128)S(1)} %add.518.places, bf16[32,128,2048]{2,1,0:T(8,128)(2,1)} %get-tuple-element.64.x_ref, f32[32,8,128]{2,1,0:T(8,128)S(1)} %gather_fusion.1, bf16[8,3,256,128]{3,2,1,0:T(8,128)(2,1)} %all-to-all-done.1.weight_ref), custom_call_target="tpu_custom_call" | custom-call | flops 6442450944 | bytes 16777216 | tf_op jit(solution)/shard_map/lead_product/pallas_call | solution.py:113
  324.8 48.8 %scan_forward.1 = (bf16[4,1024,128]{2,1,0:T(8,128)(2,1)S(1)}, f32[4,1024,128]{2,1,0:T(8,128)S(1)}, f32[4,1024,128]{2,1,0:T(8,128)}, f32[1024,8,8,128]{3,2,1,0:T(8,128)}, f32[8,8,128]{2,1,0:T(8,128)S(1)}) custom-call(bf16[4,8,160,128]{3,2,1,0:T(8,128)(2,1)S(1)} %bitcast.246, f32[4,1024,128]{2,1,0:T(8,128)} %copy-done.52, f32[4,8,8,128]{3,2,1,0:T(8,128)S(1)} %copy-done.15, ...), custom_call_target="tpu_custom_call" | custom-call | flops 46137344000 | bytes 41943040 | tf_op jit(solution)/shard_map/scan_forward/pallas_call | solution.py:430
  377.1 13.4 %lead_product.3 = (f32[32,128,128]{2,1,0:T(8,128)S(1)}, bf16[2048,384]{1,0:T(8,128)(2,1)S(1)}) custom-call(s32[32]{0:T(128)S(1)} %iota.54.places, bf16[32,128,2048]{2,1,0:T(8,128)(2,1)} %bitcast.301, f32[32,8,128]{2,1,0:T(8,128)S(1)} %stack.136.facts_ref.refs_1_, bf16[8,3,256,128]{3,2,1,0:T(8,128)(2,1)S(1)} %all-to-all-done.2.weight_ref), custom_call_target="tpu_custom_call" | custom-call | flops 6442450944 | bytes 16777216 | tf_op jit(solution)/shard_map/lead_product/pallas_call | solution.py:113
  391.9 14.0 %trail_product.5 = bf16[32,128,2048]{2,1,0:T(8,128)(2,1)} custom-call(bf16[32,128,128]{2,1,0:T(8,128)(2,1)S(1)} %bitcast.267, f32[32,8,128]{2,1,0:T(8,128)S(1)} %stack.136.facts_ref.refs_1_, bf16[2048,384]{1,0:T(8,128)(2,1)S(1)} %get-tuple-element.71.refs_2_), custom_call_target="tpu_custom_call" | custom-call | flops 6442450944 | bytes 16777216 | tf_op jit(solution)/shard_map/trail_product/pallas_call | solution.py:226
  409.0 64.9 %scan_backward.1 = (bf16[32,128,128]{2,1,0:T(8,128)(2,1)S(1)}, bf16[4,8,160,128]{3,2,1,0:T(8,128)(2,1)S(1)}, f32[4,1024,128]{2,1,0:T(8,128)}, f32[128,384]{1,0:T...) custom-call(s32[32]{0:T(128)S(1)} %scatter_custom_fusion.tables, ...), custom_call_target="tpu_custom_call" | custom-call | flops 62914560000 | bytes 41943040 | tf_op jit(solution)/shard_map/scan_backward/pallas_call | solution.py:569
  478.2 8.0 %collective-permute-done.48 = bf16[2,4,160,128]{3,2,1,0:T(8,128)(2,1)S(1)} collective-permute-done((bf16[2,4,160,128]{3,2,1,0:T(8,128)(2,1)S(1)}, bf16[2,4,160,128]{3,2,1,0:T(8,128)(2,1)S(1)}, u32[]{:S(2)}, u32[]{:S(2)}) %collective-permute-start.48) | collective-permute-done | bytes 327712 | tf_op jit(solution)/shard_map/ppermute | solution.py:796
  488.3 3.8 collective-permute-done.49
  493.9 9.3 %collective-permute-start.52 = (bf16[160,128]{1,0:T(8,128)(2,1)S(1)}, bf16[160,128]{1,0:T(8,128)(2,1)S(1)}, u32[]{:S(2)}, u32[]{:S(2)}) collective-permute-start(bf16[160,128]{1,0:T(8,128)(2,1)S(1)} %get-tuple-element.175), channel_id=1, source_target_pairs={{0,6},{2,0},{4,2},{6,4},{1,7},{3,1},{5,3},{7,5},{8,14},{10,8},{12,... | collective-permute-start | bytes 122888 | tf_op jit(solution)/shard_map/ppermute | solution.py:681
  503.2 4.2 collective-permute-start.51
  507.4 3.1 collective-permute-done.52
  514.7 2.8 collective-permute-start.53
  524.3 3.9 collective-permute-done.56
  531.2 15.5 %feature_grad.4 = bf16[8,256,384]{2,1,0:T(8,128)(2,1)S(1)} custom-call(bf16[4096,2048]{1,0:T(8,128)(2,1)} %bitcast.305, bf16[32,128,128]{2,1,0:T(8,128)(2,1)S(1)} %copy-done.50, f32[32,8,128]{2,1,0:T(8,128)S(1)} %gather_fusion.1), custom_call_target="tpu_custom_call" | custom-call | flops 19327352832 | bytes 16777216 | tf_op jit(solution)/shard_map/feature_grad/pallas_call | solution.py:259
  547.9 6.8 all-to-all-start.4
  556.2 16.3 %feature_grad.5 = bf16[8,256,384]{2,1,0:T(8,128)(2,1)} custom-call(bf16[4096,2048]{1,0:T(8,128)(2,1)} %all-gather.3.cloned.1.call-done.x_ref, bf16[32,128,128]{2,1,0:T(8,128)(2,1)S(1)} %bitcast.268, f32[32,8,128]{2,1,0:T(8,128)S(1)} %stack.136.facts_ref.refs_1_), custom_call_target="tpu_custom_call" | custom-call | flops 19327352832 | bytes 16777216 | tf_op jit(solution)/shard_map/feature_grad/pallas_call | solution.py:259
  574.7 18.0 %deconv_block.1 = (bf16[32,128,128]{2,1,0:T(8,128)(2,1)S(1)}, f32[128,384]{1,0:T(8,128)S(1)}, f32[96,128]{1,0:T(8,128)S(1)}, f32[4,128]{1,0:T(4,128)}, f32[1,128...) custom-call(s32[32]{0:T(128)S(1)} %scatter_custom_fusion.tables, bf16[4,8,160,128]{3,2,1,0:T(8,128)(2,1)S(1)} %bitcast.248, ...), custom_call_target="tpu_custom_call" | custom-call | flops 15728640000 | bytes 7340032 | tf_op jit(solution)/shard_map/deconv_block/pallas_call | solution.py:652
  592.7 7.8 trail_product.9
  600.9 7.8 trail_product.8
  608.8 7.8 trail_product.7
  616.9 7.9 %trail_product.6 = (bf16[4,128,2048]{2,1,0:T(8,128)(2,1)}, bf16[4,128,2048]{2,1,0:T(8,128)(2,1)}) custom-call(bf16[32,128,128]{2,1,0:T(8,128)(2,1)S(1)} %get-tuple-element.79.refs_0_.d_ref, bf16[32,128,128]{2,1,0:T(8,128)(2,1)S(1)} %copy-done.51, f32[32,8,128]{2,1,0:T(8,128)S(1)} %copy-done.13, bf16[2048,384]{1,0:T(8,128)(2,1)S(1)} %copy-done.46, ...), custom_call_target="tpu_custom_call" | custom-call | flops 3221225472 | bytes 4194304 | tf_op jit(solution)/shard_map/trail_product/pallas_call | solution.py:226
  625.0 15.4 %feature_grad.3 = bf16[8,256,384]{2,1,0:T(8,128)(2,1)S(1)} custom-call(bf16[4096,2048]{1,0:T(8,128)(2,1)} %bitcast.306, bf16[32,128,128]{2,1,0:T(8,128)(2,1)S(1)} %get-tuple-element.79.refs_0_.d_ref, f32[32,8,128]{2,1,0:T(8,128)S(1)} %copy-done.13), custom_call_target="tpu_custom_call" | custom-call | flops 19327352832 | bytes 16777216 | tf_op jit(solution)/shard_map/feature_grad/pallas_call | solution.py:259
  641.6 5.0 all-to-all-start.3
  654.9 2.6 add_convert_fusion.3
  658.9 4.7 collective-permute-done.72
  663.6 2.6 fusion.20
  667.9 12.5 %collective-permute-done.68 = bf16[2,128,2048]{2,1,0:T(8,128)(2,1)S(1)} collective-permute-done((bf16[2,128,2048]{2,1,0:T(8,128)(2,1)S(1)}, bf16[2,128,2048]{2,1,0:T(8,128)(2,1)S(1)}, u32[]{:S(2)}, u32[]{:S(2)}) %collective-permute-start.68) | collective-permute-done | bytes 1048608 | tf_op jit(solution)/shard_map/ppermute | solution.py:701
  684.6 5.1 all-to-all-start.5
  689.7 7.7 collective-permute-done.64
  700.8 13.5 %collective-permute-done.60 = bf16[2,128,2048]{2,1,0:T(8,128)(2,1)} collective-permute-done((bf16[2,128,2048]{2,1,0:T(8,128)(2,1)}, bf16[2,128,2048]{2,1,0:T(8,128)(2,1)}, u32[]{:S(2)}, u32[]{:S(2)}) %collective-permute-start.60) | collective-permute-done | bytes 1048608 | tf_op jit(solution)/shard_map/ppermute | solution.py:701
  721.3 2.5 fusion.14
  729.1 3.9 settle.4
  733.7 6.1 settle.3
  741.1 3.0 collective-permute-done.74
  750.6 6.0 settle.5
  757.9 11.2 %collective-permute-done.66 = bf16[128,2048]{1,0:T(8,128)(2,1)} collective-permute-done((bf16[128,2048]{1,0:T(8,128)(2,1)}, bf16[128,2048]{1,0:T(8,128)(2,1)}, u32[]{:S(2)}, u32[]{:S(2)}) %collective-permute-start.66) | collective-permute-done | bytes 524320 | tf_op jit(solution)/shard_map/ppermute | solution.py:681
  771.2 2.5 fusion.6
  (458 shorter events, 160.7 us)
Async XLA Ops:
  7.2 369.9 %all-gather.3.cloned.1.call-start = ((), (), s32[]{:S(2)}) async-start(), calls=%async_computation.8 | async-start | bytes 17301504 | tf_op jit(solution)/shard_map/all_gather | solution.py:893
  18.9 14.6 %collective-permute-start.27 = (bf16[128,2048]{1,0:T(8,128)(2,1)S(1)}, bf16[128,2048]{1,0:T(8,128)(2,1)S(1)}, u32[]{:S(2)}, u32[]{:S(2)}) collective-permute-start(bf16[128,2048]{1,0:T(8,128)(2,1)S(1)} %fusion.5.refs_0_), channel_id=1, source_target_pairs={{0,6},{2,0},{4,2},{6,4},{1,7},{3,1},{5,3},{7,5},{8,14},{10,8},{12,... | collective-permute-start | bytes 1572872 | tf_op jit(solution)/shard_map/ppermute | solution.py:681
  33.4 9.3 %collective-permute-start.28 = (bf16[128,2048]{1,0:T(8,128)(2,1)S(1)}, bf16[128,2048]{1,0:T(8,128)(2,1)}, u32[]{:S(2)}, u32[]{:S(2)}) collective-permute-start(bf16[128,2048]{1,0:T(8,128)(2,1)S(1)} %collective-permute-done.27.refs_24_), channel_id=1, source_target_pairs={{0,8},{1,17},{2,10},{3,19},{4,12},{5,21},{6,14},{7,23},{8,0},{9,25... | collective-permute-start | bytes 1572872 | tf_op jit(solution)/shard_map/ppermute | solution.py:701
  42.7 9.5 %collective-permute-start.30 = (bf16[128,2048]{1,0:T(8,128)(2,1)}, bf16[128,2048]{1,0:T(8,128)(2,1)}, u32[]{:S(2)}, u32[]{:S(2)}) collective-permute-start(bf16[128,2048]{1,0:T(8,128)(2,1)} %collective-permute-done.28.refs_25_), channel_id=1, source_target_pairs={{0,16},{1,9},{2,18},{3,11},{4,20},{5,13},{6,22},{7,15},{8,24},{9,1... | collective-permute-start | bytes 1572872 | tf_op jit(solution)/shard_map/ppermute | solution.py:701
  54.5 34.9 %collective-permute-start.19 = (bf16[128,2048]{1,0:T(8,128)(2,1)S(1)}, bf16[128,2048]{1,0:T(8,128)(2,1)}, u32[]{:S(2)}, u32[]{:S(2)}) collective-permute-start(bf16[128,2048]{1,0:T(8,128)(2,1)S(1)} %fusion.5.refs_0_), channel_id=1, source_target_pairs={{0,4},{2,6},{4,0},{6,2},{1,5},{3,7},{5,1},{7,3},{8,12},{10,14},{12... | collective-permute-start | bytes 1572872 | tf_op jit(solution)/shard_map/ppermute | solution.py:681
  57.6 44.8 %collective-permute-start.11 = (bf16[128,2048]{1,0:T(8,128)(2,1)S(1)}, bf16[128,2048]{1,0:T(8,128)(2,1)S(1)}, u32[]{:S(2)}, u32[]{:S(2)}) collective-permute-start(bf16[128,2048]{1,0:T(8,128)(2,1)S(1)} %fusion.5.refs_0_), channel_id=1, source_target_pairs={{0,2},{2,4},{4,6},{6,0},{1,3},{3,5},{5,7},{7,1},{8,10},{10,12},{12... | collective-permute-start | bytes 1572872 | tf_op jit(solution)/shard_map/ppermute | solution.py:681
  58.1 55.1 %collective-permute-start.7 = (bf16[128,2048]{1,0:T(8,128)(2,1)S(1)}, bf16[128,2048]{1,0:T(8,128)(2,1)S(1)}, u32[]{:S(2)}, u32[]{:S(2)}) collective-permute-start(bf16[128,2048]{1,0:T(8,128)(2,1)S(1)} %fusion.5.refs_0_), channel_id=1, source_target_pairs={{0,1},{1,0},{2,3},{3,2},{4,5},{5,4},{6,7},{7,6},{8,9},{9,8},{10,11... | collective-permute-start | bytes 1572872 | tf_op jit(solution)/shard_map/ppermute | solution.py:685
  58.1 55.3 %collective-permute-start.5 = (bf16[128,2048]{1,0:T(8,128)(2,1)S(1)}, bf16[128,2048]{1,0:T(8,128)(2,1)}, u32[]{:S(2)}, u32[]{:S(2)}) collective-permute-start(bf16[128,2048]{1,0:T(8,128)(2,1)S(1)} %fusion.5.refs_0_), channel_id=1, source_target_pairs={{0,16},{1,9},{2,18},{3,11},{4,20},{5,13},{6,22},{7,15},{8,24},{9,1... | collective-permute-start | bytes 1572872 | tf_op jit(solution)/shard_map/ppermute | solution.py:701
  59.6 54.3 %collective-permute-start.4 = (bf16[128,2048]{1,0:T(8,128)(2,1)S(1)}, bf16[128,2048]{1,0:T(8,128)(2,1)}, u32[]{:S(2)}, u32[]{:S(2)}) collective-permute-start(bf16[128,2048]{1,0:T(8,128)(2,1)S(1)} %fusion.5.refs_0_), channel_id=1, source_target_pairs={{0,8},{1,17},{2,10},{3,19},{4,12},{5,21},{6,14},{7,23},{8,0},{9,25... | collective-permute-start | bytes 1572872 | tf_op jit(solution)/shard_map/ppermute | solution.py:701
  89.4 26.0 %collective-permute-start.31 = (bf16[128,2048]{1,0:T(8,128)(2,1)}, bf16[128,2048]{1,0:T(8,128)(2,1)}, u32[]{:S(2)}, u32[]{:S(2)}) collective-permute-start(bf16[128,2048]{1,0:T(8,128)(2,1)} %copy-done.88), channel_id=1, source_target_pairs={{0,1},{1,0},{2,3},{3,2},{4,5},{5,4},{6,7},{7,6},{8,9},{9,8},{10,11... | collective-permute-start | bytes 1572872 | tf_op jit(solution)/shard_map/ppermute | solution.py:685
  102.4 16.7 %collective-permute-start.29 = (bf16[128,2048]{1,0:T(8,128)(2,1)}, bf16[128,2048]{1,0:T(8,128)(2,1)}, u32[]{:S(2)}, u32[]{:S(2)}) collective-permute-start(bf16[128,2048]{1,0:T(8,128)(2,1)} %copy-done.88), channel_id=1, source_target_pairs={{0,16},{1,9},{2,18},{3,11},{4,20},{5,13},{6,22},{7,15},{8,24},{9,1... | collective-permute-start | bytes 1572872 | tf_op jit(solution)/shard_map/ppermute | solution.py:701
  105.9 68.4 %all-to-all-start = ((bf16[8,3,256,128]{3,2,1,0:T(8,128)(2,1)}), bf16[8,3,256,128]{3,2,1,0:T(8,128)(2,1)}, u32[]{:S(2)}, u32[]{:S(2)}) async-start(bf16[8,3,256,128]{3,2,1,0:T(8,128)(2,1)} %bitcast.235), calls=%async_computation | async-start | bytes 3145728 | tf_op jit(solution)/shard_map/all_to_all | solution.py:746
  113.4 16.7 %collective-permute-start.21 = (bf16[128,2048]{1,0:T(8,128)(2,1)}, bf16[128,2048]{1,0:T(8,128)(2,1)S(1)}, u32[]{:S(2)}, u32[]{:S(2)}) collective-permute-start(bf16[128,2048]{1,0:T(8,128)(2,1)} %collective-permute-done.19.refs_16_), channel_id=1, source_target_pairs={{0,16},{1,9},{2,18},{3,11},{4,20},{5,13},{6,22},{7,15},{8,24},{9,1... | collective-permute-start | bytes 1572872 | tf_op jit(solution)/shard_map/ppermute | solution.py:701
  113.9 24.6 %collective-permute-start.20 = (bf16[128,2048]{1,0:T(8,128)(2,1)}, bf16[128,2048]{1,0:T(8,128)(2,1)S(1)}, u32[]{:S(2)}, u32[]{:S(2)}) collective-permute-start(bf16[128,2048]{1,0:T(8,128)(2,1)} %collective-permute-done.19.refs_16_), channel_id=1, source_target_pairs={{0,8},{1,17},{2,10},{3,19},{4,12},{5,21},{6,14},{7,23},{8,0},{9,25... | collective-permute-start | bytes 1572872 | tf_op jit(solution)/shard_map/ppermute | solution.py:701
  115.4 24.7 %collective-permute-start.15 = (bf16[128,2048]{1,0:T(8,128)(2,1)S(1)}, bf16[128,2048]{1,0:T(8,128)(2,1)S(1)}, u32[]{:S(2)}, u32[]{:S(2)}) collective-permute-start(bf16[128,2048]{1,0:T(8,128)(2,1)S(1)} %collective-permute-done.11.refs_8_), channel_id=1, source_target_pairs={{0,1},{1,0},{2,3},{3,2},{4,5},{5,4},{6,7},{7,6},{8,9},{9,8},{10,11... | collective-permute-start | bytes 1572872 | tf_op jit(solution)/shard_map/ppermute | solution.py:685
  119.0 21.9 %collective-permute-start.13 = (bf16[128,2048]{1,0:T(8,128)(2,1)S(1)}, bf16[128,2048]{1,0:T(8,128)(2,1)S(1)}, u32[]{:S(2)}, u32[]{:S(2)}) collective-permute-start(bf16[128,2048]{1,0:T(8,128)(2,1)S(1)} %collective-permute-done.11.refs_8_), channel_id=1, source_target_pairs={{0,16},{1,9},{2,18},{3,11},{4,20},{5,13},{6,22},{7,15},{8,24},{9,1... | collective-permute-start | bytes 1572872 | tf_op jit(solution)/shard_map/ppermute | solution.py:701
  119.8 29.3 %collective-permute-start.12 = (bf16[128,2048]{1,0:T(8,128)(2,1)S(1)}, bf16[128,2048]{1,0:T(8,128)(2,1)S(1)}, u32[]{:S(2)}, u32[]{:S(2)}) collective-permute-start(bf16[128,2048]{1,0:T(8,128)(2,1)S(1)} %collective-permute-done.11.refs_8_), channel_id=1, source_target_pairs={{0,8},{1,17},{2,10},{3,19},{4,12},{5,21},{6,14},{7,23},{8,0},{9,25... | collective-permute-start | bytes 1572872 | tf_op jit(solution)/shard_map/ppermute | solution.py:701
  130.1 19.5 %collective-permute-start.8 = (bf16[128,2048]{1,0:T(8,128)(2,1)}, bf16[128,2048]{1,0:T(8,128)(2,1)}, u32[]{:S(2)}, u32[]{:S(2)}) collective-permute-start(bf16[128,2048]{1,0:T(8,128)(2,1)} %collective-permute-done.4.refs_1_), channel_id=1, source_target_pairs={{0,1},{1,0},{2,3},{3,2},{4,5},{5,4},{6,7},{7,6},{8,9},{9,8},{10,11... | collective-permute-start | bytes 1572872 | tf_op jit(solution)/shard_map/ppermute | solution.py:685
  138.6 12.6 %collective-permute-start.6 = (bf16[128,2048]{1,0:T(8,128)(2,1)}, bf16[128,2048]{1,0:T(8,128)(2,1)}, u32[]{:S(2)}, u32[]{:S(2)}) collective-permute-start(bf16[128,2048]{1,0:T(8,128)(2,1)} %collective-permute-done.4.refs_1_), channel_id=1, source_target_pairs={{0,16},{1,9},{2,18},{3,11},{4,20},{5,13},{6,22},{7,15},{8,24},{9,1... | collective-permute-start | bytes 1572872 | tf_op jit(solution)/shard_map/ppermute | solution.py:701
  140.1 9.0 %collective-permute-start.9 = (bf16[128,2048]{1,0:T(8,128)(2,1)}, bf16[128,2048]{1,0:T(8,128)(2,1)}, u32[]{:S(2)}, u32[]{:S(2)}) collective-permute-start(bf16[128,2048]{1,0:T(8,128)(2,1)} %collective-permute-done.5.refs_2_), channel_id=1, source_target_pairs={{0,1},{1,0},{2,3},{3,2},{4,5},{5,4},{6,7},{7,6},{8,9},{9,8},{10,11... | collective-permute-start | bytes 1572872 | tf_op jit(solution)/shard_map/ppermute | solution.py:685
  140.9 13.2 %collective-permute-start.33 = (bf16[128,2048]{1,0:T(8,128)(2,1)}, bf16[128,2048]{1,0:T(8,128)(2,1)}, u32[]{:S(2)}, u32[]{:S(2)}) collective-permute-start(bf16[128,2048]{1,0:T(8,128)(2,1)} %collective-permute-done.29.refs_26_), channel_id=1, source_target_pairs={{0,1},{1,0},{2,3},{3,2},{4,5},{5,4},{6,7},{7,6},{8,9},{9,8},{10,11... | collective-permute-start | bytes 1572872 | tf_op jit(solution)/shard_map/ppermute | solution.py:685
  149.1 7.8 collective-permute-start.32
  149.2 8.5 %collective-permute-start.24 = (bf16[128,2048]{1,0:T(8,128)(2,1)}, bf16[128,2048]{1,0:T(8,128)(2,1)}, u32[]{:S(2)}, u32[]{:S(2)}) collective-permute-start(bf16[128,2048]{1,0:T(8,128)(2,1)} %copy-done.90), channel_id=1, source_target_pairs={{0,1},{1,0},{2,3},{3,2},{4,5},{5,4},{6,7},{7,6},{8,9},{9,8},{10,11... | collective-permute-start | bytes 1572872 | tf_op jit(solution)/shard_map/ppermute | solution.py:685
  149.7 9.5 %collective-permute-start.22 = (bf16[128,2048]{1,0:T(8,128)(2,1)}, bf16[128,2048]{1,0:T(8,128)(2,1)}, u32[]{:S(2)}, u32[]{:S(2)}) collective-permute-start(bf16[128,2048]{1,0:T(8,128)(2,1)} %copy-done.90), channel_id=1, source_target_pairs={{0,16},{1,9},{2,18},{3,11},{4,20},{5,13},{6,22},{7,15},{8,24},{9,1... | collective-permute-start | bytes 1572872 | tf_op jit(solution)/shard_map/ppermute | solution.py:701
  154.1 17.9 %collective-permute-start.14 = (bf16[128,2048]{1,0:T(8,128)(2,1)S(1)}, bf16[128,2048]{1,0:T(8,128)(2,1)}, u32[]{:S(2)}, u32[]{:S(2)}) collective-permute-start(bf16[128,2048]{1,0:T(8,128)(2,1)S(1)} %collective-permute-done.12.refs_9_), channel_id=1, source_target_pairs={{0,16},{1,9},{2,18},{3,11},{4,20},{5,13},{6,22},{7,15},{8,24},{9,1... | collective-permute-start | bytes 1572872 | tf_op jit(solution)/shard_map/ppermute | solution.py:701
  156.8 17.5 %collective-permute-start.16 = (bf16[128,2048]{1,0:T(8,128)(2,1)S(1)}, bf16[128,2048]{1,0:T(8,128)(2,1)}, u32[]{:S(2)}, u32[]{:S(2)}) collective-permute-start(bf16[128,2048]{1,0:T(8,128)(2,1)S(1)} %collective-permute-done.12.refs_9_), channel_id=1, source_target_pairs={{0,1},{1,0},{2,3},{3,2},{4,5},{5,4},{6,7},{7,6},{8,9},{9,8},{10,11... | collective-permute-start | bytes 1572872 | tf_op jit(solution)/shard_map/ppermute | solution.py:685
  156.9 17.4 %collective-permute-start.17 = (bf16[128,2048]{1,0:T(8,128)(2,1)S(1)}, bf16[128,2048]{1,0:T(8,128)(2,1)}, u32[]{:S(2)}, u32[]{:S(2)}) collective-permute-start(bf16[128,2048]{1,0:T(8,128)(2,1)S(1)} %collective-permute-done.13.refs_10_), channel_id=1, source_target_pairs={{0,1},{1,0},{2,3},{3,2},{4,5},{5,4},{6,7},{7,6},{8,9},{9,8},{10,11... | collective-permute-start | bytes 1572872 | tf_op jit(solution)/shard_map/ppermute | solution.py:685
  157.6 16.7 %collective-permute-start.10 = (bf16[128,2048]{1,0:T(8,128)(2,1)}, bf16[128,2048]{1,0:T(8,128)(2,1)S(1)}, u32[]{:S(2)}, u32[]{:S(2)}) collective-permute-start(bf16[128,2048]{1,0:T(8,128)(2,1)} %collective-permute-done.6.refs_3_), channel_id=1, source_target_pairs={{0,1},{1,0},{2,3},{3,2},{4,5},{5,4},{6,7},{7,6},{8,9},{9,8},{10,11... | collective-permute-start | bytes 1572872 | tf_op jit(solution)/shard_map/ppermute | solution.py:685
  159.2 16.0 %collective-permute-start.26 = (bf16[128,2048]{1,0:T(8,128)(2,1)}, bf16[128,2048]{1,0:T(8,128)(2,1)}, u32[]{:S(2)}, u32[]{:S(2)}) collective-permute-start(bf16[128,2048]{1,0:T(8,128)(2,1)} %collective-permute-done.22.refs_19_), channel_id=1, source_target_pairs={{0,1},{1,0},{2,3},{3,2},{4,5},{5,4},{6,7},{7,6},{8,9},{9,8},{10,11... | collective-permute-start | bytes 1572872 | tf_op jit(solution)/shard_map/ppermute | solution.py:685
  211.4 10.5 %collective-permute-start.36 = (bf16[2,4,160,128]{3,2,1,0:T(8,128)(2,1)S(1)}, bf16[2,4,160,128]{3,2,1,0:T(8,128)(2,1)S(1)}, u32[]{:S(2)}, u32[]{:S(2)}) collective-permute-start(bf16[2,4,160,128]{3,2,1,0:T(8,128)(2,1)S(1)} %fusion.23), channel_id=1, source_target_pairs={{0,16},{16,0},{1,17},{17,1},{2,18},{18,2},{3,19},{19,3},{4,20},{20... | collective-permute-start | bytes 983048 | tf_op jit(solution)/shard_map/ppermute | solution.py:796
  223.8 8.2 %collective-permute-start.37 = (bf16[4,160,128]{2,1,0:T(8,128)(2,1)}, bf16[4,160,128]{2,1,0:T(8,128)(2,1)}, u32[]{:S(2)}, u32[]{:S(2)}) collective-permute-start(bf16[4,160,128]{2,1,0:T(8,128)(2,1)} %fusion.25), channel_id=1, source_target_pairs={{0,8},{8,0},{1,9},{9,1},{2,10},{10,2},{3,11},{11,3},{4,12},{12,4},... | collective-permute-start | bytes 491528 | tf_op jit(solution)/shard_map/ppermute | solution.py:796
  226.3 71.6 %all-to-all-start.1 = ((bf16[8,3,256,128]{3,2,1,0:T(8,128)(2,1)}), bf16[8,3,256,128]{3,2,1,0:T(8,128)(2,1)}, u32[]{:S(2)}, u32[]{:S(2)}) async-start(bf16[8,3,256,128]{3,2,1,0:T(8,128)(2,1)} %bitcast.52), calls=%async_computation.1 | async-start | bytes 3145728 | tf_op jit(solution)/shard_map/all_to_all | solution.py:746
  233.0 35.9 %collective-permute-start.38 = (bf16[160,128]{1,0:T(8,128)(2,1)S(1)}, bf16[160,128]{1,0:T(8,128)(2,1)S(1)}, u32[]{:S(2)}, u32[]{:S(2)}) collective-permute-start(bf16[160,128]{1,0:T(8,128)(2,1)S(1)} %get-tuple-element.179), channel_id=1, source_target_pairs={{0,2},{2,4},{4,6},{6,0},{1,3},{3,5},{5,7},{7,1},{8,10},{10,12},{12... | collective-permute-start | bytes 122888 | tf_op jit(solution)/shard_map/ppermute | solution.py:681
  234.6 36.9 %collective-permute-start.40 = (bf16[160,128]{1,0:T(8,128)(2,1)S(1)}, bf16[160,128]{1,0:T(8,128)(2,1)S(1)}, u32[]{:S(2)}, u32[]{:S(2)}) collective-permute-start(bf16[160,128]{1,0:T(8,128)(2,1)S(1)} %get-tuple-element.180), channel_id=1, source_target_pairs={{0,6},{2,0},{4,2},{6,4},{1,7},{3,1},{5,3},{7,5},{8,14},{10,8},{12,... | collective-permute-start | bytes 122888 | tf_op jit(solution)/shard_map/ppermute | solution.py:681
  235.5 36.0 %collective-permute-start.39 = (bf16[160,128]{1,0:T(8,128)(2,1)S(1)}, bf16[160,128]{1,0:T(8,128)(2,1)S(1)}, u32[]{:S(2)}, u32[]{:S(2)}) collective-permute-start(bf16[160,128]{1,0:T(8,128)(2,1)S(1)} %get-tuple-element.181), channel_id=1, source_target_pairs={{0,4},{2,6},{4,0},{6,2},{1,5},{3,7},{5,1},{7,3},{8,12},{10,14},{12... | collective-permute-start | bytes 122888 | tf_op jit(solution)/shard_map/ppermute | solution.py:681
  284.5 7.5 collective-permute-start.45
  302.6 74.5 %all-to-all-start.2 = ((bf16[8,3,256,128]{3,2,1,0:T(8,128)(2,1)}), bf16[8,3,256,128]{3,2,1,0:T(8,128)(2,1)S(1)}, u32[]{:S(2)}, u32[]{:S(2)}) async-start(bf16[8,3,256,128]{3,2,1,0:T(8,128)(2,1)} %bitcast.270), calls=%async_computation.2 | async-start | bytes 3145728 | tf_op jit(solution)/shard_map/all_to_all | solution.py:746
  308.3 465.4 %reduce-scatter.2.cloned.1.call-start = ((), (), s32[]{:S(2)}) async-start(), calls=%async_computation.7 | async-start | bytes 17301504 | tf_op jit(solution)/shard_map/reduce_scatter | solution.py:967
  476.4 9.8 %collective-permute-start.48 = (bf16[2,4,160,128]{3,2,1,0:T(8,128)(2,1)S(1)}, bf16[2,4,160,128]{3,2,1,0:T(8,128)(2,1)S(1)}, u32[]{:S(2)}, u32[]{:S(2)}) collective-permute-start(bf16[2,4,160,128]{3,2,1,0:T(8,128)(2,1)S(1)} %fusion.24), channel_id=1, source_target_pairs={{0,16},{16,0},{1,17},{17,1},{2,18},{18,2},{3,19},{19,3},{4,20},{20... | collective-permute-start | bytes 983048 | tf_op jit(solution)/shard_map/ppermute | solution.py:796
  492.2 15.2 %collective-permute-start.50 = (bf16[160,128]{1,0:T(8,128)(2,1)S(1)}, bf16[160,128]{1,0:T(8,128)(2,1)S(1)}, u32[]{:S(2)}, u32[]{:S(2)}) collective-permute-start(bf16[160,128]{1,0:T(8,128)(2,1)S(1)} %get-tuple-element.174), channel_id=1, source_target_pairs={{0,2},{2,4},{4,6},{6,0},{1,3},{3,5},{5,7},{7,1},{8,10},{10,12},{12... | collective-permute-start | bytes 122888 | tf_op jit(solution)/shard_map/ppermute | solution.py:681
  493.9 16.6 %collective-permute-start.52 = (bf16[160,128]{1,0:T(8,128)(2,1)S(1)}, bf16[160,128]{1,0:T(8,128)(2,1)S(1)}, u32[]{:S(2)}, u32[]{:S(2)}) collective-permute-start(bf16[160,128]{1,0:T(8,128)(2,1)S(1)} %get-tuple-element.175), channel_id=1, source_target_pairs={{0,6},{2,0},{4,2},{6,4},{1,7},{3,1},{5,3},{7,5},{8,14},{10,8},{12,... | collective-permute-start | bytes 122888 | tf_op jit(solution)/shard_map/ppermute | solution.py:681
  503.2 8.7 %collective-permute-start.51 = (bf16[160,128]{1,0:T(8,128)(2,1)S(1)}, bf16[160,128]{1,0:T(8,128)(2,1)S(1)}, u32[]{:S(2)}, u32[]{:S(2)}) collective-permute-start(bf16[160,128]{1,0:T(8,128)(2,1)S(1)} %get-tuple-element.176), channel_id=1, source_target_pairs={{0,4},{2,6},{4,0},{6,2},{1,5},{3,7},{5,1},{7,3},{8,12},{10,14},{12... | collective-permute-start | bytes 122888 | tf_op jit(solution)/shard_map/ppermute | solution.py:681
  514.7 7.5 collective-permute-start.53
  530.0 24.7 %collective-permute-start.57 = (bf16[2,4,160,128]{3,2,1,0:T(8,128)(2,1)}, bf16[2,4,160,128]{3,2,1,0:T(8,128)(2,1)}, u32[]{:S(2)}, u32[]{:S(2)}) collective-permute-start(bf16[2,4,160,128]{3,2,1,0:T(8,128)(2,1)} %pad_maximum_fusion.5), channel_id=1, source_target_pairs={{0,16},{16,0},{1,17},{17,1},{2,18},{18,2},{3,19},{19,3},{4,20},{20... | collective-permute-start | bytes 983048 | tf_op jit(solution)/shard_map/ppermute | solution.py:811
  547.9 93.7 %all-to-all-start.4 = ((bf16[8,256,384]{2,1,0:T(8,128)(2,1)}), bf16[8,256,384]{2,1,0:T(8,128)(2,1)S(1)}, u32[]{:S(2)}, u32[]{:S(2)}) async-start(bf16[8,256,384]{2,1,0:T(8,128)(2,1)} %copy-done.7), calls=%async_computation.5 | async-start | bytes 3145728 | tf_op jit(solution)/shard_map/all_to_all | solution.py:746
  556.0 16.6 %collective-permute-start.58 = (bf16[2,2,4,160,128]{4,3,2,1,0:T(8,128)(2,1)S(1)}, bf16[2,2,4,160,128]{4,3,2,1,0:T(8,128)(2,1)S(1)}, u32[]{:S(2)}, u32[]{:S(2)}) collective-permute-start(bf16[2,2,4,160,128]{4,3,2,1,0:T(8,128)(2,1)S(1)} %pad_maximum_fusion.3), channel_id=1, source_target_pairs={{0,1},{1,0},{2,3},{3,2},{4,5},{5,4},{6,7},{7,6},{8,9},{9,8},{10,11... | collective-permute-start | bytes 1966088 | tf_op jit(solution)/shard_map/ppermute | solution.py:811
  600.5 46.1 %collective-permute-start.71 = (bf16[4,128,2048]{2,1,0:T(8,128)(2,1)}, bf16[4,128,2048]{2,1,0:T(8,128)(2,1)}, u32[]{:S(2)}, u32[]{:S(2)}) collective-permute-start(bf16[4,128,2048]{2,1,0:T(8,128)(2,1)} %get-tuple-element.90), channel_id=1, source_target_pairs={{0,1},{1,0},{2,3},{3,2},{4,5},{5,4},{6,7},{7,6},{8,9},{9,8},{10,11... | collective-permute-start | bytes 6291464 | tf_op jit(solution)/shard_map/ppermute | solution.py:685
  608.7 40.7 %collective-permute-start.67 = (bf16[4,128,2048]{2,1,0:T(8,128)(2,1)}, bf16[4,128,2048]{2,1,0:T(8,128)(2,1)}, u32[]{:S(2)}, u32[]{:S(2)}) collective-permute-start(bf16[4,128,2048]{2,1,0:T(8,128)(2,1)} %get-tuple-element.88), channel_id=1, source_target_pairs={{0,1},{1,0},{2,3},{3,2},{4,5},{5,4},{6,7},{7,6},{8,9},{9,8},{10,11... | collective-permute-start | bytes 6291464 | tf_op jit(solution)/shard_map/ppermute | solution.py:685
  616.6 36.0 %collective-permute-start.63 = (bf16[4,128,2048]{2,1,0:T(8,128)(2,1)}, bf16[4,128,2048]{2,1,0:T(8,128)(2,1)}, u32[]{:S(2)}, u32[]{:S(2)}) collective-permute-start(bf16[4,128,2048]{2,1,0:T(8,128)(2,1)} %get-tuple-element.86), channel_id=1, source_target_pairs={{0,1},{1,0},{2,3},{3,2},{4,5},{5,4},{6,7},{7,6},{8,9},{9,8},{10,11... | collective-permute-start | bytes 6291464 | tf_op jit(solution)/shard_map/ppermute | solution.py:685
  624.9 30.0 %collective-permute-start.59 = (bf16[4,128,2048]{2,1,0:T(8,128)(2,1)}, bf16[4,128,2048]{2,1,0:T(8,128)(2,1)}, u32[]{:S(2)}, u32[]{:S(2)}) collective-permute-start(bf16[4,128,2048]{2,1,0:T(8,128)(2,1)} %get-tuple-element.84), channel_id=1, source_target_pairs={{0,1},{1,0},{2,3},{3,2},{4,5},{5,4},{6,7},{7,6},{8,9},{9,8},{10,11... | collective-permute-start | bytes 6291464 | tf_op jit(solution)/shard_map/ppermute | solution.py:685
  641.6 43.0 %all-to-all-start.3 = ((bf16[8,256,384]{2,1,0:T(8,128)(2,1)}), bf16[8,256,384]{2,1,0:T(8,128)(2,1)}, u32[]{:S(2)}, u32[]{:S(2)}) async-start(bf16[8,256,384]{2,1,0:T(8,128)(2,1)} %copy-done.8), calls=%async_computation.4 | async-start | bytes 3145728 | tf_op jit(solution)/shard_map/all_to_all | solution.py:746
  648.7 14.9 %collective-permute-start.72 = (bf16[2,128,2048]{2,1,0:T(8,128)(2,1)S(1)}, bf16[2,128,2048]{2,1,0:T(8,128)(2,1)S(1)}, u32[]{:S(2)}, u32[]{:S(2)}) collective-permute-start(bf16[2,128,2048]{2,1,0:T(8,128)(2,1)S(1)} %add_convert_fusion), channel_id=1, source_target_pairs={{0,16},{1,9},{2,18},{3,11},{4,20},{5,13},{6,22},{7,15},{8,24},{9,1... | collective-permute-start | bytes 3145736 | tf_op jit(solution)/shard_map/ppermute | solution.py:701
  651.0 29.4 %collective-permute-start.68 = (bf16[2,128,2048]{2,1,0:T(8,128)(2,1)S(1)}, bf16[2,128,2048]{2,1,0:T(8,128)(2,1)S(1)}, u32[]{:S(2)}, u32[]{:S(2)}) collective-permute-start(bf16[2,128,2048]{2,1,0:T(8,128)(2,1)S(1)} %add_convert_fusion.1), channel_id=1, source_target_pairs={{0,16},{1,9},{2,18},{3,11},{4,20},{5,13},{6,22},{7,15},{8,24},{9,1... | collective-permute-start | bytes 3145736 | tf_op jit(solution)/shard_map/ppermute | solution.py:701
  654.2 43.2 %collective-permute-start.64 = (bf16[2,128,2048]{2,1,0:T(8,128)(2,1)S(1)}, bf16[2,128,2048]{2,1,0:T(8,128)(2,1)}, u32[]{:S(2)}, u32[]{:S(2)}) collective-permute-start(bf16[2,128,2048]{2,1,0:T(8,128)(2,1)S(1)} %add_convert_fusion.2), channel_id=1, source_target_pairs={{0,16},{1,9},{2,18},{3,11},{4,20},{5,13},{6,22},{7,15},{8,24},{9,1... | collective-permute-start | bytes 3145736 | tf_op jit(solution)/shard_map/ppermute | solution.py:701
  657.4 56.8 %collective-permute-start.60 = (bf16[2,128,2048]{2,1,0:T(8,128)(2,1)}, bf16[2,128,2048]{2,1,0:T(8,128)(2,1)}, u32[]{:S(2)}, u32[]{:S(2)}) collective-permute-start(bf16[2,128,2048]{2,1,0:T(8,128)(2,1)} %add_convert_fusion.3), channel_id=1, source_target_pairs={{0,16},{1,9},{2,18},{3,11},{4,20},{5,13},{6,22},{7,15},{8,24},{9,1... | collective-permute-start | bytes 3145736 | tf_op jit(solution)/shard_map/ppermute | solution.py:701
  666.2 90.9 %collective-permute-start.73 = (bf16[128,2048]{1,0:T(8,128)(2,1)}, bf16[128,2048]{1,0:T(8,128)(2,1)}, u32[]{:S(2)}, u32[]{:S(2)}) collective-permute-start(bf16[128,2048]{1,0:T(8,128)(2,1)} %fusion.20), channel_id=1, source_target_pairs={{0,8},{1,17},{2,10},{3,19},{4,12},{5,21},{6,14},{7,23},{8,0},{9,25... | collective-permute-start | bytes 1572872 | tf_op jit(solution)/shard_map/ppermute | solution.py:701
  682.9 34.6 %collective-permute-start.69 = (bf16[128,2048]{1,0:T(8,128)(2,1)}, bf16[128,2048]{1,0:T(8,128)(2,1)S(1)}, u32[]{:S(2)}, u32[]{:S(2)}) collective-permute-start(bf16[128,2048]{1,0:T(8,128)(2,1)} %fusion.19), channel_id=1, source_target_pairs={{0,8},{1,17},{2,10},{3,19},{4,12},{5,21},{6,14},{7,23},{8,0},{9,25... | collective-permute-start | bytes 1572872 | tf_op jit(solution)/shard_map/ppermute | solution.py:701
  684.6 65.9 %all-to-all-start.5 = ((bf16[8,256,384]{2,1,0:T(8,128)(2,1)}), bf16[8,256,384]{2,1,0:T(8,128)(2,1)}, u32[]{:S(2)}, u32[]{:S(2)}) async-start(bf16[8,256,384]{2,1,0:T(8,128)(2,1)} %feature_grad.5), calls=%async_computation.6 | async-start | bytes 3145728 | tf_op jit(solution)/shard_map/all_to_all | solution.py:746
  699.0 22.3 %collective-permute-start.65 = (bf16[128,2048]{1,0:T(8,128)(2,1)S(1)}, bf16[128,2048]{1,0:T(8,128)(2,1)S(1)}, u32[]{:S(2)}, u32[]{:S(2)}) collective-permute-start(bf16[128,2048]{1,0:T(8,128)(2,1)S(1)} %fusion.18), channel_id=1, source_target_pairs={{0,8},{1,17},{2,10},{3,19},{4,12},{5,21},{6,14},{7,23},{8,0},{9,25... | collective-permute-start | bytes 1572872 | tf_op jit(solution)/shard_map/ppermute | solution.py:701
  715.7 9.2 %collective-permute-start.61 = (bf16[128,2048]{1,0:T(8,128)(2,1)S(1)}, bf16[128,2048]{1,0:T(8,128)(2,1)S(1)}, u32[]{:S(2)}, u32[]{:S(2)}) collective-permute-start(bf16[128,2048]{1,0:T(8,128)(2,1)S(1)} %fusion.17), channel_id=1, source_target_pairs={{0,8},{1,17},{2,10},{3,19},{4,12},{5,21},{6,14},{7,23},{8,0},{9,25... | collective-permute-start | bytes 1572872 | tf_op jit(solution)/shard_map/ppermute | solution.py:701
  719.8 38.0 %collective-permute-start.70 = (bf16[128,2048]{1,0:T(8,128)(2,1)}, bf16[128,2048]{1,0:T(8,128)(2,1)}, u32[]{:S(2)}, u32[]{:S(2)}) collective-permute-start(bf16[128,2048]{1,0:T(8,128)(2,1)} %fusion.13), channel_id=1, source_target_pairs={{0,2},{2,4},{4,6},{6,0},{1,3},{3,5},{5,7},{7,1},{8,10},{10,12},{12... | collective-permute-start | bytes 1572872 | tf_op jit(solution)/shard_map/ppermute | solution.py:681
  723.8 45.3 %collective-permute-start.66 = (bf16[128,2048]{1,0:T(8,128)(2,1)}, bf16[128,2048]{1,0:T(8,128)(2,1)}, u32[]{:S(2)}, u32[]{:S(2)}) collective-permute-start(bf16[128,2048]{1,0:T(8,128)(2,1)} %fusion.14), channel_id=1, source_target_pairs={{0,4},{2,6},{4,0},{6,2},{1,5},{3,7},{5,1},{7,3},{8,12},{10,14},{12... | collective-permute-start | bytes 1572872 | tf_op jit(solution)/shard_map/ppermute | solution.py:681
  727.3 43.9 %collective-permute-start.62 = (bf16[128,2048]{1,0:T(8,128)(2,1)}, bf16[128,2048]{1,0:T(8,128)(2,1)}, u32[]{:S(2)}, u32[]{:S(2)}) collective-permute-start(bf16[128,2048]{1,0:T(8,128)(2,1)} %fusion.15), channel_id=1, source_target_pairs={{0,6},{2,0},{4,2},{6,4},{1,7},{3,1},{5,3},{7,5},{8,14},{10,8},{12,... | collective-permute-start | bytes 1572872 | tf_op jit(solution)/shard_map/ppermute | solution.py:681
  744.1 12.5 %collective-permute-start.75 = (f32[256]{0:T(256)S(1)}, f32[256]{0:T(256)S(1)}, u32[]{:S(2)}, u32[]{:S(2)}) collective-permute-start(f32[256]{0:T(256)S(1)} %add.596), channel_id=1, source_target_pairs={{0,8},{8,0},{1,9},{9,1},{2,10},{10,2},{3,11},{11,3},{4,12},{12,4},... | collective-permute-start | bytes 3080 | tf_op jit(solution)/shard_map/ppermute | solution.py:1019
  (116 other events, 2029.9 us)
Sparse Core Ops, SparseCore 0:
  54.6 160.3 all-gather.2
  406.1 225.7 reduce-scatter.1
where the time goes:
time: 789 us; the launch traced here: 783 us
  Pallas kernels  292 us (37%)
  waiting for transfers between devices  235 us (30%)
  starting transfers between devices  147 us (19%)
  other arithmetic  50.6 us (6%)
  local copies, waits for them, and re-layouts  42.1 us (5%)
  between operations  15.9 us (2%)
    ppermute x21, waiting for transfers between devices, shifted(): lax.ppermute(value, 'z', [(i, (i + by) % size) for i in range(size)])  112 us
    ppermute x20, waiting for transfers between devices, hop(): return lax.ppermute(value, team_axes, pairs)  79.8 us
    pallas_call x1, Pallas kernels, scan_backward(): pl.pallas_call(functools.partial(backward_kernel, dtw.shape[1] // mine),...  64.9 us
    pallas_call x1, Pallas kernels, scan_forward(): pl.pallas_call(functools.partial(forward_kernel, dtw.shape[1] // mine), g...  48.8 us
    pallas_call x3, Pallas kernels, feature_grad(): pl.pallas_call(functools.partial(grad_kernel, mods), grid=(wide // some,)...  47.2 us
    ppermute x21, starting transfers between devices, shifted(): lax.ppermute(value, 'z', [(i, (i + by) % size) for i in range(size)])  46.4 us
    pallas_call x5, Pallas kernels, trail_product(): pl.pallas_call(functools.partial(trail_kernel, mods, len(lefts), k), grid...  45.3 us
    all_to_all x6, starting transfers between devices, exchanged(): return lax.all_to_all(parts, group_axes, 0, 0, tiled=True)  35.7 us
  transfers between devices with their start and end apart: 84, of which 39 were waited for; matrix products, arithmetic and copies ran while one was open for 8% of the time, Pallas kernels for 34%

commit v1 on v0

--- a/solution.py
+++ b/solution.py
@@ -187,9 +187,9 @@
     )(places, facts, weight, *pieces)
 
 
-def trail_kernel(mods, count, first, *refs):
+def trail_kernel(mods, count, skipped, *refs):
     lefts, facts_ref, weights = refs[:count], refs[count], refs[count + 1 : 2 * count + 1]
-    outs = refs[2 * count + 1 :]
+    outs = refs[2 * count + 1 + skipped :]
     some, here, mine = lefts[0].shape
     label = label_column_of(facts_ref)
     total = None
@@ -207,7 +207,7 @@
                 out[...] = total
 
 
-def trail_product(lefts, facts, weights, mods, k=None):
+def trail_product(lefts, facts, weights, mods, k=None, beside=()):
     pieces, here, mine = lefts[0].shape
     features = weights[0].shape[0]
     if k is None:
@@ -224,11 +224,12 @@
             return (2 * k + 1 - i, 0, 0)
 
     return pl.pallas_call(
-        functools.partial(trail_kernel, mods, len(lefts), k),
+        functools.partial(trail_kernel, mods, len(lefts), len(beside)),
         grid=(steps,),
         in_specs=[pl.BlockSpec((4, here, mine), block) for _ in lefts]
         + [pl.BlockSpec((4, fact_columns, here), block)]
-        + [everything(weight) for weight in weights],
+        + [everything(weight) for weight in weights]
+        + [pl.BlockSpec(memory_space=pl.ANY) for _ in beside],
         out_specs=out_specs,
         out_shape=outs,
         compiler_params=params(),
@@ -236,10 +237,11 @@
             8 * steps * here * features * mods * mine * len(lefts), 8 * steps * here * features
         ),
         name="trail_product",
-    )(*lefts, facts, *weights)
-
-
-def grad_kernel(mods, x_ref, d_ref, facts_ref, out_ref, spread):
+    )(*lefts, facts, *weights, *beside)
+
+
+def grad_kernel(mods, x_ref, d_ref, facts_ref, *refs):
+    out_ref, spread = refs[-2:]
     pieces, here, mine = d_ref.shape
 
     @pl.when(pl.program_id(0) == 0)
@@ -251,7 +253,7 @@
     out_ref[0] = dot(x_ref[...], spread[...], ((0,), (0,))).astype(out_ref.dtype)
 
 
-def feature_grad(x, d, facts, mods, groups, dtype):
+def feature_grad(x, d, facts, mods, groups, dtype, beside=()):
     pieces, here, wide = x.shape
     mine = d.shape[2]
     some = min(256, wide)
@@ -263,14 +265,15 @@
             pl.BlockSpec((pieces * here, some), lambda i: (0, i)),
             everything(d),
             everything(facts),
-        ],
+        ]
+        + [pl.BlockSpec(memory_space=pl.ANY) for _ in beside],
         out_specs=pl.BlockSpec((1, some, mods * mine), lambda i: (i, 0, 0)),
         out_shape=out,
         scratch_shapes=[pltpu.VMEM((pieces * here, mods * mine), bf16)],
         compiler_params=params(),
         cost_estimate=cost(6 * pieces * here * wide * mods * mine, 2 * pieces * here * wide),
         name="feature_grad",
-    )(x.reshape(pieces * here, wide), d, facts)
+    )(x.reshape(pieces * here, wide), d, facts, *beside)
     return grad.reshape(groups, wide // groups, mods * mine)
 
 
@@ -364,14 +367,27 @@
         line[(rows + r) * here : (rows + r + 1) * here] = pltpu.roll(turned, here - narrow // 2, 1)
 
 
+def coefficient_tiles(proj_ref, rows, here, expand_ref, turned, tiles):
+    narrow = proj_ref.shape[2] - here
+    for r in range(rows):
+        small = proj_ref[r, 0, here:].astype(f32)
+        small = jnp.transpose(jnp.concatenate([small, jnp.zeros((here - narrow, here), f32)], axis=0))
+        turned[pl.ds(r, here, stride=2 * rows), :] = small
+        turned[pl.ds(rows + r, here, stride=2 * rows), :] = pltpu.roll(small, here - narrow // 2, 1)
+    some = 256
+    for i in range(turned.shape[0] // some):
+        part = slice(i * some, (i + 1) * some)
+        tiles[part] = dot(turned[part].astype(bf16), expand_ref[...], ((1,), (0,)))
+
+
 def scan_lines(r, rows, here, value, line):
     line[r * here : (r + 1) * here] = value
     line[(rows + r) * here : (rows + r + 1) * here] = value
 
 
 def forward_kernel(
-    mods, proj_ref, pre_ref, facts_ref, gate_ref, dtw_ref, dtb_ref, rate_ref, skip_ref, start_ref,
-    gated_ref, scanned_ref, dt_ref, kept_ref, end_ref, held, step_line, drive_line, coef_line, out_line,
+    mods, proj_ref, pre_ref, facts_ref, gate_ref, dtw_ref, dtb_ref, rate_ref, skip_ref, start_ref, expand_ref,
+    gated_ref, scanned_ref, dt_ref, kept_ref, end_ref, held, step_line, drive_line, turned, tiles, out_line,
 ):
     rows, here, mine = pre_ref.shape
     pieces, subl, _ = rate_ref.shape
@@ -380,7 +396,7 @@
     def _():
         held[...] = start_ref[...]
 
-    coefficient_lines(proj_ref, rows, here, coef_line)
+    coefficient_tiles(proj_ref, rows, here, expand_ref, turned, tiles)
     for r in range(rows):
         facts = columns_of(facts_ref[r, 0])
         label = facts[:, label_column : label_column + 1]
@@ -392,14 +408,15 @@
 
     def one(t, state):
         lines = pl.ds(t, subl, stride=here)
-        step, drive, coefs = step_line[lines, :], drive_line[lines, :], coef_line[lines, :]
+        step, drive = step_line[lines, :], drive_line[lines, :]
+        spot = pl.ds(pl.multiple_of(t * subl, subl), subl)
         emitted = None
         following = []
         for j in range(pieces):
             kept_ref[t, j] = state[j]
             decay = jnp.exp2(step * rate_ref[j])
-            now = decay * state[j] + drive * jnp.broadcast_to(coefs[:, j : j + 1], step.shape)
-            term = now * jnp.broadcast_to(coefs[:, pieces + j : pieces + j + 1], step.shape)
+            now = decay * state[j] + drive * tiles[spot, j * mine : (j + 1) * mine]
+            term = now * tiles[spot, (pieces + j) * mine : (pieces + j + 1) * mine]
             emitted = term if emitted is None else emitted + term
             following.append(now)
         out_line[lines, :] = emitted
@@ -427,6 +444,7 @@
     pieces, subl, _ = rates2.shape
     item = pl.BlockSpec((rows, here, mine), lambda i: (0, i, 0))
     line = pltpu.VMEM((subl * here, mine), f32)
+    expand = (jnp.arange(here)[:, None] == jnp.arange(2 * pieces * mine)[None, :] // mine).astype(bf16)
     return pl.pallas_call(
         functools.partial(forward_kernel, dtw.shape[1] // mine),
         grid=(blocks,),
@@ -436,7 +454,7 @@
             pl.BlockSpec((rows, 1, fact_columns, here), lambda i: (0, i, 0, 0)),
             item,
         ]
-        + [everything(array) for array in (dtw, dtb, rates2, skip, start)],
+        + [everything(array) for array in (dtw, dtb, rates2, skip, start, expand)],
         out_specs=[
             item,
             item,
@@ -451,17 +469,18 @@
             shape((length, pieces, subl, mine), f32),
             shape(start.shape, f32),
         ],
-        scratch_shapes=[pltpu.VMEM(start.shape, f32), line, line, line, line],
+        scratch_shapes=[pltpu.VMEM(start.shape, f32), line, line, line]
+        + [pltpu.VMEM((subl * here, 2 * pieces * mine), f32), line],
         compiler_params=params(),
         cost_estimate=cost(5500 * length * pieces * subl * mine, 5 * length * pieces * subl * mine),
         name="scan_forward",
-    )(proj, pre, facts, gate, dtw, dtb, rates2, skip, start)
+    )(proj, pre, facts, gate, dtw, dtb, rates2, skip, start, expand)
 
 
 def backward_kernel(
     mods, tables, proj_ref, pre_ref, facts_ref, gate_ref, scanned_ref, dt_ref, d_gated_ref, kept_ref, dtw_ref, rate2_ref,
-    rate_ref, skip_ref, last_ref, carry_ref, sum_ref, d_gate_ref, d_proj_ref, d_act_ref, dtw_grad_ref, dtb_grad_ref,
-    skip_grad_ref, rate_sum_ref, carry_out_ref, carried, later, products, step_line, drive_line, coef_line, back_line,
+    rate_ref, skip_ref, last_ref, carry_ref, sum_ref, expand_ref, d_gate_ref, d_proj_ref, d_act_ref, dtw_grad_ref, dtb_grad_ref,
+    skip_grad_ref, rate_sum_ref, carry_out_ref, carried, later, products, step_line, drive_line, turned, tiles, back_line,
     pulled_line, weighted_line, small_line,
 ):
     rows, here, mine = pre_ref.shape
@@ -477,7 +496,7 @@
         for ref in (rate_sum_ref, dtw_grad_ref, dtb_grad_ref, skip_grad_ref):
             ref[...] = jnp.zeros_like(ref)
 
-    coefficient_lines(proj_ref, rows, here, coef_line)
+    coefficient_tiles(proj_ref, rows, here, expand_ref, turned, tiles)
     for r in range(rows):
         facts = columns_of(facts_ref[r, 0])
         step, activated = softplus(dt_ref[r]), apply_silu(pre_ref[r])
@@ -491,16 +510,17 @@
 
     def one(t, carry, state):
         lines = pl.ds(t, subl, stride=here)
-        step, drive, coefs, back = step_line[lines, :], drive_line[lines, :], coef_line[lines, :], back_line[lines, :]
+        step, drive, back = step_line[lines, :], drive_line[lines, :], back_line[lines, :]
+        row = pl.ds(pl.multiple_of(t * subl, subl), subl)
         pulled_sum, weighted_sum = None, None
         new_carry, new_state, terms, sums = [], [], [], []
         for j in range(pieces):
             before = kept_ref[t, j]
             decay = jnp.exp2(step * rate2_ref[j])
-            adjoint = back * jnp.broadcast_to(coefs[:, pieces + j : pieces + j + 1], step.shape) + carry[j]
+            adjoint = back * tiles[row, (pieces + j) * mine : (pieces + j + 1) * mine] + carry[j]
             passed = decay * adjoint
             pulled = passed * before
-            weighted = adjoint * jnp.broadcast_to(coefs[:, j : j + 1], step.shape)
+            weighted = adjoint * tiles[row, j * mine : (j + 1) * mine]
             first = pulled * rate_ref[j]
             pulled_sum = first if pulled_sum is None else pulled_sum + first
             weighted_sum = weighted if weighted_sum is None else weighted_sum + weighted
@@ -562,6 +582,7 @@
     item = pl.BlockSpec((rows, here, mine), lambda i: (0, blocks - 1 - i, 0))
     proj_item = pl.BlockSpec((rows, 1, deep, here), lambda i: (0, blocks - 1 - i, 0, 0))
     columns = 2 * pieces * mine
+    expand = (jnp.arange(here)[:, None] == jnp.arange(columns)[None, :] // mine).astype(bf16)
     summing = (jnp.arange(columns)[:, None] // mine == jnp.arange(lanes)[None, :]).astype(bf16)
     d_gate = shape((rows * blocks, here, mine), bf16)
     line = pltpu.VMEM((subl * here, mine), f32)
@@ -580,14 +601,15 @@
             item,
             pl.BlockSpec((here, pieces, subl, mine), lambda i: (blocks - 1 - i, 0, 0, 0)),
         ]
-        + [everything(array) for array in (dtw, rates2, rates, skip, last, carry, summing)],
+        + [everything(array) for array in (dtw, rates2, rates, skip, last, carry, summing, expand)],
         out_specs=[everything(d_gate), proj_item, item] + [everything(array) for array in small + [carry]],
         out_shape=[d_gate, shape(proj.shape, bf16), shape(pre.shape, f32)] + small + [shape(carry.shape, f32)],
-        scratch_shapes=[pltpu.VMEM(carry.shape, f32)] * 2 + [pltpu.VMEM((subl * here, columns), bf16)] + [line] * 7,
+        scratch_shapes=[pltpu.VMEM(carry.shape, f32)] * 2 + [pltpu.VMEM((subl * here, columns), bf16)] + [line] * 3
+        + [pltpu.VMEM((subl * here, columns), f32)] + [line] * 4,
         compiler_params=params(),
         cost_estimate=cost(7500 * length * pieces * subl * mine, 5 * length * pieces * subl * mine),
         name="scan_backward",
-    )(tables, proj, pre, facts, gate, scanned, dt_pre, d_gated, kept, dtw, rates2, rates, skip, last, carry, summing)
+    )(tables, proj, pre, facts, gate, scanned, dt_pre, d_gated, kept, dtw, rates2, rates, skip, last, carry, summing, expand)
 
 
 def deconv_kernel(
@@ -713,33 +735,84 @@
     return (((((y + flip_y) % 2) * 2 + (x + flip_x) % 2) * depth + back) * 2 + core).reshape(-1)
 
 
-def team_gather(value):
+def nothing(*refs):
+    pass
+
+
+def tied(value, *others):
+    there = pl.BlockSpec(memory_space=pl.ANY)
+    return pl.pallas_call(
+        nothing,
+        in_specs=[there] * (1 + len(others)),
+        out_specs=there,
+        out_shape=shape(value.shape, value.dtype),
+        input_output_aliases={0: 0},
+        name="tied",
+    )(value, *others)
+
+
+def team_gather(value, weight):
+    near, first, second, third = {0: value}, {}, {}, {}
+
+    def hops(k):
+        first[k], second[k] = hop(near[k], False), hop(near[k], True)
+
+    near[1], near[3] = shifted(value, 1), shifted(value, 3)
+    weight = exchanged(tied(weight, near[1]))
+    hops(0)
+    near[2] = shifted(tied(value, first[0], second[0]), 2)
+    third[0] = hop(first[0], True)
+    near[1] = tied(near[1], first[0], second[0])
+    hops(1)
+    third[1] = hop(first[1], True)
+    near[3] = tied(near[3], third[0], first[1], second[1])
+    hops(3)
+    third[3] = hop(first[3], True)
+    near[2] = tied(near[2], third[1], first[3], second[3], weight)
+    hops(2)
+    third[2] = hop(first[2], True)
     parts = []
-    for k in range(lax.axis_size("z")):
-        near = shifted(value, k)
-        first, second = hop(near, False), hop(near, True)
-        pieces = [near, first, second, hop(first, True)]
+    for k in range(4):
+        pieces = [near[k], first[k], second[k], third[k]]
         parts += pieces + [swapped(piece) for piece in pieces]
-    return parts
-
-
-def team_scatter(made):
-    total = None
-    depth = lax.axis_size("z")
-
+    return parts, [first[2], second[2], third[3]], weight
+
+
+def team_scatter(made, beside):
     def added(*terms):
         return sum(term.astype(f32) for term in terms)
 
-    for k in list(range(1, depth)) + [0]:
-        far, near = made(k)
-        far = swapped(far)
-        come = hop(added(near[2:], far[2:]).astype(bf16), True)
-        last = hop(added(near[1], far[1], come[1]).astype(bf16), False)
-        held = added(near[0], far[0], come[0], last)
+    order = list(range(1, lax.axis_size("z"))) + [0]
+    far, near, first, second = {}, {}, {}, {}
+
+    def make(i, *others):
+        away, near[i] = made(order[i], list(others))
+        far[i] = swapped(away)
+
+    def send_first(i):
+        first[i] = added(near[i][2:], far[i][2:]).astype(bf16)
+        return first[i]
+
+    def send_second(i):
+        come = hop(first[i], True)
+        second[i] = (added(near[i][1], far[i][1], come[1]).astype(bf16), come[0])
+        return second[i][0]
+
+    make(0)
+    make(1)
+    make(2, send_first(0))
+    make(3, send_first(1), send_second(0))
+    extra = beside([send_first(2), send_second(1), send_first(3)])
+    total = None
+    for i, k in enumerate(order):
+        if i > 1:
+            send_second(i)
+        last = hop(second[i][0], False)
+        total_k = added(near[i][0], far[i][0], second[i][1], last)
         if k:
-            held = shifted(held.astype(bf16), -k).astype(f32)
-        total = held if total is None else total + held
-    return total
+            total_k = shifted(total_k.astype(bf16), -k).astype(f32)
+        total = total_k if total is None else total + total_k
+    return total, extra
 
 
 def exchanged(parts):
@@ -755,17 +828,23 @@
     return parts
 
 
+def through_outer(got):
+    return got if lax.axis_size("o") == 1 else lax.all_gather(got, "o", axis=0, tiled=True)
+
+
 def spread_done(parts):
-    got = exchanged(parts)
-    return got if lax.axis_size("o") == 1 else lax.all_gather(got, "o", axis=0, tiled=True)
-
-
-def collect_grad(parts, weight):
+    return through_outer(exchanged(parts))
+
+
+def collect(parts):
+    if lax.axis_size("o") > 1:
+        parts = lax.psum_scatter(parts, "o", scatter_dimension=0, tiled=True)
+    return exchanged(parts.astype(bf16))
+
+
+def settled(got, weight):
     outer, group = lax.axis_size("o"), lax.axis_size(group_axes)
     mods, here, wide = weight.shape
-    if outer > 1:
-        parts = lax.psum_scatter(parts, "o", scatter_dimension=0, tiled=True)
-    got = exchanged(parts.astype(bf16))
     if outer == 1:
         grad, sums = settle(got, weight)
         return grad, jnp.sum(sums, axis=1)
@@ -788,18 +867,21 @@
     return lax.dynamic_index_in_dim(value, (lax.axis_index(name) + other) % 2, axis, False)
 
 
-def team_sum(value):
+def team_sum(value, beside, final):
     depth = lax.axis_size("z")
     z = lax.axis_index("z")
 
-    def halved(value, axis, name, pairs):
-        sent = lax.ppermute(half_of(value, axis, name, 1).astype(bf16), name, pairs)
+    def halved(value, axis, name, pairs, *others):
+        sent = half_of(value, axis, name, 1).astype(bf16)
+        sent = lax.ppermute(tied(sent, *others) if others else sent, name, pairs)
         return half_of(value, axis, name, 0).astype(f32) + sent.astype(f32)
 
     swap = [(0, 1), (1, 0)]
     held = halved(value, 3, "c", swap)
     held = halved(held, 0, "y", swap)
-    held = halved(held, 0, "x", swap)
+    held = halved(held, 0, "x", swap, *beside[:1])
+    if beside[1:]:
+        held = tied(held, *beside[1:])
     own = lax.dynamic_index_in_dim(held, z, 0, False)
     for k in range(1, depth):
         own = own + shifted(lax.dynamic_index_in_dim(held, (z + k) % depth, 0, False).astype(bf16), k).astype(f32)
@@ -812,7 +894,8 @@
         flag = lax.axis_index(name) == 0
         return jnp.stack([jnp.where(flag, value, other), jnp.where(flag, other, value)], axis=axis)
 
-    return doubled(doubled(doubled(rolled, 0, "x"), 0, "y"), 3, "c")
+    wide = doubled(doubled(rolled, 0, "x"), 0, "y")
+    return doubled(tied(wide, *final) if final else wide, 3, "c")
 
 
 def entering_state(passing, local_end, backward):
@@ -878,18 +961,14 @@
     inputs = tokens[0].astype(f32)
     inv_rms = lax.rsqrt(jnp.mean(inputs * inputs, axis=-1, keepdims=True) + epsilon)
     scaled = inputs * inv_rms
-    normed_pieces = team_gather((scaled * gain).astype(bf16))
-    wx = spread_done(spread_weight(lead(in_x_weight)))
-    wz_parts, wo_parts = in_z_weight, out_weight
-    wz_parts, wx = lax.optimization_barrier((wz_parts, wx))
-    wz = spread_done(spread_weight(lead(wz_parts)))
-    wo_parts, wz = lax.optimization_barrier((wo_parts, wz))
-    wo = spread_done(spread_weight(lead(wo_parts)))
+    wz = spread_done(spread_weight(lead(in_z_weight)))
+    normed_pieces, last_pieces, wx = team_gather((scaled * gain).astype(bf16), spread_weight(lead(in_x_weight)))
+    wx = through_outer(wx)
     position = lax.axis_index(seq_axes) * here + jnp.arange(here, dtype=jnp.int32)
     own_valid = (position < lax.dynamic_index_in_dim(row_lengths, own_row, 0, False)).astype(f32)[:, None]
     upstream = cotangent[0].astype(f32)
     own_back = (upstream * own_valid).astype(bf16)
-    own_back, normed_pieces[-1] = lax.optimization_barrier((own_back, normed_pieces[-1]))
+    own_back = tied(own_back, *last_pieces)
     d_branch = lax.all_gather(own_back, team_axes)
     xdt = outer_gathered(xdt_weight, 0)
     xbc = outer_gathered(xbc_weight, 2)
@@ -920,8 +999,6 @@
     conv_in = conv_in.reshape(rows, local_len, mine)
     gate_in, wz_f = lead_product(places, normed, facts_there, wz, f32)
     gate_in = gate_in.reshape(rows, local_len, mine)
-    d_gated, wo_f = lead_product(in_order, d_branch, facts_flat, wo, f32)
-    d_gated = d_gated.reshape(rows, local_len, mine)
 
     before = jnp.zeros((rows, 8, mine), f32)
     if outer > 1:
@@ -936,10 +1013,13 @@
     dt_f = dtw.reshape(rank, mods * mine)
     pre, proj_part = conv_block(conv_in, before, facts, row_label, conv_w, conv_b[None], xdt_f, xbc_f)
 
-    def summed(part):
-        return team_sum(part.reshape((2, 2, depth, 2) + part.shape[2:])).reshape(part.shape)
-
-    proj = summed(proj_part)
+    def summed(part, beside, final):
+        return team_sum(part.reshape((2, 2, depth, 2) + part.shape[2:]), beside, final).reshape(part.shape)
+
+    proj = summed(proj_part, [gate_in], [])
+    wo = spread_done(tied(spread_weight(lead(out_weight)), proj))
+    d_gated, wo_f = lead_product(in_order, d_branch, facts_flat, wo, f32)
+    d_gated = d_gated.reshape(rows, local_len, mine)
     decay_coef = -jnp.exp(log_r)
 
     def per_state(values):
@@ -968,10 +1048,10 @@
     block_out = (inputs + own_valid * own_branch).astype(bf16)[None]
     grad_type = f32 if outer > 1 else bf16
 
-    def weight_grad(x, d, there, weight):
-        return collect_grad(feature_grad(x, d, there, mods, outer * group, grad_type), lead(weight))
-
-    out_weight_grad = lead(weight_grad(d_branch, gated, facts_flat, out_weight)[0])
+    def weight_grad(x, d, there, *beside):
+        return feature_grad(x, d, there, mods, outer * group, grad_type, beside)
+
+    out_parts = weight_grad(d_branch, gated, facts_flat)
 
     def back(carry):
         return scan_backward(
@@ -983,8 +1063,11 @@
     if outer > 1:
         results = back(entering_state(passing, results[-1], True))
     d_gate, d_proj_part, d_act, dtw_grad, dtb_grad, skip_grad, rate_total, _ = results
-    in_z_grad, gain_z = weight_grad(normed, d_gate, facts_there, in_z_weight)
-    d_proj = summed(d_proj_part)
+    z_parts = weight_grad(normed, d_gate, facts_there)
+    out_got, z_got = collect(out_parts), collect(z_parts)
+    d_proj = summed(d_proj_part, [out_parts, z_parts], [])
+    out_weight_grad = lead(settled(out_got, lead(out_weight))[0])
+    in_z_grad, gain_z = settled(z_got, lead(in_z_weight))
     rate_total = jnp.sum(rate_total.reshape(pieces, halves, rows, mine), axis=2)
     rate_total = jnp.transpose(rate_total, (1, 0, 2)).reshape(states, mine)
     log_rates_grad = outer_summed(decay_coef * rate_total, 1)
@@ -1010,8 +1093,12 @@
     xbc_grad = outer_summed(xbc_grad, 2)
     conv_weight_grad = outer_summed(taps_grad, 1)
     conv_bias_grad = outer_summed(bias_grad[0], 0)
-    d_scaled = team_scatter(lambda k: trail_product([d_conv, d_gate], facts_there, [wx_f, wz_f], mods, k)) * gain
-    in_x_grad, gain_x = weight_grad(normed, d_conv, facts_there, in_x_weight)
+    d_scaled, x_parts = team_scatter(
+        lambda k, others: trail_product([d_conv, d_gate], facts_there, [wx_f, wz_f], mods, k, others),
+        lambda others: weight_grad(normed, d_conv, facts_there, out_got, *others),
+    )
+    d_scaled = d_scaled * gain
+    in_x_grad, gain_x = settled(collect(tied(x_parts, z_got)), lead(in_x_weight))
     d_inputs = inv_rms * (d_scaled - scaled * jnp.mean(d_scaled * scaled, axis=-1, keepdims=True))
     tokens_grad = (upstream + d_inputs).astype(bf16)[None]
     gain_part = gain_x + gain_z

time: 789 us -> 744 us (0.943)
  starting transfers between devices: 147 us -> 122 us
  local copies, waits for them, and re-layouts: 42.1 us -> 65.9 us
  waiting for transfers between devices: 235 us -> 214 us
  Pallas kernels: 292 us -> 273 us
    all_to_all x6, waiting for transfers between devices: 0.02 us -> 36.4 us  [exchanged(): return lax.all_to_all(parts, group_axes, 0, 0, tiled=True)]
    ppermute x21, waiting for transfers between devices: 112 us -> 81 us  [shifted(): lax.ppermute(value, 'z', [(i, (i + by) % size) for i in range(size)])]
    ppermute x20, waiting for transfers between devices: 79.8 us -> 58.1 us  [hop(): return lax.ppermute(value, team_axes, pairs)]
    unnamed x200 -> x255, local copies, waits for them, and re-layouts: 24.1 us -> 42.8 us
    pallas_call x1, Pallas kernels: 48.8 us -> 31.3 us  [scan_forward(): pl.pallas_call(functools.partial(forward_kernel, dtw.shape[1] // mine), g...]
    ppermute x21, starting transfers between devices: 22.3 us -> 5 us  [swapped(): return lax.ppermute(value, 'c', [(0, 1), (1, 0)])]
    all_to_all x6, starting transfers between devices: 35.7 us -> 47.2 us  [exchanged(): return lax.all_to_all(parts, group_axes, 0, 0, tiled=True)]
    ppermute x6, waiting for transfers between devices: 24.3 us -> 13.8 us  [halved(): sent = lax.ppermute(tied(sent, *others) if others else sent, name, pairs)]
  transfers between devices with their start and end apart: 84 -> 84, of which waited for: 39 -> 39; matrix products, arithmetic and copies ran while one was open for 8% -> 9% of each run, Pallas kernels for 34% -> 33%
where the time goes in v1:
time: 744 us; the launch traced here: 738 us
  Pallas kernels  273 us (37%)
  waiting for transfers between devices  214 us (29%)
  starting transfers between devices  122 us (16%)
  local copies, waits for them, and re-layouts  65.9 us (9%)
  other arithmetic  46.8 us (6%)
  between operations  15.8 us (2%)
    ppermute x21, waiting for transfers between devices, shifted(): lax.ppermute(value, 'z', [(i, (i + by) % size) for i in range(size)])  81 us
    pallas_call x1, Pallas kernels, scan_backward(): pl.pallas_call(functools.partial(backward_kernel, dtw.shape[1] // mine),...  62.4 us
    ppermute x20, waiting for transfers between devices, hop(): return lax.ppermute(value, team_axes, pairs)  58.1 us
    pallas_call x5, Pallas kernels, trail_product(): pl.pallas_call(functools.partial(trail_kernel, mods, len(lefts), len(besi...  48.2 us
    pallas_call x3, Pallas kernels, feature_grad(): pl.pallas_call(functools.partial(grad_kernel, mods), grid=(wide // some,)...  48.2 us
    all_to_all x6, starting transfers between devices, exchanged(): return lax.all_to_all(parts, group_axes, 0, 0, tiled=True)  47.2 us
    unnamed x255, local copies, waits for them, and re-layouts  42.8 us
    ppermute x21, starting transfers between devices, shifted(): lax.ppermute(value, 'z', [(i, (i + by) % size) for i in range(size)])  36.7 us
  transfers between devices with their start and end apart: 84, of which 39 were waited for; matrix products, arithmetic and copies ran while one was open for 9% of the time, Pallas kernels for 33%

profile of v1, /device:TPU:8, one launch (start us, length us, event | category | flops | bytes accessed | tf_op | source)
XLA Modules:
  0.0 737.8 jit_solution(4400193993503806097)
XLA Ops:
  8.7 3.0 collective-permute-start.1
  11.8 2.5 collective-permute-start
  23.6 10.6 %collective-permute-done.4.refs_1_.refs_0_ = bf16[128,2048]{1,0:T(8,128)(2,1)S(1)} collective-permute-done((bf16[128,2048]{1,0:T(8,128)(2,1)S(1)}, bf16[128,2048]{1,0:T(8,128)(2,1)S(1)}, u32[]{:S(2)}, u32[]{:S(2)}) %collective-permute-start.4) | collective-permute-done | bytes 524320 | tf_op jit(solution)/shard_map/ppermute | solution.py:703
  35.1 7.7 %all-to-all-start = ((bf16[8,3,256,128]{3,2,1,0:T(8,128)(2,1)}), bf16[8,3,256,128]{3,2,1,0:T(8,128)(2,1)}, u32[]{:S(2)}, u32[]{:S(2)}) async-start(bf16[8,3,256,128]{3,2,1,0:T(8,128)(2,1)} %tied.11), calls=%async_computation | async-start | bytes 3145728 | tf_op jit(solution)/shard_map/all_to_all | solution.py:819
  46.0 11.2 %collective-permute-done.5.refs_1_ = bf16[128,2048]{1,0:T(8,128)(2,1)S(1)} collective-permute-done((bf16[128,2048]{1,0:T(8,128)(2,1)S(1)}, bf16[128,2048]{1,0:T(8,128)(2,1)S(1)}, u32[]{:S(2)}, u32[]{:S(2)}) %collective-permute-start.5) | collective-permute-done | bytes 524320 | tf_op jit(solution)/shard_map/ppermute | solution.py:723
  62.4 28.1 %collective-permute-done.20.refs_0_ = bf16[128,2048]{1,0:T(8,128)(2,1)S(1)} collective-permute-done((bf16[128,2048]{1,0:T(8,128)(2,1)S(1)}, bf16[128,2048]{1,0:T(8,128)(2,1)S(1)}, u32[]{:S(2)}, u32[]{:S(2)}) %collective-permute-start.20) | collective-permute-done | bytes 524320 | tf_op jit(solution)/shard_map/ppermute | solution.py:703
  96.5 11.0 %collective-permute-done.21.refs_2_.refs_25_ = bf16[128,2048]{1,0:T(8,128)(2,1)} collective-permute-done((bf16[128,2048]{1,0:T(8,128)(2,1)}, bf16[128,2048]{1,0:T(8,128)(2,1)}, u32[]{:S(2)}, u32[]{:S(2)}) %collective-permute-start.21) | collective-permute-done | bytes 524320 | tf_op jit(solution)/shard_map/ppermute | solution.py:723
  109.0 7.5 %collective-permute-done.19.refs_0_ = bf16[128,2048]{1,0:T(8,128)(2,1)} collective-permute-done((bf16[128,2048]{1,0:T(8,128)(2,1)}, bf16[128,2048]{1,0:T(8,128)(2,1)}, u32[]{:S(2)}, u32[]{:S(2)}) %collective-permute-start.19) | collective-permute-done | bytes 524320 | tf_op jit(solution)/shard_map/ppermute | solution.py:703
  120.9 11.4 %collective-permute-done.24.refs_18_.refs_2_ = bf16[128,2048]{1,0:T(8,128)(2,1)} collective-permute-done((bf16[128,2048]{1,0:T(8,128)(2,1)}, bf16[128,2048]{1,0:T(8,128)(2,1)}, u32[]{:S(2)}, u32[]{:S(2)}) %collective-permute-start.24) | collective-permute-done | bytes 524320 | tf_op jit(solution)/shard_map/ppermute | solution.py:723
  134.4 6.6 all-to-all-start.1
  153.3 5.7 collective-permute-done.25.refs_19_
  168.6 17.5 %lead_pieces.1 = (bf16[32,128,128]{2,1,0:T(8,128)(2,1)}, bf16[2048,384]{1,0:T(8,128)(2,1)}, bf16[32,128,2048]{2,1,0:T(8,128)(2,1)}) custom-call(s32[32]{0:T(128)S(1)} %copy-done.52, f32[32,8,128]{2,1,0:T(8,128)S(1)} %gather_fusion.1, bf16[8,3,256,128]{3,2,1,0:T(8,128)(2,1)} %all-to-all-done.refs_4_.weight_ref, bf16[128,2048]{1,0:T(8,128)(2,1)S(1)} %fusion.5.refs_0_, ...), custom_call_target="tpu_custom_call" | custom-call | flops 6442450944 | bytes 33554432 | tf_op jit(solution)/shard_map/lead_pieces/pallas_call | solution.py:174
  187.4 6.4 conv_block.1
  199.5 4.8 all-to-all-done.1.weight_ref
  204.3 14.4 %lead_product.2 = (f32[32,128,128]{2,1,0:T(8,128)S(1)}, bf16[2048,384]{1,0:T(8,128)(2,1)S(1)}) custom-call(s32[32]{0:T(128)S(1)} %copy-done.53, bf16[32,128,2048]{2,1,0:T(8,128)(2,1)} %get-tuple-element.55.x_ref, f32[32,8,128]{2,1,0:T(8,128)S(1)} %gather_fusion.1, bf16[8,3,256,128]{3,2,1,0:T(8,128)(2,1)} %all-to-all-done.1.weight_ref), custom_call_target="tpu_custom_call" | custom-call | flops 6442450944 | bytes 16777216 | tf_op jit(solution)/shard_map/lead_product/pallas_call | solution.py:113
  221.7 10.0 %collective-permute-done.37 = bf16[4,160,128]{2,1,0:T(8,128)(2,1)S(1)} collective-permute-done((bf16[4,160,128]{2,1,0:T(8,128)(2,1)}, bf16[4,160,128]{2,1,0:T(8,128)(2,1)S(1)}, u32[]{:S(2)}, u32[]{:S(2)}) %collective-permute-start.37) | collective-permute-done | bytes 163872 | tf_op jit(solution)/shard_map/ppermute | solution.py:876
  233.8 3.1 collective-permute-start.40
  236.9 2.4 collective-permute-start.39
  239.4 2.7 collective-permute-done.40
  242.0 2.5 collective-permute-done.39
  244.6 4.2 collective-permute-start.43
  264.4 4.4 collective-permute-done.45
  273.1 5.9 all-to-all-start.2
  282.9 31.3 %scan_forward.1 = (bf16[4,1024,128]{2,1,0:T(8,128)(2,1)S(1)}, f32[4,1024,128]{2,1,0:T(8,128)S(1)}, f32[4,1024,128]{2,1,0:T(8,128)}, f32[1024,8,8,128]{3,2,1,0:T(8,128)}, f32[8,8,128]{2,1,0:T(8,128)S(1)}) custom-call(bf16[4,8,160,128]{3,2,1,0:T(8,128)(2,1)S(1)} %bitcast.259, f32[4,1024,128]{2,1,0:T(8,128)} %copy-done.79, f32[4,8,8,128]{3,2,1,0:T(8,128)S(1)} %copy-done.33, ...), custom_call_target="tpu_custom_call" | custom-call | flops 46137344000 | bytes 41943040 | tf_op jit(solution)/shard_map/scan_forward/pallas_call | solution.py:448
  317.8 13.4 %lead_product.3 = (f32[32,128,128]{2,1,0:T(8,128)S(1)}, bf16[2048,384]{1,0:T(8,128)(2,1)S(1)}) custom-call(s32[32]{0:T(128)S(1)} %iota.68.places, bf16[32,128,2048]{2,1,0:T(8,128)(2,1)} %bitcast.317, f32[32,8,128]{2,1,0:T(8,128)S(1)} %stack.136.facts_ref.refs_1_, bf16[8,3,256,128]{3,2,1,0:T(8,128)(2,1)S(1)} %all-to-all-done.2.weight_ref), custom_call_target="tpu_custom_call" | custom-call | flops 6442450944 | bytes 16777216 | tf_op jit(solution)/shard_map/lead_product/pallas_call | solution.py:113
  332.6 14.0 %trail_product.5 = bf16[32,128,2048]{2,1,0:T(8,128)(2,1)} custom-call(bf16[32,128,128]{2,1,0:T(8,128)(2,1)S(1)} %bitcast.281, f32[32,8,128]{2,1,0:T(8,128)S(1)} %stack.136.facts_ref.refs_1_, bf16[2048,384]{1,0:T(8,128)(2,1)S(1)} %get-tuple-element.59.refs_2_), custom_call_target="tpu_custom_call" | custom-call | flops 6442450944 | bytes 16777216 | tf_op jit(solution)/shard_map/trail_product/pallas_call | solution.py:226
  348.1 62.4 %scan_backward.1 = (bf16[32,128,128]{2,1,0:T(8,128)(2,1)S(1)}, bf16[4,8,160,128]{3,2,1,0:T(8,128)(2,1)S(1)}, f32[4,1024,128]{2,1,0:T(8,128)}, f32[128,384]{1,0:T...) custom-call(s32[32]{0:T(128)S(1)} %scatter_custom_fusion.tables, ...), custom_call_target="tpu_custom_call" | custom-call | flops 62914560000 | bytes 41943040 | tf_op jit(solution)/shard_map/scan_backward/pallas_call | solution.py:590
  413.5 16.4 %feature_grad.3.refs_1_ = bf16[8,256,384]{2,1,0:T(8,128)(2,1)} custom-call(bf16[4096,2048]{1,0:T(8,128)(2,1)} %all-gather.3.cloned.1.call-done.x_ref, bf16[32,128,128]{2,1,0:T(8,128)(2,1)S(1)} %bitcast.282, f32[32,8,128]{2,1,0:T(8,128)S(1)} %stack.136.facts_ref.refs_1_), custom_call_target="tpu_custom_call" | custom-call | flops 19327352832 | bytes 16777216 | tf_op jit(solution)/shard_map/feature_grad/pallas_call | solution.py:261
  432.1 16.4 %feature_grad.4.refs_1_ = bf16[8,256,384]{2,1,0:T(8,128)(2,1)} custom-call(bf16[4096,2048]{1,0:T(8,128)(2,1)} %bitcast.321, bf16[32,128,128]{2,1,0:T(8,128)(2,1)S(1)} %get-tuple-element.66.d_ref.refs_1_, f32[32,8,128]{2,1,0:T(8,128)S(1)} %copy-done.31), custom_call_target="tpu_custom_call" | custom-call | flops 19327352832 | bytes 16777216 | tf_op jit(solution)/shard_map/feature_grad/pallas_call | solution.py:261
  452.3 2.8 collective-permute-start.51
  455.5 2.4 collective-permute-done.52
  463.6 3.0 collective-permute-start.53
  466.6 2.7 collective-permute-done.54
  472.4 5.1 collective-permute-done.56
  479.2 5.6 collective-permute-done.57
  489.2 18.0 %deconv_block.1 = (bf16[32,128,128]{2,1,0:T(8,128)(2,1)S(1)}, f32[128,384]{1,0:T(8,128)S(1)}, f32[96,128]{1,0:T(8,128)S(1)}, f32[4,128]{1,0:T(4,128)}, f32[1,128...) custom-call(s32[32]{0:T(128)S(1)} %scatter_custom_fusion.tables, bf16[4,8,160,128]{3,2,1,0:T(8,128)(2,1)S(1)} %bitcast.264, ...), custom_call_target="tpu_custom_call" | custom-call | flops 15728640000 | bytes 7340032 | tf_op jit(solution)/shard_map/deconv_block/pallas_call | solution.py:674
  507.3 7.9 %trail_product.6 = (bf16[4,128,2048]{2,1,0:T(8,128)(2,1)}, bf16[4,128,2048]{2,1,0:T(8,128)(2,1)}) custom-call(bf16[32,128,128]{2,1,0:T(8,128)(2,1)S(1)} %get-tuple-element.68.refs_0_.d_ref, bf16[32,128,128]{2,1,0:T(8,128)(2,1)S(1)} %get-tuple-element.66.d_ref.refs_1_, f32[32,8,128]{2,1,0:T(8,128)S(1)} %copy-done.31, bf16[2048,384]{1,0:T(8,128)(2,1)S(1)} %copy-done.67, ...), custom_call_target="tpu_custom_call" | custom-call | flops 3221225472 | bytes 4194304 | tf_op jit(solution)/shard_map/trail_product/pallas_call | solution.py:226
  515.3 7.8 %trail_product.7 = (bf16[4,128,2048]{2,1,0:T(8,128)(2,1)}, bf16[4,128,2048]{2,1,0:T(8,128)(2,1)}) custom-call(bf16[32,128,128]{2,1,0:T(8,128)(2,1)S(1)} %get-tuple-element.68.refs_0_.d_ref, bf16[32,128,128]{2,1,0:T(8,128)(2,1)S(1)} %get-tuple-element.66.d_ref.refs_1_, f32[32,8,128]{2,1,0:T(8,128)S(1)} %copy-done.31, bf16[2048,384]{1,0:T(8,128)(2,1)S(1)} %copy-done.67, ...), custom_call_target="tpu_custom_call" | custom-call | flops 3221225472 | bytes 4194304 | tf_op jit(solution)/shard_map/trail_product/pallas_call | solution.py:226
  526.3 14.0 %all-to-all-start.3 = ((bf16[8,256,384]{2,1,0:T(8,128)(2,1)}), bf16[8,256,384]{2,1,0:T(8,128)(2,1)S(1)}, u32[]{:S(2)}, u32[]{:S(2)}) async-start(bf16[8,256,384]{2,1,0:T(8,128)(2,1)} %feature_grad.3.refs_1_), calls=%async_computation.4 | async-start | bytes 3145728 | tf_op jit(solution)/shard_map/all_to_all | solution.py:819
  544.1 9.3 %trail_product.8 = (bf16[4,128,2048]{2,1,0:T(8,128)(2,1)}, bf16[4,128,2048]{2,1,0:T(8,128)(2,1)}) custom-call(bf16[32,128,128]{2,1,0:T(8,128)(2,1)S(1)} %copy-done.76, bf16[32,128,128]{2,1,0:T(8,128)(2,1)S(1)} %copy-done.73, f32[32,8,128]{2,1,0:T(8,128)S(1)} %copy-done.31, bf16[2048,384]{1,0:T(8,128)(2,1)S(1)} %copy-done.68, bf16[2048,384]{1,0:T(8,128)(2,1)} %copy-done.70, ...), custom_call_target="tpu_custom_call" | custom-call | flops 3221225472 | bytes 4194304 | tf_op jit(solution)/shard_map/trail_product/pallas_call | solution.py:226
  555.3 2.4 fusion.18.refs_6_
  557.8 9.2 %trail_product.9 = (bf16[4,128,2048]{2,1,0:T(8,128)(2,1)}, bf16[4,128,2048]{2,1,0:T(8,128)(2,1)}) custom-call(bf16[32,128,128]{2,1,0:T(8,128)(2,1)S(1)} %copy-done.77, bf16[32,128,128]{2,1,0:T(8,128)(2,1)S(1)} %copy-done.74, f32[32,8,128]{2,1,0:T(8,128)S(1)} %copy-done.31, bf16[2048,384]{1,0:T(8,128)(2,1)S(1)} %copy-done.69, bf16[2048,384]{1,0:T(8,128)(2,1)} %copy-done.70, ...), custom_call_target="tpu_custom_call" | custom-call | flops 3221225472 | bytes 4194304 | tf_op jit(solution)/shard_map/trail_product/pallas_call | solution.py:226
  569.1 18.7 %collective-permute-done.64 = bf16[2,128,2048]{2,1,0:T(8,128)(2,1)S(1)} collective-permute-done((bf16[2,128,2048]{2,1,0:T(8,128)(2,1)S(1)}, bf16[2,128,2048]{2,1,0:T(8,128)(2,1)S(1)}, u32[]{:S(2)}, u32[]{:S(2)}) %collective-permute-start.64) | collective-permute-done | bytes 1048608 | tf_op jit(solution)/shard_map/ppermute | solution.py:723
  587.8 2.4 fusion.19.refs_2_
  591.4 5.1 all-to-all-start.4
  596.5 3.1 add_convert_fusion.1.refs_1_
  600.1 2.6 add_convert_fusion.refs_3_
  604.2 15.4 %feature_grad.5.refs_0_ = bf16[8,256,384]{2,1,0:T(8,128)(2,1)S(1)} custom-call(bf16[4096,2048]{1,0:T(8,128)(2,1)} %bitcast.322, bf16[32,128,128]{2,1,0:T(8,128)(2,1)S(1)} %copy-done.78, f32[32,8,128]{2,1,0:T(8,128)S(1)} %copy-done.31, bf16[8,256,384]{2,1,0:T(8,128)(2,1)} %copy-done.8, bf16[2,128,2048]{2,1,0:T(8,128)(2,1)} %add_convert_fusion.1.refs_1_, ...), custom_call_target="tpu_custom_call" | custom-call | flops 19327352832 | bytes 16777216 | tf_op jit(solution)/shard_map/feature_grad/pallas_call | solution.py:261
  620.7 10.1 %all-to-all-done.4.refs_1_.got_ref = bf16[8,256,384]{2,1,0:T(8,128)(2,1)S(1)} async-done(((bf16[8,256,384]{2,1,0:T(8,128)(2,1)}), bf16[8,256,384]{2,1,0:T(8,128)(2,1)S(1)}, u32[]{:S(2)}, u32[]{:S(2)}) %all-to-all-start.4) | async-done | bytes 1572896 | tf_op jit(solution)/shard_map/all_to_all | solution.py:819
  632.0 7.9 %all-to-all-start.5 = ((bf16[8,256,384]{2,1,0:T(8,128)(2,1)}), bf16[8,256,384]{2,1,0:T(8,128)(2,1)}, u32[]{:S(2)}, u32[]{:S(2)}) async-start(bf16[8,256,384]{2,1,0:T(8,128)(2,1)} %tied.21), calls=%async_computation.6 | async-start | bytes 3145728 | tf_op jit(solution)/shard_map/all_to_all | solution.py:819
  642.3 2.5 fusion.14
  644.8 2.4 collective-permute-start.66
  647.2 2.6 fusion.15
  650.6 2.4 fusion.13
  654.7 2.4 fusion.21
  665.0 3.7 settle.4
  671.6 3.7 settle.5
  675.3 21.4 %all-to-all-done.5.got_ref = bf16[8,256,384]{2,1,0:T(8,128)(2,1)} async-done(((bf16[8,256,384]{2,1,0:T(8,128)(2,1)}), bf16[8,256,384]{2,1,0:T(8,128)(2,1)}, u32[]{:S(2)}, u32[]{:S(2)}) %all-to-all-start.5) | async-done | bytes 1572896 | tf_op jit(solution)/shard_map/all_to_all | solution.py:819
  698.2 5.9 settle.3
  704.9 3.1 collective-permute-done.66
  708.0 13.3 %collective-permute-done.62 = bf16[128,2048]{1,0:T(8,128)(2,1)} collective-permute-done((bf16[128,2048]{1,0:T(8,128)(2,1)}, bf16[128,2048]{1,0:T(8,128)(2,1)}, u32[]{:S(2)}, u32[]{:S(2)}) %collective-permute-start.62) | collective-permute-done | bytes 524320 | tf_op jit(solution)/shard_map/ppermute | solution.py:703
  721.4 2.7 fusion.6
  725.0 2.7 collective-permute-done.75
  728.3 2.4 fusion.23
  (526 shorter events, 157.7 us)
Async XLA Ops:
  8.7 6.8 collective-permute-start.2
  8.7 6.8 collective-permute-start.1
  19.4 14.9 %collective-permute-start.4 = (bf16[128,2048]{1,0:T(8,128)(2,1)S(1)}, bf16[128,2048]{1,0:T(8,128)(2,1)S(1)}, u32[]{:S(2)}, u32[]{:S(2)}) collective-permute-start(bf16[128,2048]{1,0:T(8,128)(2,1)S(1)} %fusion.5.refs_0_), channel_id=1, source_target_pairs={{0,2},{2,4},{4,6},{6,0},{1,3},{3,5},{5,7},{7,1},{8,10},{10,12},{12... | collective-permute-start | bytes 1572872 | tf_op jit(solution)/shard_map/ppermute | solution.py:703
  35.1 81.4 %all-to-all-start = ((bf16[8,3,256,128]{3,2,1,0:T(8,128)(2,1)}), bf16[8,3,256,128]{3,2,1,0:T(8,128)(2,1)}, u32[]{:S(2)}, u32[]{:S(2)}) async-start(bf16[8,3,256,128]{3,2,1,0:T(8,128)(2,1)} %tied.11), calls=%async_computation | async-start | bytes 3145728 | tf_op jit(solution)/shard_map/all_to_all | solution.py:819
  42.8 275.0 %all-gather.3.cloned.1.call-start = ((), (), s32[]{:S(2)}) async-start(), calls=%async_computation.8 | async-start | bytes 17301504 | tf_op jit(solution)/shard_map/all_gather | solution.py:972
  42.8 14.5 %collective-permute-start.5 = (bf16[128,2048]{1,0:T(8,128)(2,1)S(1)}, bf16[128,2048]{1,0:T(8,128)(2,1)S(1)}, u32[]{:S(2)}, u32[]{:S(2)}) collective-permute-start(bf16[128,2048]{1,0:T(8,128)(2,1)S(1)} %fusion.5.refs_0_), channel_id=1, source_target_pairs={{0,8},{1,17},{2,10},{3,19},{4,12},{5,21},{6,14},{7,23},{8,0},{9,25... | collective-permute-start | bytes 1572872 | tf_op jit(solution)/shard_map/ppermute | solution.py:723
  44.3 14.2 %collective-permute-start.6 = (bf16[128,2048]{1,0:T(8,128)(2,1)S(1)}, bf16[128,2048]{1,0:T(8,128)(2,1)S(1)}, u32[]{:S(2)}, u32[]{:S(2)}) collective-permute-start(bf16[128,2048]{1,0:T(8,128)(2,1)S(1)} %fusion.5.refs_0_), channel_id=1, source_target_pairs={{0,16},{1,9},{2,18},{3,11},{4,20},{5,13},{6,22},{7,15},{8,24},{9,1... | collective-permute-start | bytes 1572872 | tf_op jit(solution)/shard_map/ppermute | solution.py:723
  45.8 44.6 %collective-permute-start.20 = (bf16[128,2048]{1,0:T(8,128)(2,1)S(1)}, bf16[128,2048]{1,0:T(8,128)(2,1)S(1)}, u32[]{:S(2)}, u32[]{:S(2)}) collective-permute-start(bf16[128,2048]{1,0:T(8,128)(2,1)S(1)} %fusion.5.refs_0_), channel_id=1, source_target_pairs={{0,6},{2,0},{4,2},{6,4},{1,7},{3,1},{5,3},{7,5},{8,14},{10,8},{12,... | collective-permute-start | bytes 1572872 | tf_op jit(solution)/shard_map/ppermute | solution.py:703
  57.2 33.2 %collective-permute-start.7 = (bf16[128,2048]{1,0:T(8,128)(2,1)S(1)}, bf16[128,2048]{1,0:T(8,128)(2,1)S(1)}, u32[]{:S(2)}, u32[]{:S(2)}) collective-permute-start(bf16[128,2048]{1,0:T(8,128)(2,1)S(1)} %collective-permute-done.5.refs_1_), channel_id=1, source_target_pairs={{0,16},{1,9},{2,18},{3,11},{4,20},{5,13},{6,22},{7,15},{8,24},{9,1... | collective-permute-start | bytes 1572872 | tf_op jit(solution)/shard_map/ppermute | solution.py:723
  59.3 31.1 %collective-permute-start.13 = (bf16[128,2048]{1,0:T(8,128)(2,1)}, bf16[128,2048]{1,0:T(8,128)(2,1)S(1)}, u32[]{:S(2)}, u32[]{:S(2)}) collective-permute-start(bf16[128,2048]{1,0:T(8,128)(2,1)} %tied.12.refs_8_), channel_id=1, source_target_pairs={{0,16},{1,9},{2,18},{3,11},{4,20},{5,13},{6,22},{7,15},{8,24},{9,1... | collective-permute-start | bytes 1572872 | tf_op jit(solution)/shard_map/ppermute | solution.py:723
  60.1 30.4 %collective-permute-start.12 = (bf16[128,2048]{1,0:T(8,128)(2,1)}, bf16[128,2048]{1,0:T(8,128)(2,1)S(1)}, u32[]{:S(2)}, u32[]{:S(2)}) collective-permute-start(bf16[128,2048]{1,0:T(8,128)(2,1)} %tied.12.refs_8_), channel_id=1, source_target_pairs={{0,8},{1,17},{2,10},{3,19},{4,12},{5,21},{6,14},{7,23},{8,0},{9,25... | collective-permute-start | bytes 1572872 | tf_op jit(solution)/shard_map/ppermute | solution.py:723
  92.4 15.1 %collective-permute-start.21 = (bf16[128,2048]{1,0:T(8,128)(2,1)}, bf16[128,2048]{1,0:T(8,128)(2,1)}, u32[]{:S(2)}, u32[]{:S(2)}) collective-permute-start(bf16[128,2048]{1,0:T(8,128)(2,1)} %tied.14.refs_24_), channel_id=1, source_target_pairs={{0,8},{1,17},{2,10},{3,19},{4,12},{5,21},{6,14},{7,23},{8,0},{9,25... | collective-permute-start | bytes 1572872 | tf_op jit(solution)/shard_map/ppermute | solution.py:723
  93.9 22.6 %collective-permute-start.19 = (bf16[128,2048]{1,0:T(8,128)(2,1)}, bf16[128,2048]{1,0:T(8,128)(2,1)}, u32[]{:S(2)}, u32[]{:S(2)}) collective-permute-start(bf16[128,2048]{1,0:T(8,128)(2,1)} %tied.13), channel_id=1, source_target_pairs={{0,4},{2,6},{4,0},{6,2},{1,5},{3,7},{5,1},{7,3},{8,12},{10,14},{12... | collective-permute-start | bytes 1572872 | tf_op jit(solution)/shard_map/ppermute | solution.py:703
  93.9 22.6 %collective-permute-start.22 = (bf16[128,2048]{1,0:T(8,128)(2,1)S(1)}, bf16[128,2048]{1,0:T(8,128)(2,1)S(1)}, u32[]{:S(2)}, u32[]{:S(2)}) collective-permute-start(bf16[128,2048]{1,0:T(8,128)(2,1)S(1)} %copy-done.96), channel_id=1, source_target_pairs={{0,16},{1,9},{2,18},{3,11},{4,20},{5,13},{6,22},{7,15},{8,24},{9,1... | collective-permute-start | bytes 1572872 | tf_op jit(solution)/shard_map/ppermute | solution.py:723
  95.4 21.0 %collective-permute-start.14 = (bf16[128,2048]{1,0:T(8,128)(2,1)S(1)}, bf16[128,2048]{1,0:T(8,128)(2,1)}, u32[]{:S(2)}, u32[]{:S(2)}) collective-permute-start(bf16[128,2048]{1,0:T(8,128)(2,1)S(1)} %copy-done.24), channel_id=1, source_target_pairs={{0,16},{1,9},{2,18},{3,11},{4,20},{5,13},{6,22},{7,15},{8,24},{9,1... | collective-permute-start | bytes 1572872 | tf_op jit(solution)/shard_map/ppermute | solution.py:723
  107.5 13.4 %collective-permute-start.30 = (bf16[128,2048]{1,0:T(8,128)(2,1)}, bf16[128,2048]{1,0:T(8,128)(2,1)S(1)}, u32[]{:S(2)}, u32[]{:S(2)}) collective-permute-start(bf16[128,2048]{1,0:T(8,128)(2,1)} %collective-permute-done.21.refs_2_.refs_25_), channel_id=1, source_target_pairs={{0,16},{1,9},{2,18},{3,11},{4,20},{5,13},{6,22},{7,15},{8,24},{9,1... | collective-permute-start | bytes 1572872 | tf_op jit(solution)/shard_map/ppermute | solution.py:723
  117.3 15.0 %collective-permute-start.24 = (bf16[128,2048]{1,0:T(8,128)(2,1)}, bf16[128,2048]{1,0:T(8,128)(2,1)}, u32[]{:S(2)}, u32[]{:S(2)}) collective-permute-start(bf16[128,2048]{1,0:T(8,128)(2,1)} %tied.15.refs_16_), channel_id=1, source_target_pairs={{0,16},{1,9},{2,18},{3,11},{4,20},{5,13},{6,22},{7,15},{8,24},{9,1... | collective-permute-start | bytes 1572872 | tf_op jit(solution)/shard_map/ppermute | solution.py:723
  117.8 14.5 %collective-permute-start.23 = (bf16[128,2048]{1,0:T(8,128)(2,1)}, bf16[128,2048]{1,0:T(8,128)(2,1)}, u32[]{:S(2)}, u32[]{:S(2)}) collective-permute-start(bf16[128,2048]{1,0:T(8,128)(2,1)} %tied.15.refs_16_), channel_id=1, source_target_pairs={{0,8},{1,17},{2,10},{3,19},{4,12},{5,21},{6,14},{7,23},{8,0},{9,25... | collective-permute-start | bytes 1572872 | tf_op jit(solution)/shard_map/ppermute | solution.py:723
  134.4 69.9 %all-to-all-start.1 = ((bf16[8,3,256,128]{3,2,1,0:T(8,128)(2,1)}), bf16[8,3,256,128]{3,2,1,0:T(8,128)(2,1)}, u32[]{:S(2)}, u32[]{:S(2)}) async-start(bf16[8,3,256,128]{3,2,1,0:T(8,128)(2,1)} %bitcast.286), calls=%async_computation.1 | async-start | bytes 3145728 | tf_op jit(solution)/shard_map/all_to_all | solution.py:819
  141.7 7.0 collective-permute-start.15
  142.0 6.4 collective-permute-start.9
  142.3 7.1 collective-permute-start.31
  149.4 9.5 %collective-permute-start.25 = (bf16[128,2048]{1,0:T(8,128)(2,1)}, bf16[128,2048]{1,0:T(8,128)(2,1)}, u32[]{:S(2)}, u32[]{:S(2)}) collective-permute-start(bf16[128,2048]{1,0:T(8,128)(2,1)} %collective-permute-done.23.refs_17_.refs_1_), channel_id=1, source_target_pairs={{0,16},{1,9},{2,18},{3,11},{4,20},{5,13},{6,22},{7,15},{8,24},{9,1... | collective-permute-start | bytes 1572872 | tf_op jit(solution)/shard_map/ppermute | solution.py:723
  151.7 13.0 %collective-permute-start.34 = (bf16[128,2048]{1,0:T(8,128)(2,1)}, bf16[128,2048]{1,0:T(8,128)(2,1)}, u32[]{:S(2)}, u32[]{:S(2)}) collective-permute-start(bf16[128,2048]{1,0:T(8,128)(2,1)} %copy-done.94), channel_id=1, source_target_pairs={{0,1},{1,0},{2,3},{3,2},{4,5},{5,4},{6,7},{7,6},{8,9},{9,8},{10,11... | collective-permute-start | bytes 1572872 | tf_op jit(solution)/shard_map/ppermute | solution.py:707
  152.1 12.7 %collective-permute-start.26 = (bf16[128,2048]{1,0:T(8,128)(2,1)}, bf16[128,2048]{1,0:T(8,128)(2,1)}, u32[]{:S(2)}, u32[]{:S(2)}) collective-permute-start(bf16[128,2048]{1,0:T(8,128)(2,1)} %tied.15.refs_16_), channel_id=1, source_target_pairs={{0,1},{1,0},{2,3},{3,2},{4,5},{5,4},{6,7},{7,6},{8,9},{9,8},{10,11... | collective-permute-start | bytes 1572872 | tf_op jit(solution)/shard_map/ppermute | solution.py:707
  152.3 12.5 %collective-permute-start.28 = (bf16[128,2048]{1,0:T(8,128)(2,1)}, bf16[128,2048]{1,0:T(8,128)(2,1)}, u32[]{:S(2)}, u32[]{:S(2)}) collective-permute-start(bf16[128,2048]{1,0:T(8,128)(2,1)} %collective-permute-done.24.refs_18_.refs_2_), channel_id=1, source_target_pairs={{0,1},{1,0},{2,3},{3,2},{4,5},{5,4},{6,7},{7,6},{8,9},{9,8},{10,11... | collective-permute-start | bytes 1572872 | tf_op jit(solution)/shard_map/ppermute | solution.py:707
  152.9 11.9 %collective-permute-start.27 = (bf16[128,2048]{1,0:T(8,128)(2,1)}, bf16[128,2048]{1,0:T(8,128)(2,1)}, u32[]{:S(2)}, u32[]{:S(2)}) collective-permute-start(bf16[128,2048]{1,0:T(8,128)(2,1)} %collective-permute-done.23.refs_17_.refs_1_), channel_id=1, source_target_pairs={{0,1},{1,0},{2,3},{3,2},{4,5},{5,4},{6,7},{7,6},{8,9},{9,8},{10,11... | collective-permute-start | bytes 1572872 | tf_op jit(solution)/shard_map/ppermute | solution.py:707
  158.9 5.9 collective-permute-start.29
  198.9 21.2 %collective-permute-start.36 = (bf16[2,4,160,128]{3,2,1,0:T(8,128)(2,1)S(1)}, bf16[2,4,160,128]{3,2,1,0:T(8,128)(2,1)S(1)}, u32[]{:S(2)}, u32[]{:S(2)}) collective-permute-start(bf16[2,4,160,128]{3,2,1,0:T(8,128)(2,1)S(1)} %fusion.24), channel_id=1, source_target_pairs={{0,16},{16,0},{1,17},{17,1},{2,18},{18,2},{3,19},{19,3},{4,20},{20... | collective-permute-start | bytes 983048 | tf_op jit(solution)/shard_map/ppermute | solution.py:876
  221.3 10.4 %collective-permute-start.37 = (bf16[4,160,128]{2,1,0:T(8,128)(2,1)}, bf16[4,160,128]{2,1,0:T(8,128)(2,1)S(1)}, u32[]{:S(2)}, u32[]{:S(2)}) collective-permute-start(bf16[4,160,128]{2,1,0:T(8,128)(2,1)} %tied.16), channel_id=1, source_target_pairs={{0,8},{8,0},{1,9},{9,1},{2,10},{10,2},{3,11},{11,3},{4,12},{12,4},... | collective-permute-start | bytes 491528 | tf_op jit(solution)/shard_map/ppermute | solution.py:876
  231.8 7.6 %collective-permute-start.38 = (bf16[160,128]{1,0:T(8,128)(2,1)S(1)}, bf16[160,128]{1,0:T(8,128)(2,1)S(1)}, u32[]{:S(2)}, u32[]{:S(2)}) collective-permute-start(bf16[160,128]{1,0:T(8,128)(2,1)S(1)} %get-tuple-element.167), channel_id=1, source_target_pairs={{0,2},{2,4},{4,6},{6,0},{1,3},{3,5},{5,7},{7,1},{8,10},{10,12},{12... | collective-permute-start | bytes 122888 | tf_op jit(solution)/shard_map/ppermute | solution.py:703
  233.8 8.2 %collective-permute-start.40 = (bf16[160,128]{1,0:T(8,128)(2,1)S(1)}, bf16[160,128]{1,0:T(8,128)(2,1)S(1)}, u32[]{:S(2)}, u32[]{:S(2)}) collective-permute-start(bf16[160,128]{1,0:T(8,128)(2,1)S(1)} %get-tuple-element.168), channel_id=1, source_target_pairs={{0,6},{2,0},{4,2},{6,4},{1,7},{3,1},{5,3},{7,5},{8,14},{10,8},{12,... | collective-permute-start | bytes 122888 | tf_op jit(solution)/shard_map/ppermute | solution.py:703
  236.9 7.6 %collective-permute-start.39 = (bf16[160,128]{1,0:T(8,128)(2,1)S(1)}, bf16[160,128]{1,0:T(8,128)(2,1)S(1)}, u32[]{:S(2)}, u32[]{:S(2)}) collective-permute-start(bf16[160,128]{1,0:T(8,128)(2,1)S(1)} %get-tuple-element.169), channel_id=1, source_target_pairs={{0,4},{2,6},{4,0},{6,2},{1,5},{3,7},{5,1},{7,3},{8,12},{10,14},{12... | collective-permute-start | bytes 122888 | tf_op jit(solution)/shard_map/ppermute | solution.py:703
  244.6 7.5 %collective-permute-start.43 = (bf16[160,128]{1,0:T(8,128)(2,1)S(1)}, bf16[160,128]{1,0:T(8,128)(2,1)S(1)}, u32[]{:S(2)}, u32[]{:S(2)}) collective-permute-start(bf16[160,128]{1,0:T(8,128)(2,1)S(1)} %fusion.33), channel_id=1, source_target_pairs={{0,6},{2,0},{4,2},{6,4},{1,7},{3,1},{5,3},{7,5},{8,14},{10,8},{12,... | collective-permute-start | bytes 122888 | tf_op jit(solution)/shard_map/ppermute | solution.py:703
  261.7 7.1 collective-permute-start.45
  273.1 44.7 %all-to-all-start.2 = ((bf16[8,3,256,128]{3,2,1,0:T(8,128)(2,1)}), bf16[8,3,256,128]{3,2,1,0:T(8,128)(2,1)S(1)}, u32[]{:S(2)}, u32[]{:S(2)}) async-start(bf16[8,3,256,128]{3,2,1,0:T(8,128)(2,1)} %tied.18), calls=%async_computation.2 | async-start | bytes 3145728 | tf_op jit(solution)/shard_map/all_to_all | solution.py:819
  279.0 449.3 %reduce-scatter.2.cloned.1.call-start = ((), (), s32[]{:S(2)}) async-start(), calls=%async_computation.7 | async-start | bytes 17301504 | tf_op jit(solution)/shard_map/reduce_scatter | solution.py:1047
  413.0 16.8 %collective-permute-start.48 = (bf16[2,4,160,128]{3,2,1,0:T(8,128)(2,1)S(1)}, bf16[2,4,160,128]{3,2,1,0:T(8,128)(2,1)S(1)}, u32[]{:S(2)}, u32[]{:S(2)}) collective-permute-start(bf16[2,4,160,128]{3,2,1,0:T(8,128)(2,1)S(1)} %fusion.25), channel_id=1, source_target_pairs={{0,16},{16,0},{1,17},{17,1},{2,18},{18,2},{3,19},{19,3},{4,20},{20... | collective-permute-start | bytes 983048 | tf_op jit(solution)/shard_map/ppermute | solution.py:876
  430.6 17.9 %collective-permute-start.49 = (bf16[4,160,128]{2,1,0:T(8,128)(2,1)}, bf16[4,160,128]{2,1,0:T(8,128)(2,1)S(1)}, u32[]{:S(2)}, u32[]{:S(2)}) collective-permute-start(bf16[4,160,128]{2,1,0:T(8,128)(2,1)} %tied.19), channel_id=1, source_target_pairs={{0,8},{8,0},{1,9},{9,1},{2,10},{10,2},{3,11},{11,3},{4,12},{12,4},... | collective-permute-start | bytes 491528 | tf_op jit(solution)/shard_map/ppermute | solution.py:876
  451.8 6.1 collective-permute-start.52
  452.3 7.6 %collective-permute-start.51 = (bf16[160,128]{1,0:T(8,128)(2,1)S(1)}, bf16[160,128]{1,0:T(8,128)(2,1)S(1)}, u32[]{:S(2)}, u32[]{:S(2)}) collective-permute-start(bf16[160,128]{1,0:T(8,128)(2,1)S(1)} %get-tuple-element.164), channel_id=1, source_target_pairs={{0,4},{2,6},{4,0},{6,2},{1,5},{3,7},{5,1},{7,3},{8,12},{10,14},{12... | collective-permute-start | bytes 122888 | tf_op jit(solution)/shard_map/ppermute | solution.py:703
  460.8 5.8 collective-permute-start.55
  463.1 6.3 collective-permute-start.54
  463.6 7.7 %collective-permute-start.53 = (bf16[160,128]{1,0:T(8,128)(2,1)S(1)}, bf16[160,128]{1,0:T(8,128)(2,1)S(1)}, u32[]{:S(2)}, u32[]{:S(2)}) collective-permute-start(bf16[160,128]{1,0:T(8,128)(2,1)S(1)} %fusion.30), channel_id=1, source_target_pairs={{0,2},{2,4},{4,6},{6,0},{1,3},{3,5},{5,7},{7,1},{8,10},{10,12},{12... | collective-permute-start | bytes 122888 | tf_op jit(solution)/shard_map/ppermute | solution.py:703
  477.6 7.2 collective-permute-start.57
  515.1 8.3 %collective-permute-start.59 = (bf16[4,128,2048]{2,1,0:T(8,128)(2,1)}, bf16[4,128,2048]{2,1,0:T(8,128)(2,1)S(1)}, u32[]{:S(2)}, u32[]{:S(2)}) collective-permute-start(bf16[4,128,2048]{2,1,0:T(8,128)(2,1)} %get-tuple-element.72), channel_id=1, source_target_pairs={{0,1},{1,0},{2,3},{3,2},{4,5},{5,4},{6,7},{7,6},{8,9},{9,8},{10,11... | collective-permute-start | bytes 6291464 | tf_op jit(solution)/shard_map/ppermute | solution.py:707
  523.1 30.5 %collective-permute-start.63 = (bf16[4,128,2048]{2,1,0:T(8,128)(2,1)}, bf16[4,128,2048]{2,1,0:T(8,128)(2,1)}, u32[]{:S(2)}, u32[]{:S(2)}) collective-permute-start(bf16[4,128,2048]{2,1,0:T(8,128)(2,1)} %get-tuple-element.74), channel_id=1, source_target_pairs={{0,1},{1,0},{2,3},{3,2},{4,5},{5,4},{6,7},{7,6},{8,9},{9,8},{10,11... | collective-permute-start | bytes 6291464 | tf_op jit(solution)/shard_map/ppermute | solution.py:707
  524.8 30.6 %collective-permute-start.60 = (bf16[2,128,2048]{2,1,0:T(8,128)(2,1)S(1)}, bf16[2,128,2048]{2,1,0:T(8,128)(2,1)}, u32[]{:S(2)}, u32[]{:S(2)}) collective-permute-start(bf16[2,128,2048]{2,1,0:T(8,128)(2,1)S(1)} %add_convert_fusion.3.refs_5_), channel_id=1, source_target_pairs={{0,16},{1,9},{2,18},{3,11},{4,20},{5,13},{6,22},{7,15},{8,24},{9,1... | collective-permute-start | bytes 3145736 | tf_op jit(solution)/shard_map/ppermute | solution.py:723
  526.3 65.0 %all-to-all-start.3 = ((bf16[8,256,384]{2,1,0:T(8,128)(2,1)}), bf16[8,256,384]{2,1,0:T(8,128)(2,1)S(1)}, u32[]{:S(2)}, u32[]{:S(2)}) async-start(bf16[8,256,384]{2,1,0:T(8,128)(2,1)} %feature_grad.3.refs_1_), calls=%async_computation.4 | async-start | bytes 3145728 | tf_op jit(solution)/shard_map/all_to_all | solution.py:819
  553.4 43.1 %collective-permute-start.67 = (bf16[4,128,2048]{2,1,0:T(8,128)(2,1)}, bf16[4,128,2048]{2,1,0:T(8,128)(2,1)}, u32[]{:S(2)}, u32[]{:S(2)}) collective-permute-start(bf16[4,128,2048]{2,1,0:T(8,128)(2,1)} %get-tuple-element.76), channel_id=1, source_target_pairs={{0,1},{1,0},{2,3},{3,2},{4,5},{5,4},{6,7},{7,6},{8,9},{9,8},{10,11... | collective-permute-start | bytes 6291464 | tf_op jit(solution)/shard_map/ppermute | solution.py:707
  567.0 33.1 %collective-permute-start.71 = (bf16[4,128,2048]{2,1,0:T(8,128)(2,1)}, bf16[4,128,2048]{2,1,0:T(8,128)(2,1)}, u32[]{:S(2)}, u32[]{:S(2)}) collective-permute-start(bf16[4,128,2048]{2,1,0:T(8,128)(2,1)} %get-tuple-element.78), channel_id=1, source_target_pairs={{0,1},{1,0},{2,3},{3,2},{4,5},{5,4},{6,7},{7,6},{8,9},{9,8},{10,11... | collective-permute-start | bytes 6291464 | tf_op jit(solution)/shard_map/ppermute | solution.py:707
  567.4 20.4 %collective-permute-start.64 = (bf16[2,128,2048]{2,1,0:T(8,128)(2,1)S(1)}, bf16[2,128,2048]{2,1,0:T(8,128)(2,1)S(1)}, u32[]{:S(2)}, u32[]{:S(2)}) collective-permute-start(bf16[2,128,2048]{2,1,0:T(8,128)(2,1)S(1)} %add_convert_fusion.2.refs_5_), channel_id=1, source_target_pairs={{0,16},{1,9},{2,18},{3,11},{4,20},{5,13},{6,22},{7,15},{8,24},{9,1... | collective-permute-start | bytes 3145736 | tf_op jit(solution)/shard_map/ppermute | solution.py:723
  568.2 79.0 %collective-permute-start.61 = (bf16[128,2048]{1,0:T(8,128)(2,1)}, bf16[128,2048]{1,0:T(8,128)(2,1)}, u32[]{:S(2)}, u32[]{:S(2)}) collective-permute-start(bf16[128,2048]{1,0:T(8,128)(2,1)} %fusion.18.refs_6_), channel_id=1, source_target_pairs={{0,8},{1,17},{2,10},{3,19},{4,12},{5,21},{6,14},{7,23},{8,0},{9,25... | collective-permute-start | bytes 1572872 | tf_op jit(solution)/shard_map/ppermute | solution.py:723
  590.2 52.1 %collective-permute-start.65 = (bf16[128,2048]{1,0:T(8,128)(2,1)}, bf16[128,2048]{1,0:T(8,128)(2,1)}, u32[]{:S(2)}, u32[]{:S(2)}) collective-permute-start(bf16[128,2048]{1,0:T(8,128)(2,1)} %fusion.19.refs_2_), channel_id=1, source_target_pairs={{0,8},{1,17},{2,10},{3,19},{4,12},{5,21},{6,14},{7,23},{8,0},{9,25... | collective-permute-start | bytes 1572872 | tf_op jit(solution)/shard_map/ppermute | solution.py:723
  591.4 39.5 %all-to-all-start.4 = ((bf16[8,256,384]{2,1,0:T(8,128)(2,1)}), bf16[8,256,384]{2,1,0:T(8,128)(2,1)S(1)}, u32[]{:S(2)}, u32[]{:S(2)}) async-start(bf16[8,256,384]{2,1,0:T(8,128)(2,1)} %feature_grad.4.refs_1_), calls=%async_computation.5 | async-start | bytes 3145728 | tf_op jit(solution)/shard_map/all_to_all | solution.py:819
  599.5 40.4 %collective-permute-start.68 = (bf16[2,128,2048]{2,1,0:T(8,128)(2,1)}, bf16[2,128,2048]{2,1,0:T(8,128)(2,1)}, u32[]{:S(2)}, u32[]{:S(2)}) collective-permute-start(bf16[2,128,2048]{2,1,0:T(8,128)(2,1)} %add_convert_fusion.1.refs_1_), channel_id=1, source_target_pairs={{0,16},{1,9},{2,18},{3,11},{4,20},{5,13},{6,22},{7,15},{8,24},{9,1... | collective-permute-start | bytes 3145736 | tf_op jit(solution)/shard_map/ppermute | solution.py:723
  602.7 52.0 %collective-permute-start.72 = (bf16[2,128,2048]{2,1,0:T(8,128)(2,1)}, bf16[2,128,2048]{2,1,0:T(8,128)(2,1)}, u32[]{:S(2)}, u32[]{:S(2)}) collective-permute-start(bf16[2,128,2048]{2,1,0:T(8,128)(2,1)} %add_convert_fusion.refs_3_), channel_id=1, source_target_pairs={{0,16},{1,9},{2,18},{3,11},{4,20},{5,13},{6,22},{7,15},{8,24},{9,1... | collective-permute-start | bytes 3145736 | tf_op jit(solution)/shard_map/ppermute | solution.py:723
  632.0 64.8 %all-to-all-start.5 = ((bf16[8,256,384]{2,1,0:T(8,128)(2,1)}), bf16[8,256,384]{2,1,0:T(8,128)(2,1)}, u32[]{:S(2)}, u32[]{:S(2)}) async-start(bf16[8,256,384]{2,1,0:T(8,128)(2,1)} %tied.21), calls=%async_computation.6 | async-start | bytes 3145728 | tf_op jit(solution)/shard_map/all_to_all | solution.py:819
  641.3 9.2 %collective-permute-start.69 = (bf16[128,2048]{1,0:T(8,128)(2,1)S(1)}, bf16[128,2048]{1,0:T(8,128)(2,1)S(1)}, u32[]{:S(2)}, u32[]{:S(2)}) collective-permute-start(bf16[128,2048]{1,0:T(8,128)(2,1)S(1)} %fusion.20), channel_id=1, source_target_pairs={{0,8},{1,17},{2,10},{3,19},{4,12},{5,21},{6,14},{7,23},{8,0},{9,25... | collective-permute-start | bytes 1572872 | tf_op jit(solution)/shard_map/ppermute | solution.py:723
  644.8 63.1 %collective-permute-start.66 = (bf16[128,2048]{1,0:T(8,128)(2,1)}, bf16[128,2048]{1,0:T(8,128)(2,1)}, u32[]{:S(2)}, u32[]{:S(2)}) collective-permute-start(bf16[128,2048]{1,0:T(8,128)(2,1)} %fusion.14), channel_id=1, source_target_pairs={{0,4},{2,6},{4,0},{6,2},{1,5},{3,7},{5,1},{7,3},{8,12},{10,14},{12... | collective-permute-start | bytes 1572872 | tf_op jit(solution)/shard_map/ppermute | solution.py:703
  649.9 71.4 %collective-permute-start.62 = (bf16[128,2048]{1,0:T(8,128)(2,1)}, bf16[128,2048]{1,0:T(8,128)(2,1)}, u32[]{:S(2)}, u32[]{:S(2)}) collective-permute-start(bf16[128,2048]{1,0:T(8,128)(2,1)} %fusion.15), channel_id=1, source_target_pairs={{0,6},{2,0},{4,2},{6,4},{1,7},{3,1},{5,3},{7,5},{8,14},{10,8},{12,... | collective-permute-start | bytes 1572872 | tf_op jit(solution)/shard_map/ppermute | solution.py:703
  652.9 68.4 %collective-permute-start.70 = (bf16[128,2048]{1,0:T(8,128)(2,1)}, bf16[128,2048]{1,0:T(8,128)(2,1)}, u32[]{:S(2)}, u32[]{:S(2)}) collective-permute-start(bf16[128,2048]{1,0:T(8,128)(2,1)} %fusion.13), channel_id=1, source_target_pairs={{0,2},{2,4},{4,6},{6,0},{1,3},{3,5},{5,7},{7,1},{8,10},{10,12},{12... | collective-permute-start | bytes 1572872 | tf_op jit(solution)/shard_map/ppermute | solution.py:703
  657.0 64.3 %collective-permute-start.73 = (bf16[128,2048]{1,0:T(8,128)(2,1)}, bf16[128,2048]{1,0:T(8,128)(2,1)}, u32[]{:S(2)}, u32[]{:S(2)}) collective-permute-start(bf16[128,2048]{1,0:T(8,128)(2,1)} %fusion.21), channel_id=1, source_target_pairs={{0,8},{1,17},{2,10},{3,19},{4,12},{5,21},{6,14},{7,23},{8,0},{9,25... | collective-permute-start | bytes 1572872 | tf_op jit(solution)/shard_map/ppermute | solution.py:723
  704.3 19.8 %collective-permute-start.74 = (f32[256]{0:T(256)S(1)}, f32[256]{0:T(256)S(1)}, u32[]{:S(2)}, u32[]{:S(2)}) collective-permute-start(f32[256]{0:T(256)S(1)} %add.601), channel_id=1, source_target_pairs={{0,16},{16,0},{1,17},{17,1},{2,18},{18,2},{3,19},{19,3},{4,20},{20... | collective-permute-start | bytes 3080 | tf_op jit(solution)/shard_map/ppermute | solution.py:1106
  (142 other events, 1197.1 us)
Sparse Core Ops, SparseCore 0:
  132.5 139.4 all-gather.2
  346.8 187.7 reduce-scatter.1

commit v2 on v1

--- a/solution.py
+++ b/solution.py
@@ -200,28 +200,35 @@
     if len(outs) == 1:
         outs[0][...] = total
     else:
-        for i, out in enumerate(outs):
-
-            @pl.when(pl.program_id(0) == i)
-            def _():
-                out[...] = total
-
-
-def trail_product(lefts, facts, weights, mods, k=None, beside=()):
+        is_far = pl.program_id(0) < pl.num_programs(0) // 2
+
+        @pl.when(is_far)
+        def _():
+            outs[0][...] = total
+
+        @pl.when(jnp.logical_not(is_far))
+        def _():
+            outs[1][...] = total
+
+
+def trail_product(lefts, facts, weights, mods, ks=None, beside=()):
     pieces, here, mine = lefts[0].shape
     features = weights[0].shape[0]
-    if k is None:
+    if ks is None:
         steps, outs = pieces // 4, [shape((pieces, here, features), bf16)]
         out_specs = [pl.BlockSpec((4, here, features), lambda i: (i, 0, 0))]
 
         def block(i):
             return (i, 0, 0)
     else:
-        steps, outs = 2, [shape((4, here, features), bf16)] * 2
-        out_specs = [everything(out) for out in outs]
+        steps, outs = 4, [shape((8, here, features), bf16)] * 2
+        out_specs = [
+            pl.BlockSpec((4, here, features), lambda i: (jnp.minimum(i, 1), 0, 0)),
+            pl.BlockSpec((4, here, features), lambda i: (jnp.maximum(i - 2, 0), 0, 0)),
+        ]
 
         def block(i):
-            return (2 * k + 1 - i, 0, 0)
+            return (2 * jnp.where(i % 2 == 0, ks[0], ks[1]) + jnp.where(i < 2, 1, 0), 0, 0)
 
     return pl.pallas_call(
         functools.partial(trail_kernel, mods, len(lefts), len(beside)),
@@ -479,7 +486,7 @@
 
 def backward_kernel(
     mods, tables, proj_ref, pre_ref, facts_ref, gate_ref, scanned_ref, dt_ref, d_gated_ref, kept_ref, dtw_ref, rate2_ref,
-    rate_ref, skip_ref, last_ref, carry_ref, sum_ref, expand_ref, d_gate_ref, d_proj_ref, d_act_ref, dtw_grad_ref, dtb_grad_ref,
+    rate_ref, skip_ref, last_ref, carry_ref, sum_ref, expand_ref, _, d_gate_ref, d_proj_ref, d_act_ref, dtw_grad_ref, dtb_grad_ref,
     skip_grad_ref, rate_sum_ref, carry_out_ref, carried, later, products, step_line, drive_line, turned, tiles, back_line,
     pulled_line, weighted_line, small_line,
 ):
@@ -575,7 +582,9 @@
         d_proj_ref[r, 0, here:] = small[:narrow].astype(bf16)
 
 
-def scan_backward(tables, proj, pre, facts, gate, scanned, dt_pre, d_gated, kept, dtw, rates2, rates, skip, last, carry):
+def scan_backward(
+    tables, proj, pre, facts, gate, scanned, dt_pre, d_gated, kept, dtw, rates2, rates, skip, last, carry, beside
+):
     rows, length, mine = pre.shape
     _, blocks, deep, here = proj.shape
     pieces, subl, _ = rates2.shape
@@ -601,7 +610,8 @@
             item,
             pl.BlockSpec((here, pieces, subl, mine), lambda i: (blocks - 1 - i, 0, 0, 0)),
         ]
-        + [everything(array) for array in (dtw, rates2, rates, skip, last, carry, summing, expand)],
+        + [everything(array) for array in (dtw, rates2, rates, skip, last, carry, summing, expand)]
+        + [pl.BlockSpec(memory_space=pl.ANY)],
         out_specs=[everything(d_gate), proj_item, item] + [everything(array) for array in small + [carry]],
         out_shape=[d_gate, shape(proj.shape, bf16), shape(pre.shape, f32)] + small + [shape(carry.shape, f32)],
         scratch_shapes=[pltpu.VMEM(carry.shape, f32)] * 2 + [pltpu.VMEM((subl * here, columns), bf16)] + [line] * 3
@@ -609,7 +619,7 @@
         compiler_params=params(),
         cost_estimate=cost(7500 * length * pieces * subl * mine, 5 * length * pieces * subl * mine),
         name="scan_backward",
-    )(tables, proj, pre, facts, gate, scanned, dt_pre, d_gated, kept, dtw, rates2, rates, skip, last, carry, summing, expand)
+    )(tables, proj, pre, facts, gate, scanned, dt_pre, d_gated, kept, dtw, rates2, rates, skip, last, carry, summing, expand, beside)
 
 
 def deconv_kernel(
@@ -782,37 +792,22 @@
     def added(*terms):
         return sum(term.astype(f32) for term in terms)
 
-    order = list(range(1, lax.axis_size("z"))) + [0]
-    far, near, first, second = {}, {}, {}, {}
-
-    def make(i, *others):
-        away, near[i] = made(order[i], list(others))
-        far[i] = swapped(away)
-
-    def send_first(i):
-        first[i] = added(near[i][2:], far[i][2:]).astype(bf16)
-        return first[i]
-
-    def send_second(i):
-        come = hop(first[i], True)
-        second[i] = (added(near[i][1], far[i][1], come[1]).astype(bf16), come[0])
-        return second[i][0]
-
-    make(0)
-    make(1)
-    make(2, send_first(0))
-    make(3, send_first(1), send_second(0))
-    extra = beside([send_first(2), send_second(1), send_first(3)])
+    groups = [(1, 2), (3, 0)]
+    far, near = {}, {}
+    for i, ks in enumerate(groups):
+        away, here = made(ks, [beside[i]])
+        far[i] = swapped(away).reshape((len(ks), 4) + away.shape[1:])
+        near[i] = here.reshape((len(ks), 4) + here.shape[1:])
     total = None
-    for i, k in enumerate(order):
-        if i > 1:
-            send_second(i)
-        last = hop(second[i][0], False)
-        total_k = added(near[i][0], far[i][0], second[i][1], last)
-        if k:
-            total_k = shifted(total_k.astype(bf16), -k).astype(f32)
-        total = total_k if total is None else total + total_k
-    return total, extra
+    for i, ks in enumerate(groups):
+        payload = added(near[i][:, 2:], far[i][:, 2:]).astype(bf16)
+        come = hop(payload, True)
+        last = hop(added(near[i][:, 1], far[i][:, 1], come[:, 1]).astype(bf16), False)
+        held = added(near[i][:, 0], far[i][:, 0], come[:, 0], last)
+        for j, k in enumerate(ks):
+            own = shifted(held[j].astype(bf16), -k).astype(f32) if k else held[j]
+            total = own if total is None else total + own
+    return total
 
 
 def exchanged(parts):
@@ -1016,7 +1011,7 @@
     def summed(part, beside, final):
         return team_sum(part.reshape((2, 2, depth, 2) + part.shape[2:]), beside, final).reshape(part.shape)
 
-    proj = summed(proj_part, [gate_in], [])
+    proj = summed(proj_part, [facts, gate_in], [])
     wo = spread_done(tied(spread_weight(lead(out_weight)), proj))
     d_gated, wo_f = lead_product(in_order, d_branch, facts_flat, wo, f32)
     d_gated = d_gated.reshape(rows, local_len, mine)
@@ -1056,7 +1051,7 @@
     def back(carry):
         return scan_backward(
             relative, proj, pre, facts, gate_in, scanned, dt_pre, d_gated, kept, dt_f, rates2, rates, skip_row, last_state,
-            carry,
+            carry, out_parts,
         )
 
     results = back(zero_state)
@@ -1065,7 +1060,7 @@
     d_gate, d_proj_part, d_act, dtw_grad, dtb_grad, skip_grad, rate_total, _ = results
     z_parts = weight_grad(normed, d_gate, facts_there)
     out_got, z_got = collect(out_parts), collect(z_parts)
-    d_proj = summed(d_proj_part, [out_parts, z_parts], [])
+    d_proj = summed(tied(d_proj_part, out_got), [z_parts], [])
     out_weight_grad = lead(settled(out_got, lead(out_weight))[0])
     in_z_grad, gain_z = settled(z_got, lead(in_z_weight))
     rate_total = jnp.sum(rate_total.reshape(pieces, halves, rows, mine), axis=2)
@@ -1093,12 +1088,12 @@
     xbc_grad = outer_summed(xbc_grad, 2)
     conv_weight_grad = outer_summed(taps_grad, 1)
     conv_bias_grad = outer_summed(bias_grad[0], 0)
-    d_scaled, x_parts = team_scatter(
-        lambda k, others: trail_product([d_conv, d_gate], facts_there, [wx_f, wz_f], mods, k, others),
-        lambda others: weight_grad(normed, d_conv, facts_there, out_got, *others),
+    x_parts = weight_grad(normed, d_conv, facts_there)
+    d_scaled = team_scatter(
+        lambda ks, others: trail_product([d_conv, d_gate], facts_there, [wx_f, wz_f], mods, ks, others), [z_got, x_parts]
     )
     d_scaled = d_scaled * gain
-    in_x_grad, gain_x = settled(collect(tied(x_parts, z_got)), lead(in_x_weight))
+    in_x_grad, gain_x = settled(collect(x_parts), lead(in_x_weight))
     d_inputs = inv_rms * (d_scaled - scaled * jnp.mean(d_scaled * scaled, axis=-1, keepdims=True))
     tokens_grad = (upstream + d_inputs).astype(bf16)[None]
     gain_part = gain_x + gain_z

time: 744 us -> 738 us (level)
    all_to_all x6, waiting for transfers between devices: 36.4 us -> 2.25 us  [exchanged(): return lax.all_to_all(parts, group_axes, 0, 0, tiled=True)]
    ppermute x20 -> x16, waiting for transfers between devices: 58.1 us -> 88.6 us  [hop(): return lax.ppermute(value, team_axes, pairs)]
    convert_element_type x11 -> x4, other arithmetic: 24 us -> 9.54 us  [the longest x2 5.98 us: team_scatter(): added(near[i][:, 1], far[i][:, 1], come[:, 1]).astype(bf16)]
    ppermute x21, waiting for transfers between devices: 81 us -> 72.7 us  [shifted(): lax.ppermute(value, 'z', [(i, (i + by) % size) for i in range(size)])]
    pallas_call x5 -> x3, Pallas kernels: 48.2 us -> 41.2 us  [trail_product(): pl.pallas_call(functools.partial(trail_kernel, mods, len(lefts), len(besi...]
    unnamed x255 -> x245, local copies, waits for them, and re-layouts: 42.8 us -> 49.6 us
    ppermute x20 -> x16, starting transfers between devices: 22.4 us -> 17.1 us  [hop(): return lax.ppermute(value, team_axes, pairs)]
  transfers between devices with their start and end apart: 84 -> 78, of which waited for: 39 -> 39; matrix products, arithmetic and copies ran while one was open for 9% -> 8% of each run, Pallas kernels for 33% -> 33%
where the time goes in v2:
time: 738 us; the launch traced here: 727 us
  Pallas kernels  267 us (36%)
  waiting for transfers between devices  209 us (28%)
  starting transfers between devices  121 us (16%)
  local copies, waits for them, and re-layouts  72.3 us (10%)
  other arithmetic  41.2 us (6%)
  between operations  15.8 us (2%)
    ppermute x16, waiting for transfers between devices, hop(): return lax.ppermute(value, team_axes, pairs)  88.6 us
    ppermute x21, waiting for transfers between devices, shifted(): lax.ppermute(value, 'z', [(i, (i + by) % size) for i in range(size)])  72.7 us
    pallas_call x1, Pallas kernels, scan_backward(): pl.pallas_call(functools.partial(backward_kernel, dtw.shape[1] // mine),...  62.4 us
    unnamed x245, local copies, waits for them, and re-layouts  49.6 us
    all_to_all x6, starting transfers between devices, exchanged(): return lax.all_to_all(parts, group_axes, 0, 0, tiled=True)  49.5 us
    pallas_call x3, Pallas kernels, feature_grad(): pl.pallas_call(functools.partial(grad_kernel, mods), grid=(wide // some,)...  48.6 us
    pallas_call x3, Pallas kernels, trail_product(): pl.pallas_call(functools.partial(trail_kernel, mods, len(lefts), len(besi...  41.2 us
    ppermute x21, starting transfers between devices, shifted(): lax.ppermute(value, 'z', [(i, (i + by) % size) for i in range(size)])  39 us
  transfers between devices with their start and end apart: 78, of which 39 were waited for; matrix products, arithmetic and copies ran while one was open for 8% of the time, Pallas kernels for 33%

profile of v2, /device:TPU:8, one launch (start us, length us, event | category | flops | bytes accessed | tf_op | source)
XLA Modules:
  0.0 726.8 jit_solution(14864876088194383450)
XLA Ops:
  8.7 3.0 collective-permute-start.1
  11.8 2.5 collective-permute-start
  19.3 2.3 collective-permute-start.4
  23.6 10.6 %collective-permute-done.4.refs_1_.refs_0_ = bf16[128,2048]{1,0:T(8,128)(2,1)S(1)} collective-permute-done((bf16[128,2048]{1,0:T(8,128)(2,1)S(1)}, bf16[128,2048]{1,0:T(8,128)(2,1)S(1)}, u32[]{:S(2)}, u32[]{:S(2)}) %collective-permute-start.4) | collective-permute-done | bytes 524320 | tf_op jit(solution)/shard_map/ppermute | solution.py:713
  35.1 7.7 %all-to-all-start = ((bf16[8,3,256,128]{3,2,1,0:T(8,128)(2,1)}), bf16[8,3,256,128]{3,2,1,0:T(8,128)(2,1)}, u32[]{:S(2)}, u32[]{:S(2)}) async-start(bf16[8,3,256,128]{3,2,1,0:T(8,128)(2,1)} %tied.11), calls=%async_computation | async-start | bytes 3145728 | tf_op jit(solution)/shard_map/all_to_all | solution.py:814
  46.1 11.2 %collective-permute-done.5.refs_1_ = bf16[128,2048]{1,0:T(8,128)(2,1)S(1)} collective-permute-done((bf16[128,2048]{1,0:T(8,128)(2,1)S(1)}, bf16[128,2048]{1,0:T(8,128)(2,1)S(1)}, u32[]{:S(2)}, u32[]{:S(2)}) %collective-permute-start.5) | collective-permute-done | bytes 524320 | tf_op jit(solution)/shard_map/ppermute | solution.py:733
  62.4 28.1 %collective-permute-done.20.refs_0_ = bf16[128,2048]{1,0:T(8,128)(2,1)S(1)} collective-permute-done((bf16[128,2048]{1,0:T(8,128)(2,1)S(1)}, bf16[128,2048]{1,0:T(8,128)(2,1)S(1)}, u32[]{:S(2)}, u32[]{:S(2)}) %collective-permute-start.20) | collective-permute-done | bytes 524320 | tf_op jit(solution)/shard_map/ppermute | solution.py:713
  96.5 11.0 %collective-permute-done.21.refs_2_.refs_25_ = bf16[128,2048]{1,0:T(8,128)(2,1)} collective-permute-done((bf16[128,2048]{1,0:T(8,128)(2,1)}, bf16[128,2048]{1,0:T(8,128)(2,1)}, u32[]{:S(2)}, u32[]{:S(2)}) %collective-permute-start.21) | collective-permute-done | bytes 524320 | tf_op jit(solution)/shard_map/ppermute | solution.py:733
  108.9 7.5 %collective-permute-done.19.refs_0_ = bf16[128,2048]{1,0:T(8,128)(2,1)} collective-permute-done((bf16[128,2048]{1,0:T(8,128)(2,1)}, bf16[128,2048]{1,0:T(8,128)(2,1)}, u32[]{:S(2)}, u32[]{:S(2)}) %collective-permute-start.19) | collective-permute-done | bytes 524320 | tf_op jit(solution)/shard_map/ppermute | solution.py:713
  120.9 11.4 %collective-permute-done.24.refs_18_.refs_2_ = bf16[128,2048]{1,0:T(8,128)(2,1)} collective-permute-done((bf16[128,2048]{1,0:T(8,128)(2,1)}, bf16[128,2048]{1,0:T(8,128)(2,1)}, u32[]{:S(2)}, u32[]{:S(2)}) %collective-permute-start.24) | collective-permute-done | bytes 524320 | tf_op jit(solution)/shard_map/ppermute | solution.py:733
  134.3 6.7 all-to-all-start.1
  151.6 5.8 collective-permute-done.25.refs_19_
  167.0 17.6 %lead_pieces.1 = (bf16[32,128,128]{2,1,0:T(8,128)(2,1)}, bf16[2048,384]{1,0:T(8,128)(2,1)}, bf16[32,128,2048]{2,1,0:T(8,128)(2,1)}) custom-call(s32[32]{0:T(128)S(1)} %add.476.places, f32[32,8,128]{2,1,0:T(8,128)S(1)} %gather_fusion.1, bf16[8,3,256,128]{3,2,1,0:T(8,128)(2,1)} %all-to-all-done.refs_4_.weight_ref, bf16[128,2048]{1,0:T(8,128)(2,1)S(1)} %fusion.6.refs_0_, ...), custom_call_target="tpu_custom_call" | custom-call | flops 6442450944 | bytes 33554432 | tf_op jit(solution)/shard_map/lead_pieces/pallas_call | solution.py:174
  186.6 6.4 conv_block.1
  197.6 9.3 %collective-permute-done.36 = bf16[2,4,160,128]{3,2,1,0:T(8,128)(2,1)S(1)} collective-permute-done((bf16[2,4,160,128]{3,2,1,0:T(8,128)(2,1)S(1)}, bf16[2,4,160,128]{3,2,1,0:T(8,128)(2,1)S(1)}, u32[]{:S(2)}, u32[]{:S(2)}) %collective-permute-start.36) | collective-permute-done | bytes 327712 | tf_op jit(solution)/shard_map/ppermute | solution.py:871
  208.6 14.5 %lead_product.2 = (f32[32,128,128]{2,1,0:T(8,128)S(1)}, bf16[2048,384]{1,0:T(8,128)(2,1)S(1)}) custom-call(s32[32]{0:T(128)S(1)} %add.476.places, bf16[32,128,2048]{2,1,0:T(8,128)(2,1)} %get-tuple-element.51.x_ref, f32[32,8,128]{2,1,0:T(8,128)S(1)} %gather_fusion.1, bf16[8,3,256,128]{3,2,1,0:T(8,128)(2,1)} %all-to-all-done.1.weight_ref), custom_call_target="tpu_custom_call" | custom-call | flops 6442450944 | bytes 16777216 | tf_op jit(solution)/shard_map/lead_product/pallas_call | solution.py:113
  230.1 2.3 collective-permute-start.39
  232.5 2.9 collective-permute-done.40
  237.9 4.0 collective-permute-start.43
  241.8 2.2 collective-permute-start.41
  244.6 3.2 collective-permute-done.42
  260.0 5.5 collective-permute-done.45
  265.8 1.9 collective-permute-done.46
  269.2 7.4 %all-to-all-start.2 = ((bf16[8,3,256,128]{3,2,1,0:T(8,128)(2,1)}), bf16[8,3,256,128]{3,2,1,0:T(8,128)(2,1)S(1)}, u32[]{:S(2)}, u32[]{:S(2)}) async-start(bf16[8,3,256,128]{3,2,1,0:T(8,128)(2,1)} %tied.19), calls=%async_computation.2 | async-start | bytes 3145728 | tf_op jit(solution)/shard_map/all_to_all | solution.py:814
  278.3 31.4 %scan_forward.1 = (bf16[4,1024,128]{2,1,0:T(8,128)(2,1)S(1)}, f32[4,1024,128]{2,1,0:T(8,128)S(1)}, f32[4,1024,128]{2,1,0:T(8,128)}, f32[1024,8,8,128]{3,2,1,0:T(8,128)}, f32[8,8,128]{2,1,0:T(8,128)S(1)}) custom-call(bf16[4,8,160,128]{3,2,1,0:T(8,128)(2,1)S(1)} %bitcast.296, f32[4,1024,128]{2,1,0:T(8,128)} %copy-done.75, f32[4,8,8,128]{3,2,1,0:T(8,128)S(1)} %copy-done.28, ...), custom_call_target="tpu_custom_call" | custom-call | flops 46137344000 | bytes 41943040 | tf_op jit(solution)/shard_map/scan_forward/pallas_call | solution.py:455
  314.3 13.4 %lead_product.3 = (f32[32,128,128]{2,1,0:T(8,128)S(1)}, bf16[2048,384]{1,0:T(8,128)(2,1)S(1)}) custom-call(s32[32]{0:T(128)S(1)} %iota.68.places, bf16[32,128,2048]{2,1,0:T(8,128)(2,1)} %bitcast.362, f32[32,8,128]{2,1,0:T(8,128)S(1)} %copy-done.31, bf16[8,3,256,128]{3,2,1,0:T(8,128)(2,1)S(1)} %all-to-all-done.2.weight_ref), custom_call_target="tpu_custom_call" | custom-call | flops 6442450944 | bytes 16777216 | tf_op jit(solution)/shard_map/lead_product/pallas_call | solution.py:113
  329.0 14.0 %trail_product.3 = bf16[32,128,2048]{2,1,0:T(8,128)(2,1)} custom-call(bf16[32,128,128]{2,1,0:T(8,128)(2,1)S(1)} %bitcast.316, f32[32,8,128]{2,1,0:T(8,128)S(1)} %copy-done.31, bf16[2048,384]{1,0:T(8,128)(2,1)S(1)} %get-tuple-element.55.refs_2_), custom_call_target="tpu_custom_call" | custom-call | flops 6442450944 | bytes 16777216 | tf_op jit(solution)/shard_map/trail_product/pallas_call | solution.py:233
  345.2 15.4 %feature_grad.3._ = bf16[8,256,384]{2,1,0:T(8,128)(2,1)S(1)} custom-call(bf16[4096,2048]{1,0:T(8,128)(2,1)} %all-gather.3.cloned.1.call-done.x_ref, bf16[32,128,128]{2,1,0:T(8,128)(2,1)S(1)} %bitcast.317, f32[32,8,128]{2,1,0:T(8,128)S(1)} %copy-done.32), custom_call_target="tpu_custom_call" | custom-call | flops 19327352832 | bytes 16777216 | tf_op jit(solution)/shard_map/feature_grad/pallas_call | solution.py:268
  361.8 5.3 all-to-all-start.3
  372.1 62.4 %scan_backward.1 = (bf16[32,128,128]{2,1,0:T(8,128)(2,1)S(1)}, bf16[4,8,160,128]{3,2,1,0:T(8,128)(2,1)S(1)}, f32[4,1024,128]{2,1,0:T(8,128)}, f32[128,384]{1,0:T...) custom-call(s32[32]{0:T(128)S(1)} %scatter_custom_fusion.tables, ...), custom_call_target="tpu_custom_call" | custom-call | flops 62914560000 | bytes 41943040 | tf_op jit(solution)/shard_map/scan_backward/pallas_call | solution.py:599
  445.2 16.4 %feature_grad.4.refs_1_ = bf16[8,256,384]{2,1,0:T(8,128)(2,1)} custom-call(bf16[4096,2048]{1,0:T(8,128)(2,1)} %bitcast.366, bf16[32,128,128]{2,1,0:T(8,128)(2,1)S(1)} %copy-done.72, f32[32,8,128]{2,1,0:T(8,128)S(1)} %copy-done.38), custom_call_target="tpu_custom_call" | custom-call | flops 19327352832 | bytes 16777216 | tf_op jit(solution)/shard_map/feature_grad/pallas_call | solution.py:268
  463.9 4.7 collective-permute-done.49
  470.3 2.4 collective-permute-start.52
  472.7 4.0 collective-permute-start.51
  476.7 2.9 collective-permute-done.52
  481.5 2.0 collective-permute-start.55
  484.2 2.8 collective-permute-start.53
  489.6 2.1 collective-permute-done.53
  494.0 3.9 collective-permute-done.56
  498.4 6.7 collective-permute-done.57
  506.7 13.5 %all-to-all-start.4 = ((bf16[8,256,384]{2,1,0:T(8,128)(2,1)}), bf16[8,256,384]{2,1,0:T(8,128)(2,1)S(1)}, u32[]{:S(2)}, u32[]{:S(2)}) async-start(bf16[8,256,384]{2,1,0:T(8,128)(2,1)} %feature_grad.4.refs_1_), calls=%async_computation.5 | async-start | bytes 3145728 | tf_op jit(solution)/shard_map/all_to_all | solution.py:814
  523.5 17.8 %deconv_block.1 = (bf16[32,128,128]{2,1,0:T(8,128)(2,1)S(1)}, f32[128,384]{1,0:T(8,128)S(1)}, f32[96,128]{1,0:T(8,128)S(1)}, f32[4,128]{1,0:T(4,128)}, f32[1,128...) custom-call(s32[32]{0:T(128)S(1)} %scatter_custom_fusion.tables, bf16[4,8,160,128]{3,2,1,0:T(8,128)(2,1)S(1)} %bitcast.301, ...), custom_call_target="tpu_custom_call" | custom-call | flops 15728640000 | bytes 7340032 | tf_op jit(solution)/shard_map/deconv_block/pallas_call | solution.py:684
  541.4 16.8 %feature_grad.5.refs_5_ = bf16[8,256,384]{2,1,0:T(8,128)(2,1)} custom-call(bf16[4096,2048]{1,0:T(8,128)(2,1)} %bitcast.367, bf16[32,128,128]{2,1,0:T(8,128)(2,1)S(1)} %get-tuple-element.64.refs_0_.d_ref, f32[32,8,128]{2,1,0:T(8,128)S(1)} %copy-done.38), custom_call_target="tpu_custom_call" | custom-call | flops 19327352832 | bytes 16777216 | tf_op jit(solution)/shard_map/feature_grad/pallas_call | solution.py:268
  558.2 13.6 %trail_product.5 = (bf16[8,128,2048]{2,1,0:T(8,128)(2,1)}, bf16[8,128,2048]{2,1,0:T(8,128)(2,1)}) custom-call(bf16[32,128,128]{2,1,0:T(8,128)(2,1)S(1)} %get-tuple-element.64.refs_0_.d_ref, bf16[32,128,128]{2,1,0:T(8,128)(2,1)S(1)} %copy-done.72, f32[32,8,128]{2,1,0:T(8,128)S(1)} %copy-done.38, bf16[2048,384]{1,0:T(8,128)(2,1)S(1)} %copy-done.66, ...), custom_call_target="tpu_custom_call" | custom-call | flops 6442450944 | bytes 8388608 | tf_op jit(solution)/shard_map/trail_product/pallas_call | solution.py:233
  572.0 2.2 all-to-all-done.4.refs_5_.got_ref
  579.4 13.5 %trail_product.4 = (bf16[8,128,2048]{2,1,0:T(8,128)(2,1)}, bf16[8,128,2048]{2,1,0:T(8,128)(2,1)}) custom-call(bf16[32,128,128]{2,1,0:T(8,128)(2,1)S(1)} %copy-done.74, bf16[32,128,128]{2,1,0:T(8,128)(2,1)S(1)} %copy-done.72, f32[32,8,128]{2,1,0:T(8,128)S(1)} %copy-done.38, bf16[2048,384]{1,0:T(8,128)(2,1)S(1)} %copy-done.67, ...), custom_call_target="tpu_custom_call" | custom-call | flops 6442450944 | bytes 8388608 | tf_op jit(solution)/shard_map/trail_product/pallas_call | solution.py:233
  593.0 2.7 add_convert_fusion
  596.8 3.5 collective-permute-done.59
  603.5 18.3 %collective-permute-done.65 = bf16[2,2,128,2048]{3,2,0,1:T(8,128)(2,1)S(1)} collective-permute-done((bf16[2,2,128,2048]{3,2,0,1:T(8,128)(2,1)S(1)}, bf16[2,2,128,2048]{3,2,0,1:T(8,128)(2,1)S(1)}, u32[]{:S(2)}, u32[]{:S(2)}) %collective-permute-start.65) | collective-permute-done | bytes 2097184 | tf_op jit(solution)/shard_map/ppermute | solution.py:733
  621.8 3.5 fusion.13
  625.8 8.8 %all-to-all-start.5 = ((bf16[8,256,384]{2,1,0:T(8,128)(2,1)}), bf16[8,256,384]{2,1,0:T(8,128)(2,1)}, u32[]{:S(2)}, u32[]{:S(2)}) async-start(bf16[8,256,384]{2,1,0:T(8,128)(2,1)} %feature_grad.5.refs_5_), calls=%async_computation.6 | async-start | bytes 3145728 | tf_op jit(solution)/shard_map/all_to_all | solution.py:814
  634.6 21.1 %collective-permute-done.60 = bf16[2,2,128,2048]{3,2,0,1:T(8,128)(2,1)} collective-permute-done((bf16[2,2,128,2048]{3,2,0,1:T(8,128)(2,1)S(1)}, bf16[2,2,128,2048]{3,2,0,1:T(8,128)(2,1)}, u32[]{:S(2)}, u32[]{:S(2)}) %collective-permute-start.60) | collective-permute-done | bytes 2097184 | tf_op jit(solution)/shard_map/ppermute | solution.py:733
  655.6 2.4 fusion.12
  658.5 2.2 bitcast_add_fusion
  663.1 9.8 %collective-permute-done.61 = bf16[2,128,2048]{2,1,0:T(8,128)(2,1)S(1)} collective-permute-done((bf16[2,128,2048]{2,1,0:T(8,128)(2,1)S(1)}, bf16[2,128,2048]{2,1,0:T(8,128)(2,1)S(1)}, u32[]{:S(2)}, u32[]{:S(2)}) %collective-permute-start.61) | collective-permute-done | bytes 1048608 | tf_op jit(solution)/shard_map/ppermute | solution.py:733
  672.9 2.7 fusion
  676.8 4.8 collective-permute-start.62
  681.5 3.7 settle.4
  685.4 6.1 settle.3
  694.0 2.8 collective-permute-done.68
  700.8 3.7 settle.5
  706.7 7.2 collective-permute-done.63
  713.9 2.1 fusion.7
  716.1 3.6 fusion.20
  (499 shorter events, 149.5 us)
Async XLA Ops:
  8.7 6.8 collective-permute-start.2
  8.7 6.8 collective-permute-start.1
  19.3 14.9 %collective-permute-start.4 = (bf16[128,2048]{1,0:T(8,128)(2,1)S(1)}, bf16[128,2048]{1,0:T(8,128)(2,1)S(1)}, u32[]{:S(2)}, u32[]{:S(2)}) collective-permute-start(bf16[128,2048]{1,0:T(8,128)(2,1)S(1)} %fusion.6.refs_0_), channel_id=1, source_target_pairs={{0,2},{2,4},{4,6},{6,0},{1,3},{3,5},{5,7},{7,1},{8,10},{10,12},{12... | collective-permute-start | bytes 1572872 | tf_op jit(solution)/shard_map/ppermute | solution.py:713
  35.1 81.4 %all-to-all-start = ((bf16[8,3,256,128]{3,2,1,0:T(8,128)(2,1)}), bf16[8,3,256,128]{3,2,1,0:T(8,128)(2,1)}, u32[]{:S(2)}, u32[]{:S(2)}) async-start(bf16[8,3,256,128]{3,2,1,0:T(8,128)(2,1)} %tied.11), calls=%async_computation | async-start | bytes 3145728 | tf_op jit(solution)/shard_map/all_to_all | solution.py:814
  42.8 270.5 %all-gather.3.cloned.1.call-start = ((), (), s32[]{:S(2)}) async-start(), calls=%async_computation.8 | async-start | bytes 17301504 | tf_op jit(solution)/shard_map/all_gather | solution.py:967
  42.8 14.5 %collective-permute-start.5 = (bf16[128,2048]{1,0:T(8,128)(2,1)S(1)}, bf16[128,2048]{1,0:T(8,128)(2,1)S(1)}, u32[]{:S(2)}, u32[]{:S(2)}) collective-permute-start(bf16[128,2048]{1,0:T(8,128)(2,1)S(1)} %fusion.6.refs_0_), channel_id=1, source_target_pairs={{0,8},{1,17},{2,10},{3,19},{4,12},{5,21},{6,14},{7,23},{8,0},{9,25... | collective-permute-start | bytes 1572872 | tf_op jit(solution)/shard_map/ppermute | solution.py:733
  44.3 14.2 %collective-permute-start.6 = (bf16[128,2048]{1,0:T(8,128)(2,1)S(1)}, bf16[128,2048]{1,0:T(8,128)(2,1)S(1)}, u32[]{:S(2)}, u32[]{:S(2)}) collective-permute-start(bf16[128,2048]{1,0:T(8,128)(2,1)S(1)} %fusion.6.refs_0_), channel_id=1, source_target_pairs={{0,16},{1,9},{2,18},{3,11},{4,20},{5,13},{6,22},{7,15},{8,24},{9,1... | collective-permute-start | bytes 1572872 | tf_op jit(solution)/shard_map/ppermute | solution.py:733
  45.8 44.6 %collective-permute-start.20 = (bf16[128,2048]{1,0:T(8,128)(2,1)S(1)}, bf16[128,2048]{1,0:T(8,128)(2,1)S(1)}, u32[]{:S(2)}, u32[]{:S(2)}) collective-permute-start(bf16[128,2048]{1,0:T(8,128)(2,1)S(1)} %fusion.6.refs_0_), channel_id=1, source_target_pairs={{0,6},{2,0},{4,2},{6,4},{1,7},{3,1},{5,3},{7,5},{8,14},{10,8},{12,... | collective-permute-start | bytes 1572872 | tf_op jit(solution)/shard_map/ppermute | solution.py:713
  57.3 33.2 %collective-permute-start.7 = (bf16[128,2048]{1,0:T(8,128)(2,1)S(1)}, bf16[128,2048]{1,0:T(8,128)(2,1)S(1)}, u32[]{:S(2)}, u32[]{:S(2)}) collective-permute-start(bf16[128,2048]{1,0:T(8,128)(2,1)S(1)} %collective-permute-done.5.refs_1_), channel_id=1, source_target_pairs={{0,16},{1,9},{2,18},{3,11},{4,20},{5,13},{6,22},{7,15},{8,24},{9,1... | collective-permute-start | bytes 1572872 | tf_op jit(solution)/shard_map/ppermute | solution.py:733
  59.3 31.1 %collective-permute-start.13 = (bf16[128,2048]{1,0:T(8,128)(2,1)}, bf16[128,2048]{1,0:T(8,128)(2,1)S(1)}, u32[]{:S(2)}, u32[]{:S(2)}) collective-permute-start(bf16[128,2048]{1,0:T(8,128)(2,1)} %tied.12.refs_8_), channel_id=1, source_target_pairs={{0,16},{1,9},{2,18},{3,11},{4,20},{5,13},{6,22},{7,15},{8,24},{9,1... | collective-permute-start | bytes 1572872 | tf_op jit(solution)/shard_map/ppermute | solution.py:733
  60.1 30.4 %collective-permute-start.12 = (bf16[128,2048]{1,0:T(8,128)(2,1)}, bf16[128,2048]{1,0:T(8,128)(2,1)S(1)}, u32[]{:S(2)}, u32[]{:S(2)}) collective-permute-start(bf16[128,2048]{1,0:T(8,128)(2,1)} %tied.12.refs_8_), channel_id=1, source_target_pairs={{0,8},{1,17},{2,10},{3,19},{4,12},{5,21},{6,14},{7,23},{8,0},{9,25... | collective-permute-start | bytes 1572872 | tf_op jit(solution)/shard_map/ppermute | solution.py:733
  92.4 15.1 %collective-permute-start.21 = (bf16[128,2048]{1,0:T(8,128)(2,1)}, bf16[128,2048]{1,0:T(8,128)(2,1)}, u32[]{:S(2)}, u32[]{:S(2)}) collective-permute-start(bf16[128,2048]{1,0:T(8,128)(2,1)} %tied.14.refs_24_), channel_id=1, source_target_pairs={{0,8},{1,17},{2,10},{3,19},{4,12},{5,21},{6,14},{7,23},{8,0},{9,25... | collective-permute-start | bytes 1572872 | tf_op jit(solution)/shard_map/ppermute | solution.py:733
  93.9 22.6 %collective-permute-start.19 = (bf16[128,2048]{1,0:T(8,128)(2,1)}, bf16[128,2048]{1,0:T(8,128)(2,1)}, u32[]{:S(2)}, u32[]{:S(2)}) collective-permute-start(bf16[128,2048]{1,0:T(8,128)(2,1)} %tied.13), channel_id=1, source_target_pairs={{0,4},{2,6},{4,0},{6,2},{1,5},{3,7},{5,1},{7,3},{8,12},{10,14},{12... | collective-permute-start | bytes 1572872 | tf_op jit(solution)/shard_map/ppermute | solution.py:713
  93.9 22.6 %collective-permute-start.22 = (bf16[128,2048]{1,0:T(8,128)(2,1)S(1)}, bf16[128,2048]{1,0:T(8,128)(2,1)S(1)}, u32[]{:S(2)}, u32[]{:S(2)}) collective-permute-start(bf16[128,2048]{1,0:T(8,128)(2,1)S(1)} %copy-done.92), channel_id=1, source_target_pairs={{0,16},{1,9},{2,18},{3,11},{4,20},{5,13},{6,22},{7,15},{8,24},{9,1... | collective-permute-start | bytes 1572872 | tf_op jit(solution)/shard_map/ppermute | solution.py:733
  95.4 21.0 %collective-permute-start.14 = (bf16[128,2048]{1,0:T(8,128)(2,1)S(1)}, bf16[128,2048]{1,0:T(8,128)(2,1)}, u32[]{:S(2)}, u32[]{:S(2)}) collective-permute-start(bf16[128,2048]{1,0:T(8,128)(2,1)S(1)} %copy-done.25), channel_id=1, source_target_pairs={{0,16},{1,9},{2,18},{3,11},{4,20},{5,13},{6,22},{7,15},{8,24},{9,1... | collective-permute-start | bytes 1572872 | tf_op jit(solution)/shard_map/ppermute | solution.py:733
  107.5 13.4 %collective-permute-start.30 = (bf16[128,2048]{1,0:T(8,128)(2,1)}, bf16[128,2048]{1,0:T(8,128)(2,1)S(1)}, u32[]{:S(2)}, u32[]{:S(2)}) collective-permute-start(bf16[128,2048]{1,0:T(8,128)(2,1)} %collective-permute-done.21.refs_2_.refs_25_), channel_id=1, source_target_pairs={{0,16},{1,9},{2,18},{3,11},{4,20},{5,13},{6,22},{7,15},{8,24},{9,1... | collective-permute-start | bytes 1572872 | tf_op jit(solution)/shard_map/ppermute | solution.py:733
  117.2 15.0 %collective-permute-start.24 = (bf16[128,2048]{1,0:T(8,128)(2,1)}, bf16[128,2048]{1,0:T(8,128)(2,1)}, u32[]{:S(2)}, u32[]{:S(2)}) collective-permute-start(bf16[128,2048]{1,0:T(8,128)(2,1)} %tied.15.refs_16_), channel_id=1, source_target_pairs={{0,16},{1,9},{2,18},{3,11},{4,20},{5,13},{6,22},{7,15},{8,24},{9,1... | collective-permute-start | bytes 1572872 | tf_op jit(solution)/shard_map/ppermute | solution.py:733
  117.7 14.5 %collective-permute-start.23 = (bf16[128,2048]{1,0:T(8,128)(2,1)}, bf16[128,2048]{1,0:T(8,128)(2,1)}, u32[]{:S(2)}, u32[]{:S(2)}) collective-permute-start(bf16[128,2048]{1,0:T(8,128)(2,1)} %tied.15.refs_16_), channel_id=1, source_target_pairs={{0,8},{1,17},{2,10},{3,19},{4,12},{5,21},{6,14},{7,23},{8,0},{9,25... | collective-permute-start | bytes 1572872 | tf_op jit(solution)/shard_map/ppermute | solution.py:733
  134.3 74.3 %all-to-all-start.1 = ((bf16[8,3,256,128]{3,2,1,0:T(8,128)(2,1)}), bf16[8,3,256,128]{3,2,1,0:T(8,128)(2,1)}, u32[]{:S(2)}, u32[]{:S(2)}) async-start(bf16[8,3,256,128]{3,2,1,0:T(8,128)(2,1)} %bitcast.321), calls=%async_computation.1 | async-start | bytes 3145728 | tf_op jit(solution)/shard_map/all_to_all | solution.py:814
  141.8 5.3 collective-permute-start.15
  142.0 4.7 collective-permute-start.9
  142.4 5.5 collective-permute-start.31
  147.9 9.5 %collective-permute-start.25 = (bf16[128,2048]{1,0:T(8,128)(2,1)}, bf16[128,2048]{1,0:T(8,128)(2,1)}, u32[]{:S(2)}, u32[]{:S(2)}) collective-permute-start(bf16[128,2048]{1,0:T(8,128)(2,1)} %collective-permute-done.23.refs_17_.refs_1_), channel_id=1, source_target_pairs={{0,16},{1,9},{2,18},{3,11},{4,20},{5,13},{6,22},{7,15},{8,24},{9,1... | collective-permute-start | bytes 1572872 | tf_op jit(solution)/shard_map/ppermute | solution.py:733
  150.2 13.7 %collective-permute-start.34 = (bf16[128,2048]{1,0:T(8,128)(2,1)}, bf16[128,2048]{1,0:T(8,128)(2,1)}, u32[]{:S(2)}, u32[]{:S(2)}) collective-permute-start(bf16[128,2048]{1,0:T(8,128)(2,1)} %copy-done.90), channel_id=1, source_target_pairs={{0,1},{1,0},{2,3},{3,2},{4,5},{5,4},{6,7},{7,6},{8,9},{9,8},{10,11... | collective-permute-start | bytes 1572872 | tf_op jit(solution)/shard_map/ppermute | solution.py:717
  150.5 13.3 %collective-permute-start.26 = (bf16[128,2048]{1,0:T(8,128)(2,1)}, bf16[128,2048]{1,0:T(8,128)(2,1)}, u32[]{:S(2)}, u32[]{:S(2)}) collective-permute-start(bf16[128,2048]{1,0:T(8,128)(2,1)} %tied.15.refs_16_), channel_id=1, source_target_pairs={{0,1},{1,0},{2,3},{3,2},{4,5},{5,4},{6,7},{7,6},{8,9},{9,8},{10,11... | collective-permute-start | bytes 1572872 | tf_op jit(solution)/shard_map/ppermute | solution.py:717
  150.7 13.1 %collective-permute-start.28 = (bf16[128,2048]{1,0:T(8,128)(2,1)}, bf16[128,2048]{1,0:T(8,128)(2,1)}, u32[]{:S(2)}, u32[]{:S(2)}) collective-permute-start(bf16[128,2048]{1,0:T(8,128)(2,1)} %collective-permute-done.24.refs_18_.refs_2_), channel_id=1, source_target_pairs={{0,1},{1,0},{2,3},{3,2},{4,5},{5,4},{6,7},{7,6},{8,9},{9,8},{10,11... | collective-permute-start | bytes 1572872 | tf_op jit(solution)/shard_map/ppermute | solution.py:717
  151.2 12.6 %collective-permute-start.27 = (bf16[128,2048]{1,0:T(8,128)(2,1)}, bf16[128,2048]{1,0:T(8,128)(2,1)}, u32[]{:S(2)}, u32[]{:S(2)}) collective-permute-start(bf16[128,2048]{1,0:T(8,128)(2,1)} %collective-permute-done.23.refs_17_.refs_1_), channel_id=1, source_target_pairs={{0,1},{1,0},{2,3},{3,2},{4,5},{5,4},{6,7},{7,6},{8,9},{9,8},{10,11... | collective-permute-start | bytes 1572872 | tf_op jit(solution)/shard_map/ppermute | solution.py:717
  157.4 6.5 collective-permute-start.29
  196.8 10.1 %collective-permute-start.36 = (bf16[2,4,160,128]{3,2,1,0:T(8,128)(2,1)S(1)}, bf16[2,4,160,128]{3,2,1,0:T(8,128)(2,1)S(1)}, u32[]{:S(2)}, u32[]{:S(2)}) collective-permute-start(bf16[2,4,160,128]{3,2,1,0:T(8,128)(2,1)S(1)} %fusion.21), channel_id=1, source_target_pairs={{0,16},{16,0},{1,17},{17,1},{2,18},{18,2},{3,19},{19,3},{4,20},{20... | collective-permute-start | bytes 983048 | tf_op jit(solution)/shard_map/ppermute | solution.py:871
  207.6 18.0 %collective-permute-start.37 = (bf16[4,160,128]{2,1,0:T(8,128)(2,1)}, bf16[4,160,128]{2,1,0:T(8,128)(2,1)S(1)}, u32[]{:S(2)}, u32[]{:S(2)}) collective-permute-start(bf16[4,160,128]{2,1,0:T(8,128)(2,1)} %tied.16), channel_id=1, source_target_pairs={{0,8},{8,0},{1,9},{9,1},{2,10},{10,2},{3,11},{11,3},{4,12},{12,4},... | collective-permute-start | bytes 491528 | tf_op jit(solution)/shard_map/ppermute | solution.py:871
  227.5 5.1 collective-permute-start.38
  228.9 6.5 collective-permute-start.40
  230.1 6.9 collective-permute-start.39
  237.9 6.7 collective-permute-start.43
  241.8 6.0 collective-permute-start.42
  241.8 7.6 %collective-permute-start.41 = (bf16[160,128]{1,0:T(8,128)(2,1)S(1)}, bf16[160,128]{1,0:T(8,128)(2,1)S(1)}, u32[]{:S(2)}, u32[]{:S(2)}) collective-permute-start(bf16[160,128]{1,0:T(8,128)(2,1)S(1)} %fusion.30), channel_id=1, source_target_pairs={{0,2},{2,4},{4,6},{6,0},{1,3},{3,5},{5,7},{7,1},{8,10},{10,12},{12... | collective-permute-start | bytes 122888 | tf_op jit(solution)/shard_map/ppermute | solution.py:713
  250.2 5.9 collective-permute-start.44
  257.1 8.4 %collective-permute-start.45 = (bf16[2,4,160,128]{3,2,1,0:T(8,128)(2,1)S(1)}, bf16[2,4,160,128]{3,2,1,0:T(8,128)(2,1)S(1)}, u32[]{:S(2)}, u32[]{:S(2)}) collective-permute-start(bf16[2,4,160,128]{3,2,1,0:T(8,128)(2,1)S(1)} %pad_maximum_fusion.4), channel_id=1, source_target_pairs={{0,16},{16,0},{1,17},{17,1},{2,18},{18,2},{3,19},{19,3},{4,20},{20... | collective-permute-start | bytes 983048 | tf_op jit(solution)/shard_map/ppermute | solution.py:888
  269.2 44.1 %all-to-all-start.2 = ((bf16[8,3,256,128]{3,2,1,0:T(8,128)(2,1)}), bf16[8,3,256,128]{3,2,1,0:T(8,128)(2,1)S(1)}, u32[]{:S(2)}, u32[]{:S(2)}) async-start(bf16[8,3,256,128]{3,2,1,0:T(8,128)(2,1)} %tied.19), calls=%async_computation.2 | async-start | bytes 3145728 | tf_op jit(solution)/shard_map/all_to_all | solution.py:814
  276.6 439.4 %reduce-scatter.2.cloned.1.call-start = ((), (), s32[]{:S(2)}) async-start(), calls=%async_computation.7 | async-start | bytes 17301504 | tf_op jit(solution)/shard_map/reduce_scatter | solution.py:1042
  361.8 76.0 %all-to-all-start.3 = ((bf16[8,256,384]{2,1,0:T(8,128)(2,1)}), bf16[8,256,384]{2,1,0:T(8,128)(2,1)S(1)}, u32[]{:S(2)}, u32[]{:S(2)}) async-start(bf16[8,256,384]{2,1,0:T(8,128)(2,1)} %copy-done.19), calls=%async_computation.4 | async-start | bytes 3145728 | tf_op jit(solution)/shard_map/all_to_all | solution.py:814
  443.7 17.9 %collective-permute-start.48 = (bf16[2,4,160,128]{3,2,1,0:T(8,128)(2,1)S(1)}, bf16[2,4,160,128]{3,2,1,0:T(8,128)(2,1)S(1)}, u32[]{:S(2)}, u32[]{:S(2)}) collective-permute-start(bf16[2,4,160,128]{3,2,1,0:T(8,128)(2,1)S(1)} %fusion.22), channel_id=1, source_target_pairs={{0,16},{16,0},{1,17},{17,1},{2,18},{18,2},{3,19},{19,3},{4,20},{20... | collective-permute-start | bytes 983048 | tf_op jit(solution)/shard_map/ppermute | solution.py:871
  462.4 6.3 collective-permute-start.49
  468.7 8.0 %collective-permute-start.50 = (bf16[160,128]{1,0:T(8,128)(2,1)S(1)}, bf16[160,128]{1,0:T(8,128)(2,1)S(1)}, u32[]{:S(2)}, u32[]{:S(2)}) collective-permute-start(bf16[160,128]{1,0:T(8,128)(2,1)S(1)} %get-tuple-element.154), channel_id=1, source_target_pairs={{0,2},{2,4},{4,6},{6,0},{1,3},{3,5},{5,7},{7,1},{8,10},{10,12},{12... | collective-permute-start | bytes 122888 | tf_op jit(solution)/shard_map/ppermute | solution.py:713
  470.3 9.3 %collective-permute-start.52 = (bf16[160,128]{1,0:T(8,128)(2,1)S(1)}, bf16[160,128]{1,0:T(8,128)(2,1)S(1)}, u32[]{:S(2)}, u32[]{:S(2)}) collective-permute-start(bf16[160,128]{1,0:T(8,128)(2,1)S(1)} %get-tuple-element.155), channel_id=1, source_target_pairs={{0,6},{2,0},{4,2},{6,4},{1,7},{3,1},{5,3},{7,5},{8,14},{10,8},{12,... | collective-permute-start | bytes 122888 | tf_op jit(solution)/shard_map/ppermute | solution.py:713
  472.7 8.8 %collective-permute-start.51 = (bf16[160,128]{1,0:T(8,128)(2,1)S(1)}, bf16[160,128]{1,0:T(8,128)(2,1)S(1)}, u32[]{:S(2)}, u32[]{:S(2)}) collective-permute-start(bf16[160,128]{1,0:T(8,128)(2,1)S(1)} %get-tuple-element.156), channel_id=1, source_target_pairs={{0,4},{2,6},{4,0},{6,2},{1,5},{3,7},{5,1},{7,3},{8,12},{10,14},{12... | collective-permute-start | bytes 122888 | tf_op jit(solution)/shard_map/ppermute | solution.py:713
  481.5 6.4 collective-permute-start.55
  483.5 6.1 collective-permute-start.54
  484.2 7.5 %collective-permute-start.53 = (bf16[160,128]{1,0:T(8,128)(2,1)S(1)}, bf16[160,128]{1,0:T(8,128)(2,1)S(1)}, u32[]{:S(2)}, u32[]{:S(2)}) collective-permute-start(bf16[160,128]{1,0:T(8,128)(2,1)S(1)} %fusion.27), channel_id=1, source_target_pairs={{0,2},{2,4},{4,6},{6,0},{1,3},{3,5},{5,7},{7,1},{8,10},{10,12},{12... | collective-permute-start | bytes 122888 | tf_op jit(solution)/shard_map/ppermute | solution.py:713
  492.4 5.4 collective-permute-start.56
  497.9 7.1 collective-permute-start.57
  506.7 13.5 %collective-permute-start.58 = (bf16[2,2,4,160,128]{4,3,2,1,0:T(8,128)(2,1)}, bf16[2,2,4,160,128]{4,3,2,1,0:T(8,128)(2,1)}, u32[]{:S(2)}, u32[]{:S(2)}) collective-permute-start(bf16[2,2,4,160,128]{4,3,2,1,0:T(8,128)(2,1)} %pad_maximum_fusion.3), channel_id=1, source_target_pairs={{0,1},{1,0},{2,3},{3,2},{4,5},{5,4},{6,7},{7,6},{8,9},{9,8},{10,11... | collective-permute-start | bytes 1966088 | tf_op jit(solution)/shard_map/ppermute | solution.py:888
  506.7 67.5 %all-to-all-start.4 = ((bf16[8,256,384]{2,1,0:T(8,128)(2,1)}), bf16[8,256,384]{2,1,0:T(8,128)(2,1)S(1)}, u32[]{:S(2)}, u32[]{:S(2)}) async-start(bf16[8,256,384]{2,1,0:T(8,128)(2,1)} %feature_grad.4.refs_1_), calls=%async_computation.5 | async-start | bytes 3145728 | tf_op jit(solution)/shard_map/all_to_all | solution.py:814
  571.8 21.2 %collective-permute-start.64 = (bf16[8,128,2048]{2,1,0:T(8,128)(2,1)}, bf16[8,128,2048]{2,1,0:T(8,128)(2,1)}, u32[]{:S(2)}, u32[]{:S(2)}) collective-permute-start(bf16[8,128,2048]{2,1,0:T(8,128)(2,1)} %get-tuple-element.70), channel_id=1, source_target_pairs={{0,1},{1,0},{2,3},{3,2},{4,5},{5,4},{6,7},{7,6},{8,9},{9,8},{10,11... | collective-permute-start | bytes 12582920 | tf_op jit(solution)/shard_map/ppermute | solution.py:717
  592.9 7.4 %collective-permute-start.59 = (bf16[8,128,2048]{2,1,0:T(8,128)(2,1)}, bf16[8,128,2048]{2,1,0:T(8,128)(2,1)S(1)}, u32[]{:S(2)}, u32[]{:S(2)}) collective-permute-start(bf16[8,128,2048]{2,1,0:T(8,128)(2,1)} %get-tuple-element.68), channel_id=1, source_target_pairs={{0,1},{1,0},{2,3},{3,2},{4,5},{5,4},{6,7},{7,6},{8,9},{9,8},{10,11... | collective-permute-start | bytes 12582920 | tf_op jit(solution)/shard_map/ppermute | solution.py:717
  595.7 26.1 %collective-permute-start.65 = (bf16[2,2,128,2048]{3,2,0,1:T(8,128)(2,1)S(1)}, bf16[2,2,128,2048]{3,2,0,1:T(8,128)(2,1)S(1)}, u32[]{:S(2)}, u32[]{:S(2)}) collective-permute-start(bf16[2,2,128,2048]{3,2,0,1:T(8,128)(2,1)S(1)} %add_convert_fusion), channel_id=1, source_target_pairs={{0,16},{1,9},{2,18},{3,11},{4,20},{5,13},{6,22},{7,15},{8,24},{9,1... | collective-permute-start | bytes 6291464 | tf_op jit(solution)/shard_map/ppermute | solution.py:733
  602.4 53.2 %collective-permute-start.60 = (bf16[2,2,128,2048]{3,2,0,1:T(8,128)(2,1)S(1)}, bf16[2,2,128,2048]{3,2,0,1:T(8,128)(2,1)}, u32[]{:S(2)}, u32[]{:S(2)}) collective-permute-start(bf16[2,2,128,2048]{3,2,0,1:T(8,128)(2,1)S(1)} %add_convert_fusion.1), channel_id=1, source_target_pairs={{0,16},{1,9},{2,18},{3,11},{4,20},{5,13},{6,22},{7,15},{8,24},{9,1... | collective-permute-start | bytes 6291464 | tf_op jit(solution)/shard_map/ppermute | solution.py:733
  625.4 33.2 %collective-permute-start.66 = (bf16[2,128,2048]{2,1,0:T(8,128)(2,1)}, bf16[2,128,2048]{2,1,0:T(8,128)(2,1)S(1)}, u32[]{:S(2)}, u32[]{:S(2)}) collective-permute-start(bf16[2,128,2048]{2,1,0:T(8,128)(2,1)} %fusion.13), channel_id=1, source_target_pairs={{0,8},{1,17},{2,10},{3,19},{4,12},{5,21},{6,14},{7,23},{8,0},{9,25... | collective-permute-start | bytes 3145736 | tf_op jit(solution)/shard_map/ppermute | solution.py:733
  625.8 59.6 %all-to-all-start.5 = ((bf16[8,256,384]{2,1,0:T(8,128)(2,1)}), bf16[8,256,384]{2,1,0:T(8,128)(2,1)}, u32[]{:S(2)}, u32[]{:S(2)}) async-start(bf16[8,256,384]{2,1,0:T(8,128)(2,1)} %feature_grad.5.refs_5_), calls=%async_computation.6 | async-start | bytes 3145728 | tf_op jit(solution)/shard_map/all_to_all | solution.py:814
  658.0 14.9 %collective-permute-start.61 = (bf16[2,128,2048]{2,1,0:T(8,128)(2,1)S(1)}, bf16[2,128,2048]{2,1,0:T(8,128)(2,1)S(1)}, u32[]{:S(2)}, u32[]{:S(2)}) collective-permute-start(bf16[2,128,2048]{2,1,0:T(8,128)(2,1)S(1)} %fusion.12), channel_id=1, source_target_pairs={{0,8},{1,17},{2,10},{3,19},{4,12},{5,21},{6,14},{7,23},{8,0},{9,25... | collective-permute-start | bytes 3145736 | tf_op jit(solution)/shard_map/ppermute | solution.py:733
  661.7 45.1 %collective-permute-start.67 = (bf16[128,2048]{1,0:T(8,128)(2,1)}, bf16[128,2048]{1,0:T(8,128)(2,1)}, u32[]{:S(2)}, u32[]{:S(2)}) collective-permute-start(bf16[128,2048]{1,0:T(8,128)(2,1)} %fusion.18), channel_id=1, source_target_pairs={{0,2},{2,4},{4,6},{6,0},{1,3},{3,5},{5,7},{7,1},{8,10},{10,12},{12... | collective-permute-start | bytes 1572872 | tf_op jit(solution)/shard_map/ppermute | solution.py:713
  676.8 30.0 %collective-permute-start.62 = (bf16[128,2048]{1,0:T(8,128)(2,1)}, bf16[128,2048]{1,0:T(8,128)(2,1)}, u32[]{:S(2)}, u32[]{:S(2)}) collective-permute-start(bf16[128,2048]{1,0:T(8,128)(2,1)} %get-tuple-element.144), channel_id=1, source_target_pairs={{0,6},{2,0},{4,2},{6,4},{1,7},{3,1},{5,3},{7,5},{8,14},{10,8},{12,... | collective-permute-start | bytes 1572872 | tf_op jit(solution)/shard_map/ppermute | solution.py:713
  681.5 32.4 %collective-permute-start.63 = (bf16[128,2048]{1,0:T(8,128)(2,1)}, bf16[128,2048]{1,0:T(8,128)(2,1)}, u32[]{:S(2)}, u32[]{:S(2)}) collective-permute-start(bf16[128,2048]{1,0:T(8,128)(2,1)} %get-tuple-element.145), channel_id=1, source_target_pairs={{0,4},{2,6},{4,0},{6,2},{1,5},{3,7},{5,1},{7,3},{8,12},{10,14},{12... | collective-permute-start | bytes 1572872 | tf_op jit(solution)/shard_map/ppermute | solution.py:713
  696.8 9.4 %collective-permute-start.69 = (f32[256]{0:T(256)S(1)}, f32[256]{0:T(256)S(1)}, u32[]{:S(2)}, u32[]{:S(2)}) collective-permute-start(f32[256]{0:T(256)S(1)} %add.540), channel_id=1, source_target_pairs={{0,8},{8,0},{1,9},{9,1},{2,10},{10,2},{3,11},{11,3},{4,12},{12,4},... | collective-permute-start | bytes 3080 | tf_op jit(solution)/shard_map/ppermute | solution.py:1101
  (131 other events, 922.3 us)
Sparse Core Ops, SparseCore 0:
  132.4 137.6 all-gather.2
  343.2 260.3 reduce-scatter.1

commit v3 on v2

--- a/solution.py
+++ b/solution.py
@@ -785,7 +785,7 @@
     for k in range(4):
         pieces = [near[k], first[k], second[k], third[k]]
         parts += pieces + [swapped(piece) for piece in pieces]
-    return parts, [first[2], second[2], third[3]], weight
+    return parts, [third[2], second[2], third[3]], weight
 
 
 def team_scatter(made, beside):

time: 738 us -> 749 us (1.015)
  waiting for transfers between devices: 209 us -> 223 us
    unnamed x245 -> x241, local copies, waits for them, and re-layouts: 49.6 us -> 47.9 us
  transfers between devices with their start and end apart: 78 -> 78, of which waited for: 39 -> 43; matrix products, arithmetic and copies ran while one was open for 8% -> 8% of each run, Pallas kernels for 33% -> 32%
where the time goes in v3:
time: 749 us; the launch traced here: 739 us
  Pallas kernels  266 us (36%)
  waiting for transfers between devices  223 us (30%)
  starting transfers between devices  122 us (16%)
  local copies, waits for them, and re-layouts  70.7 us (9%)
  other arithmetic  41.3 us (6%)
  between operations  15.8 us (2%)
    ppermute x16, waiting for transfers between devices, hop(): return lax.ppermute(value, team_axes, pairs)  94.2 us
    ppermute x21, waiting for transfers between devices, shifted(): lax.ppermute(value, 'z', [(i, (i + by) % size) for i in range(size)])  78.8 us
    pallas_call x1, Pallas kernels, scan_backward(): pl.pallas_call(functools.partial(backward_kernel, dtw.shape[1] // mine),...  62.4 us
    pallas_call x3, Pallas kernels, feature_grad(): pl.pallas_call(functools.partial(grad_kernel, mods), grid=(wide // some,)...  48.6 us
    unnamed x241, local copies, waits for them, and re-layouts  47.9 us
    all_to_all x6, starting transfers between devices, exchanged(): return lax.all_to_all(parts, group_axes, 0, 0, tiled=True)  47.4 us
    ppermute x21, starting transfers between devices, shifted(): lax.ppermute(value, 'z', [(i, (i + by) % size) for i in range(size)])  43 us
    pallas_call x3, Pallas kernels, trail_product(): pl.pallas_call(functools.partial(trail_kernel, mods, len(lefts), len(besi...  41.2 us
  transfers between devices with their start and end apart: 78, of which 43 were waited for; matrix products, arithmetic and copies ran while one was open for 8% of the time, Pallas kernels for 32%

profile of v3, /device:TPU:8, one launch (start us, length us, event | category | flops | bytes accessed | tf_op | source)
XLA Modules:
  0.0 738.7 jit_solution(10520176673033818534)
XLA Ops:
  8.7 3.0 collective-permute-start.1
  11.8 2.5 collective-permute-start
  19.3 2.3 collective-permute-start.4
  23.6 10.6 %collective-permute-done.4.refs_1_.refs_0_ = bf16[128,2048]{1,0:T(8,128)(2,1)S(1)} collective-permute-done((bf16[128,2048]{1,0:T(8,128)(2,1)S(1)}, bf16[128,2048]{1,0:T(8,128)(2,1)S(1)}, u32[]{:S(2)}, u32[]{:S(2)}) %collective-permute-start.4) | collective-permute-done | bytes 524320 | tf_op jit(solution)/shard_map/ppermute | solution.py:713
  35.1 7.7 %all-to-all-start = ((bf16[8,3,256,128]{3,2,1,0:T(8,128)(2,1)}), bf16[8,3,256,128]{3,2,1,0:T(8,128)(2,1)}, u32[]{:S(2)}, u32[]{:S(2)}) async-start(bf16[8,3,256,128]{3,2,1,0:T(8,128)(2,1)} %tied.11), calls=%async_computation | async-start | bytes 3145728 | tf_op jit(solution)/shard_map/all_to_all | solution.py:814
  46.0 11.2 %collective-permute-done.5.refs_1_ = bf16[128,2048]{1,0:T(8,128)(2,1)S(1)} collective-permute-done((bf16[128,2048]{1,0:T(8,128)(2,1)S(1)}, bf16[128,2048]{1,0:T(8,128)(2,1)S(1)}, u32[]{:S(2)}, u32[]{:S(2)}) %collective-permute-start.5) | collective-permute-done | bytes 524320 | tf_op jit(solution)/shard_map/ppermute | solution.py:733
  62.4 2.4 collective-permute-start.19
  64.8 37.4 %collective-permute-done.20.refs_0_ = bf16[128,2048]{1,0:T(8,128)(2,1)S(1)} collective-permute-done((bf16[128,2048]{1,0:T(8,128)(2,1)S(1)}, bf16[128,2048]{1,0:T(8,128)(2,1)S(1)}, u32[]{:S(2)}, u32[]{:S(2)}) %collective-permute-start.20) | collective-permute-done | bytes 524320 | tf_op jit(solution)/shard_map/ppermute | solution.py:713
  107.6 3.2 collective-permute-done.19.refs_0_
  110.8 7.7 %collective-permute-done.22.refs_3_.refs_26_ = bf16[128,2048]{1,0:T(8,128)(2,1)S(1)} collective-permute-done((bf16[128,2048]{1,0:T(8,128)(2,1)}, bf16[128,2048]{1,0:T(8,128)(2,1)S(1)}, u32[]{:S(2)}, u32[]{:S(2)}) %collective-permute-start.22) | collective-permute-done | bytes 524320 | tf_op jit(solution)/shard_map/ppermute | solution.py:733
  118.5 2.2 collective-permute-done.21.refs_2_.refs_25_
  120.7 3.4 collective-permute-done.14.refs_1_.refs_11_
  128.1 12.0 %collective-permute-done.23.refs_17_ = bf16[128,2048]{1,0:T(8,128)(2,1)} collective-permute-done((bf16[128,2048]{1,0:T(8,128)(2,1)}, bf16[128,2048]{1,0:T(8,128)(2,1)}, u32[]{:S(2)}, u32[]{:S(2)}) %collective-permute-start.23) | collective-permute-done | bytes 524320 | tf_op jit(solution)/shard_map/ppermute | solution.py:733
  143.6 5.9 collective-permute-done.25.refs_19_.refs_1_
  151.7 4.8 all-to-all-start.1
  176.3 17.8 %lead_pieces.1 = (bf16[32,128,128]{2,1,0:T(8,128)(2,1)}, bf16[2048,384]{1,0:T(8,128)(2,1)}, bf16[32,128,2048]{2,1,0:T(8,128)(2,1)}) custom-call(s32[32]{0:T(128)S(1)} %add.476.places, f32[32,8,128]{2,1,0:T(8,128)S(1)} %gather_fusion.1, bf16[8,3,256,128]{3,2,1,0:T(8,128)(2,1)} %all-to-all-done.refs_4_.weight_ref, bf16[128,2048]{1,0:T(8,128)(2,1)S(1)} %fusion.6.refs_0_, ...), custom_call_target="tpu_custom_call" | custom-call | flops 6442450944 | bytes 33554432 | tf_op jit(solution)/shard_map/lead_pieces/pallas_call | solution.py:174
  196.0 6.4 conv_block.1
  206.8 9.2 %collective-permute-done.36 = bf16[2,4,160,128]{3,2,1,0:T(8,128)(2,1)S(1)} collective-permute-done((bf16[2,4,160,128]{3,2,1,0:T(8,128)(2,1)S(1)}, bf16[2,4,160,128]{3,2,1,0:T(8,128)(2,1)S(1)}, u32[]{:S(2)}, u32[]{:S(2)}) %collective-permute-start.36) | collective-permute-done | bytes 327712 | tf_op jit(solution)/shard_map/ppermute | solution.py:871
  217.6 2.1 all-to-all-done.1.weight_ref
  219.7 14.0 %lead_product.2 = (f32[32,128,128]{2,1,0:T(8,128)S(1)}, bf16[2048,384]{1,0:T(8,128)(2,1)S(1)}) custom-call(s32[32]{0:T(128)S(1)} %add.476.places, bf16[32,128,2048]{2,1,0:T(8,128)(2,1)} %get-tuple-element.51.x_ref, f32[32,8,128]{2,1,0:T(8,128)S(1)} %gather_fusion.1, bf16[8,3,256,128]{3,2,1,0:T(8,128)(2,1)} %all-to-all-done.1.weight_ref), custom_call_target="tpu_custom_call" | custom-call | flops 6442450944 | bytes 16777216 | tf_op jit(solution)/shard_map/lead_product/pallas_call | solution.py:113
  238.1 3.6 collective-permute-start.38
  241.7 2.5 collective-permute-start.40
  244.2 2.4 collective-permute-start.39
  246.5 3.7 collective-permute-done.40
  253.0 4.1 collective-permute-start.43
  257.1 2.2 collective-permute-start.41
  272.4 5.2 collective-permute-done.45
  281.4 7.9 %all-to-all-start.2 = ((bf16[8,3,256,128]{3,2,1,0:T(8,128)(2,1)}), bf16[8,3,256,128]{3,2,1,0:T(8,128)(2,1)S(1)}, u32[]{:S(2)}, u32[]{:S(2)}) async-start(bf16[8,3,256,128]{3,2,1,0:T(8,128)(2,1)} %tied.19), calls=%async_computation.2 | async-start | bytes 3145728 | tf_op jit(solution)/shard_map/all_to_all | solution.py:814
  290.9 31.4 %scan_forward.1 = (bf16[4,1024,128]{2,1,0:T(8,128)(2,1)S(1)}, f32[4,1024,128]{2,1,0:T(8,128)S(1)}, f32[4,1024,128]{2,1,0:T(8,128)}, f32[1024,8,8,128]{3,2,1,0:T(8,128)}, f32[8,8,128]{2,1,0:T(8,128)S(1)}) custom-call(bf16[4,8,160,128]{3,2,1,0:T(8,128)(2,1)S(1)} %bitcast.296, f32[4,1024,128]{2,1,0:T(8,128)} %copy-done.72, f32[4,8,8,128]{3,2,1,0:T(8,128)S(1)} %copy-done.27, ...), custom_call_target="tpu_custom_call" | custom-call | flops 46137344000 | bytes 41943040 | tf_op jit(solution)/shard_map/scan_forward/pallas_call | solution.py:455
  326.8 13.4 %lead_product.3 = (f32[32,128,128]{2,1,0:T(8,128)S(1)}, bf16[2048,384]{1,0:T(8,128)(2,1)S(1)}) custom-call(s32[32]{0:T(128)S(1)} %iota.68.places, bf16[32,128,2048]{2,1,0:T(8,128)(2,1)} %bitcast.362, f32[32,8,128]{2,1,0:T(8,128)S(1)} %copy-done.30, bf16[8,3,256,128]{3,2,1,0:T(8,128)(2,1)S(1)} %all-to-all-done.2.weight_ref), custom_call_target="tpu_custom_call" | custom-call | flops 6442450944 | bytes 16777216 | tf_op jit(solution)/shard_map/lead_product/pallas_call | solution.py:113
  341.6 14.0 %trail_product.3 = bf16[32,128,2048]{2,1,0:T(8,128)(2,1)} custom-call(bf16[32,128,128]{2,1,0:T(8,128)(2,1)S(1)} %bitcast.316, f32[32,8,128]{2,1,0:T(8,128)S(1)} %copy-done.30, bf16[2048,384]{1,0:T(8,128)(2,1)S(1)} %get-tuple-element.55.refs_2_), custom_call_target="tpu_custom_call" | custom-call | flops 6442450944 | bytes 16777216 | tf_op jit(solution)/shard_map/trail_product/pallas_call | solution.py:233
  357.8 15.4 %feature_grad.3._ = bf16[8,256,384]{2,1,0:T(8,128)(2,1)S(1)} custom-call(bf16[4096,2048]{1,0:T(8,128)(2,1)} %all-gather.3.cloned.1.call-done.x_ref, bf16[32,128,128]{2,1,0:T(8,128)(2,1)S(1)} %bitcast.317, f32[32,8,128]{2,1,0:T(8,128)S(1)} %copy-done.31), custom_call_target="tpu_custom_call" | custom-call | flops 19327352832 | bytes 16777216 | tf_op jit(solution)/shard_map/feature_grad/pallas_call | solution.py:268
  374.3 5.3 all-to-all-start.3
  384.6 62.4 %scan_backward.1 = (bf16[32,128,128]{2,1,0:T(8,128)(2,1)S(1)}, bf16[4,8,160,128]{3,2,1,0:T(8,128)(2,1)S(1)}, f32[4,1024,128]{2,1,0:T(8,128)}, f32[128,384]{1,0:T...) custom-call(s32[32]{0:T(128)S(1)} %scatter_custom_fusion.tables, ...), custom_call_target="tpu_custom_call" | custom-call | flops 62914560000 | bytes 41943040 | tf_op jit(solution)/shard_map/scan_backward/pallas_call | solution.py:599
  456.4 16.4 %feature_grad.4.refs_1_ = bf16[8,256,384]{2,1,0:T(8,128)(2,1)} custom-call(bf16[4096,2048]{1,0:T(8,128)(2,1)} %bitcast.366, bf16[32,128,128]{2,1,0:T(8,128)(2,1)S(1)} %copy-done.69, f32[32,8,128]{2,1,0:T(8,128)S(1)} %copy-done.37), custom_call_target="tpu_custom_call" | custom-call | flops 19327352832 | bytes 16777216 | tf_op jit(solution)/shard_map/feature_grad/pallas_call | solution.py:268
  474.6 5.4 collective-permute-done.49
  481.6 2.6 collective-permute-start.52
  484.2 3.8 collective-permute-start.51
  488.0 3.0 collective-permute-done.52
  495.5 2.8 collective-permute-start.53
  504.6 4.7 collective-permute-done.56
  510.9 5.5 collective-permute-done.57
  518.1 14.2 %all-to-all-start.4 = ((bf16[8,256,384]{2,1,0:T(8,128)(2,1)}), bf16[8,256,384]{2,1,0:T(8,128)(2,1)S(1)}, u32[]{:S(2)}, u32[]{:S(2)}) async-start(bf16[8,256,384]{2,1,0:T(8,128)(2,1)} %feature_grad.4.refs_1_), calls=%async_computation.5 | async-start | bytes 3145728 | tf_op jit(solution)/shard_map/all_to_all | solution.py:814
  535.6 17.8 %deconv_block.1 = (bf16[32,128,128]{2,1,0:T(8,128)(2,1)S(1)}, f32[128,384]{1,0:T(8,128)S(1)}, f32[96,128]{1,0:T(8,128)S(1)}, f32[4,128]{1,0:T(4,128)}, f32[1,128...) custom-call(s32[32]{0:T(128)S(1)} %scatter_custom_fusion.tables, bf16[4,8,160,128]{3,2,1,0:T(8,128)(2,1)S(1)} %bitcast.301, ...), custom_call_target="tpu_custom_call" | custom-call | flops 15728640000 | bytes 7340032 | tf_op jit(solution)/shard_map/deconv_block/pallas_call | solution.py:684
  553.5 16.8 %feature_grad.5.refs_5_ = bf16[8,256,384]{2,1,0:T(8,128)(2,1)} custom-call(bf16[4096,2048]{1,0:T(8,128)(2,1)} %bitcast.367, bf16[32,128,128]{2,1,0:T(8,128)(2,1)S(1)} %get-tuple-element.64.refs_0_.d_ref, f32[32,8,128]{2,1,0:T(8,128)S(1)} %copy-done.37), custom_call_target="tpu_custom_call" | custom-call | flops 19327352832 | bytes 16777216 | tf_op jit(solution)/shard_map/feature_grad/pallas_call | solution.py:268
  570.3 13.6 %trail_product.5 = (bf16[8,128,2048]{2,1,0:T(8,128)(2,1)}, bf16[8,128,2048]{2,1,0:T(8,128)(2,1)}) custom-call(bf16[32,128,128]{2,1,0:T(8,128)(2,1)S(1)} %get-tuple-element.64.refs_0_.d_ref, bf16[32,128,128]{2,1,0:T(8,128)(2,1)S(1)} %copy-done.69, f32[32,8,128]{2,1,0:T(8,128)S(1)} %copy-done.37, bf16[2048,384]{1,0:T(8,128)(2,1)S(1)} %copy-done.63, ...), custom_call_target="tpu_custom_call" | custom-call | flops 6442450944 | bytes 8388608 | tf_op jit(solution)/shard_map/trail_product/pallas_call | solution.py:233
  584.1 2.4 all-to-all-done.4.refs_5_.got_ref
  591.7 13.5 %trail_product.4 = (bf16[8,128,2048]{2,1,0:T(8,128)(2,1)}, bf16[8,128,2048]{2,1,0:T(8,128)(2,1)}) custom-call(bf16[32,128,128]{2,1,0:T(8,128)(2,1)S(1)} %copy-done.71, bf16[32,128,128]{2,1,0:T(8,128)(2,1)S(1)} %copy-done.69, f32[32,8,128]{2,1,0:T(8,128)S(1)} %copy-done.37, bf16[2048,384]{1,0:T(8,128)(2,1)S(1)} %copy-done.64, ...), custom_call_target="tpu_custom_call" | custom-call | flops 6442450944 | bytes 8388608 | tf_op jit(solution)/shard_map/trail_product/pallas_call | solution.py:233
  605.5 2.7 add_convert_fusion
  609.4 3.5 collective-permute-done.59
  616.0 18.2 %collective-permute-done.65 = bf16[2,2,128,2048]{3,2,0,1:T(8,128)(2,1)S(1)} collective-permute-done((bf16[2,2,128,2048]{3,2,0,1:T(8,128)(2,1)S(1)}, bf16[2,2,128,2048]{3,2,0,1:T(8,128)(2,1)S(1)}, u32[]{:S(2)}, u32[]{:S(2)}) %collective-permute-start.65) | collective-permute-done | bytes 2097184 | tf_op jit(solution)/shard_map/ppermute | solution.py:733
  634.2 3.5 fusion.13
  637.8 7.5 %all-to-all-start.5 = ((bf16[8,256,384]{2,1,0:T(8,128)(2,1)}), bf16[8,256,384]{2,1,0:T(8,128)(2,1)}, u32[]{:S(2)}, u32[]{:S(2)}) async-start(bf16[8,256,384]{2,1,0:T(8,128)(2,1)} %feature_grad.5.refs_5_), calls=%async_computation.6 | async-start | bytes 3145728 | tf_op jit(solution)/shard_map/all_to_all | solution.py:814
  645.3 22.7 %collective-permute-done.60 = bf16[2,2,128,2048]{3,2,0,1:T(8,128)(2,1)} collective-permute-done((bf16[2,2,128,2048]{3,2,0,1:T(8,128)(2,1)S(1)}, bf16[2,2,128,2048]{3,2,0,1:T(8,128)(2,1)}, u32[]{:S(2)}, u32[]{:S(2)}) %collective-permute-start.60) | collective-permute-done | bytes 2097184 | tf_op jit(solution)/shard_map/ppermute | solution.py:733
  668.1 2.4 fusion.12
  670.6 2.2 bitcast_add_fusion
  674.9 10.4 %collective-permute-done.61 = bf16[2,128,2048]{2,1,0:T(8,128)(2,1)S(1)} collective-permute-done((bf16[2,128,2048]{2,1,0:T(8,128)(2,1)S(1)}, bf16[2,128,2048]{2,1,0:T(8,128)(2,1)S(1)}, u32[]{:S(2)}, u32[]{:S(2)}) %collective-permute-start.61) | collective-permute-done | bytes 1048608 | tf_op jit(solution)/shard_map/ppermute | solution.py:733
  685.4 2.7 fusion
  689.2 3.1 collective-permute-start.62
  692.4 3.7 settle.4
  696.2 6.1 settle.3
  711.4 3.7 settle.5
  717.3 8.4 %collective-permute-done.63 = bf16[128,2048]{1,0:T(8,128)(2,1)} collective-permute-done((bf16[128,2048]{1,0:T(8,128)(2,1)}, bf16[128,2048]{1,0:T(8,128)(2,1)}, u32[]{:S(2)}, u32[]{:S(2)}) %collective-permute-start.63) | collective-permute-done | bytes 524320 | tf_op jit(solution)/shard_map/ppermute | solution.py:713
  727.9 3.6 fusion.20
  (495 shorter events, 156.1 us)
Async XLA Ops:
  8.7 6.8 collective-permute-start.2
  8.7 6.8 collective-permute-start.1
  19.3 14.9 %collective-permute-start.4 = (bf16[128,2048]{1,0:T(8,128)(2,1)S(1)}, bf16[128,2048]{1,0:T(8,128)(2,1)S(1)}, u32[]{:S(2)}, u32[]{:S(2)}) collective-permute-start(bf16[128,2048]{1,0:T(8,128)(2,1)S(1)} %fusion.6.refs_0_), channel_id=1, source_target_pairs={{0,2},{2,4},{4,6},{6,0},{1,3},{3,5},{5,7},{7,1},{8,10},{10,12},{12... | collective-permute-start | bytes 1572872 | tf_op jit(solution)/shard_map/ppermute | solution.py:713
  35.1 89.1 %all-to-all-start = ((bf16[8,3,256,128]{3,2,1,0:T(8,128)(2,1)}), bf16[8,3,256,128]{3,2,1,0:T(8,128)(2,1)}, u32[]{:S(2)}, u32[]{:S(2)}) async-start(bf16[8,3,256,128]{3,2,1,0:T(8,128)(2,1)} %tied.11), calls=%async_computation | async-start | bytes 3145728 | tf_op jit(solution)/shard_map/all_to_all | solution.py:814
  42.8 283.1 %all-gather.3.cloned.1.call-start = ((), (), s32[]{:S(2)}) async-start(), calls=%async_computation.8 | async-start | bytes 17301504 | tf_op jit(solution)/shard_map/all_gather | solution.py:967
  42.8 14.5 %collective-permute-start.5 = (bf16[128,2048]{1,0:T(8,128)(2,1)S(1)}, bf16[128,2048]{1,0:T(8,128)(2,1)S(1)}, u32[]{:S(2)}, u32[]{:S(2)}) collective-permute-start(bf16[128,2048]{1,0:T(8,128)(2,1)S(1)} %fusion.6.refs_0_), channel_id=1, source_target_pairs={{0,8},{1,17},{2,10},{3,19},{4,12},{5,21},{6,14},{7,23},{8,0},{9,25... | collective-permute-start | bytes 1572872 | tf_op jit(solution)/shard_map/ppermute | solution.py:733
  44.3 14.2 %collective-permute-start.6 = (bf16[128,2048]{1,0:T(8,128)(2,1)S(1)}, bf16[128,2048]{1,0:T(8,128)(2,1)S(1)}, u32[]{:S(2)}, u32[]{:S(2)}) collective-permute-start(bf16[128,2048]{1,0:T(8,128)(2,1)S(1)} %fusion.6.refs_0_), channel_id=1, source_target_pairs={{0,16},{1,9},{2,18},{3,11},{4,20},{5,13},{6,22},{7,15},{8,24},{9,1... | collective-permute-start | bytes 1572872 | tf_op jit(solution)/shard_map/ppermute | solution.py:733
  45.8 56.3 %collective-permute-start.20 = (bf16[128,2048]{1,0:T(8,128)(2,1)S(1)}, bf16[128,2048]{1,0:T(8,128)(2,1)S(1)}, u32[]{:S(2)}, u32[]{:S(2)}) collective-permute-start(bf16[128,2048]{1,0:T(8,128)(2,1)S(1)} %fusion.6.refs_0_), channel_id=1, source_target_pairs={{0,6},{2,0},{4,2},{6,4},{1,7},{3,1},{5,3},{7,5},{8,14},{10,8},{12,... | collective-permute-start | bytes 1572872 | tf_op jit(solution)/shard_map/ppermute | solution.py:713
  57.3 44.9 %collective-permute-start.7 = (bf16[128,2048]{1,0:T(8,128)(2,1)S(1)}, bf16[128,2048]{1,0:T(8,128)(2,1)S(1)}, u32[]{:S(2)}, u32[]{:S(2)}) collective-permute-start(bf16[128,2048]{1,0:T(8,128)(2,1)S(1)} %collective-permute-done.5.refs_1_), channel_id=1, source_target_pairs={{0,16},{1,9},{2,18},{3,11},{4,20},{5,13},{6,22},{7,15},{8,24},{9,1... | collective-permute-start | bytes 1572872 | tf_op jit(solution)/shard_map/ppermute | solution.py:733
  59.3 42.9 %collective-permute-start.13 = (bf16[128,2048]{1,0:T(8,128)(2,1)}, bf16[128,2048]{1,0:T(8,128)(2,1)S(1)}, u32[]{:S(2)}, u32[]{:S(2)}) collective-permute-start(bf16[128,2048]{1,0:T(8,128)(2,1)} %tied.12.refs_8_), channel_id=1, source_target_pairs={{0,16},{1,9},{2,18},{3,11},{4,20},{5,13},{6,22},{7,15},{8,24},{9,1... | collective-permute-start | bytes 1572872 | tf_op jit(solution)/shard_map/ppermute | solution.py:733
  60.1 42.1 %collective-permute-start.12 = (bf16[128,2048]{1,0:T(8,128)(2,1)}, bf16[128,2048]{1,0:T(8,128)(2,1)S(1)}, u32[]{:S(2)}, u32[]{:S(2)}) collective-permute-start(bf16[128,2048]{1,0:T(8,128)(2,1)} %tied.12.refs_8_), channel_id=1, source_target_pairs={{0,8},{1,17},{2,10},{3,19},{4,12},{5,21},{6,14},{7,23},{8,0},{9,25... | collective-permute-start | bytes 1572872 | tf_op jit(solution)/shard_map/ppermute | solution.py:733
  62.4 48.4 %collective-permute-start.19 = (bf16[128,2048]{1,0:T(8,128)(2,1)}, bf16[128,2048]{1,0:T(8,128)(2,1)}, u32[]{:S(2)}, u32[]{:S(2)}) collective-permute-start(bf16[128,2048]{1,0:T(8,128)(2,1)} %tied.13), channel_id=1, source_target_pairs={{0,4},{2,6},{4,0},{6,2},{1,5},{3,7},{5,1},{7,3},{8,12},{10,14},{12... | collective-permute-start | bytes 1572872 | tf_op jit(solution)/shard_map/ppermute | solution.py:713
  104.1 14.4 %collective-permute-start.22 = (bf16[128,2048]{1,0:T(8,128)(2,1)}, bf16[128,2048]{1,0:T(8,128)(2,1)S(1)}, u32[]{:S(2)}, u32[]{:S(2)}) collective-permute-start(bf16[128,2048]{1,0:T(8,128)(2,1)} %tied.14.refs_24_), channel_id=1, source_target_pairs={{0,16},{1,9},{2,18},{3,11},{4,20},{5,13},{6,22},{7,15},{8,24},{9,1... | collective-permute-start | bytes 1572872 | tf_op jit(solution)/shard_map/ppermute | solution.py:733
  105.7 15.1 %collective-permute-start.21 = (bf16[128,2048]{1,0:T(8,128)(2,1)}, bf16[128,2048]{1,0:T(8,128)(2,1)S(1)}, u32[]{:S(2)}, u32[]{:S(2)}) collective-permute-start(bf16[128,2048]{1,0:T(8,128)(2,1)} %tied.14.refs_24_), channel_id=1, source_target_pairs={{0,8},{1,17},{2,10},{3,19},{4,12},{5,21},{6,14},{7,23},{8,0},{9,25... | collective-permute-start | bytes 1572872 | tf_op jit(solution)/shard_map/ppermute | solution.py:733
  107.1 17.0 %collective-permute-start.14 = (bf16[128,2048]{1,0:T(8,128)(2,1)}, bf16[128,2048]{1,0:T(8,128)(2,1)S(1)}, u32[]{:S(2)}, u32[]{:S(2)}) collective-permute-start(bf16[128,2048]{1,0:T(8,128)(2,1)} %copy-done.24), channel_id=1, source_target_pairs={{0,16},{1,9},{2,18},{3,11},{4,20},{5,13},{6,22},{7,15},{8,24},{9,1... | collective-permute-start | bytes 1572872 | tf_op jit(solution)/shard_map/ppermute | solution.py:733
  125.0 15.1 %collective-permute-start.23 = (bf16[128,2048]{1,0:T(8,128)(2,1)}, bf16[128,2048]{1,0:T(8,128)(2,1)}, u32[]{:S(2)}, u32[]{:S(2)}) collective-permute-start(bf16[128,2048]{1,0:T(8,128)(2,1)} %tied.15.refs_16_), channel_id=1, source_target_pairs={{0,8},{1,17},{2,10},{3,19},{4,12},{5,21},{6,14},{7,23},{8,0},{9,25... | collective-permute-start | bytes 1572872 | tf_op jit(solution)/shard_map/ppermute | solution.py:733
  126.1 17.2 %collective-permute-start.30 = (bf16[128,2048]{1,0:T(8,128)(2,1)}, bf16[128,2048]{1,0:T(8,128)(2,1)S(1)}, u32[]{:S(2)}, u32[]{:S(2)}) collective-permute-start(bf16[128,2048]{1,0:T(8,128)(2,1)} %copy-done.90), channel_id=1, source_target_pairs={{0,16},{1,9},{2,18},{3,11},{4,20},{5,13},{6,22},{7,15},{8,24},{9,1... | collective-permute-start | bytes 1572872 | tf_op jit(solution)/shard_map/ppermute | solution.py:733
  127.6 16.0 %collective-permute-start.24 = (bf16[128,2048]{1,0:T(8,128)(2,1)}, bf16[128,2048]{1,0:T(8,128)(2,1)}, u32[]{:S(2)}, u32[]{:S(2)}) collective-permute-start(bf16[128,2048]{1,0:T(8,128)(2,1)} %tied.15.refs_16_), channel_id=1, source_target_pairs={{0,16},{1,9},{2,18},{3,11},{4,20},{5,13},{6,22},{7,15},{8,24},{9,1... | collective-permute-start | bytes 1572872 | tf_op jit(solution)/shard_map/ppermute | solution.py:733
  140.1 9.5 %collective-permute-start.25 = (bf16[128,2048]{1,0:T(8,128)(2,1)}, bf16[128,2048]{1,0:T(8,128)(2,1)}, u32[]{:S(2)}, u32[]{:S(2)}) collective-permute-start(bf16[128,2048]{1,0:T(8,128)(2,1)} %collective-permute-done.23.refs_17_), channel_id=1, source_target_pairs={{0,16},{1,9},{2,18},{3,11},{4,20},{5,13},{6,22},{7,15},{8,24},{9,1... | collective-permute-start | bytes 1572872 | tf_op jit(solution)/shard_map/ppermute | solution.py:733
  151.7 68.0 %all-to-all-start.1 = ((bf16[8,3,256,128]{3,2,1,0:T(8,128)(2,1)}), bf16[8,3,256,128]{3,2,1,0:T(8,128)(2,1)}, u32[]{:S(2)}, u32[]{:S(2)}) async-start(bf16[8,3,256,128]{3,2,1,0:T(8,128)(2,1)} %bitcast.321), calls=%async_computation.1 | async-start | bytes 3145728 | tf_op jit(solution)/shard_map/all_to_all | solution.py:814
  158.0 4.3 collective-permute-start.15
  162.6 4.0 collective-permute-start.32
  163.3 4.0 collective-permute-start.18
  165.5 8.6 %collective-permute-start.34 = (bf16[128,2048]{1,0:T(8,128)(2,1)}, bf16[128,2048]{1,0:T(8,128)(2,1)}, u32[]{:S(2)}, u32[]{:S(2)}) collective-permute-start(bf16[128,2048]{1,0:T(8,128)(2,1)} %copy-done.87), channel_id=1, source_target_pairs={{0,1},{1,0},{2,3},{3,2},{4,5},{5,4},{6,7},{7,6},{8,9},{9,8},{10,11... | collective-permute-start | bytes 1572872 | tf_op jit(solution)/shard_map/ppermute | solution.py:717
  165.7 8.5 %collective-permute-start.26 = (bf16[128,2048]{1,0:T(8,128)(2,1)}, bf16[128,2048]{1,0:T(8,128)(2,1)}, u32[]{:S(2)}, u32[]{:S(2)}) collective-permute-start(bf16[128,2048]{1,0:T(8,128)(2,1)} %tied.15.refs_16_), channel_id=1, source_target_pairs={{0,1},{1,0},{2,3},{3,2},{4,5},{5,4},{6,7},{7,6},{8,9},{9,8},{10,11... | collective-permute-start | bytes 1572872 | tf_op jit(solution)/shard_map/ppermute | solution.py:717
  166.1 8.1 %collective-permute-start.28 = (bf16[128,2048]{1,0:T(8,128)(2,1)}, bf16[128,2048]{1,0:T(8,128)(2,1)}, u32[]{:S(2)}, u32[]{:S(2)}) collective-permute-start(bf16[128,2048]{1,0:T(8,128)(2,1)} %collective-permute-done.24.refs_18_.refs_2_), channel_id=1, source_target_pairs={{0,1},{1,0},{2,3},{3,2},{4,5},{5,4},{6,7},{7,6},{8,9},{9,8},{10,11... | collective-permute-start | bytes 1572872 | tf_op jit(solution)/shard_map/ppermute | solution.py:717
  166.5 7.6 %collective-permute-start.27 = (bf16[128,2048]{1,0:T(8,128)(2,1)}, bf16[128,2048]{1,0:T(8,128)(2,1)}, u32[]{:S(2)}, u32[]{:S(2)}) collective-permute-start(bf16[128,2048]{1,0:T(8,128)(2,1)} %collective-permute-done.23.refs_17_), channel_id=1, source_target_pairs={{0,1},{1,0},{2,3},{3,2},{4,5},{5,4},{6,7},{7,6},{8,9},{9,8},{10,11... | collective-permute-start | bytes 1572872 | tf_op jit(solution)/shard_map/ppermute | solution.py:717
  167.3 6.9 collective-permute-start.29
  206.2 9.8 %collective-permute-start.36 = (bf16[2,4,160,128]{3,2,1,0:T(8,128)(2,1)S(1)}, bf16[2,4,160,128]{3,2,1,0:T(8,128)(2,1)S(1)}, u32[]{:S(2)}, u32[]{:S(2)}) collective-permute-start(bf16[2,4,160,128]{3,2,1,0:T(8,128)(2,1)S(1)} %fusion.21), channel_id=1, source_target_pairs={{0,16},{16,0},{1,17},{17,1},{2,18},{18,2},{3,19},{19,3},{4,20},{20... | collective-permute-start | bytes 983048 | tf_op jit(solution)/shard_map/ppermute | solution.py:871
  216.8 19.4 %collective-permute-start.37 = (bf16[4,160,128]{2,1,0:T(8,128)(2,1)}, bf16[4,160,128]{2,1,0:T(8,128)(2,1)S(1)}, u32[]{:S(2)}, u32[]{:S(2)}) collective-permute-start(bf16[4,160,128]{2,1,0:T(8,128)(2,1)} %tied.16), channel_id=1, source_target_pairs={{0,8},{8,0},{1,9},{9,1},{2,10},{10,2},{3,11},{11,3},{4,12},{12,4},... | collective-permute-start | bytes 491528 | tf_op jit(solution)/shard_map/ppermute | solution.py:871
  238.1 8.5 %collective-permute-start.38 = (bf16[160,128]{1,0:T(8,128)(2,1)S(1)}, bf16[160,128]{1,0:T(8,128)(2,1)S(1)}, u32[]{:S(2)}, u32[]{:S(2)}) collective-permute-start(bf16[160,128]{1,0:T(8,128)(2,1)S(1)} %get-tuple-element.159), channel_id=1, source_target_pairs={{0,2},{2,4},{4,6},{6,0},{1,3},{3,5},{5,7},{7,1},{8,10},{10,12},{12... | collective-permute-start | bytes 122888 | tf_op jit(solution)/shard_map/ppermute | solution.py:713
  241.7 8.5 %collective-permute-start.40 = (bf16[160,128]{1,0:T(8,128)(2,1)S(1)}, bf16[160,128]{1,0:T(8,128)(2,1)S(1)}, u32[]{:S(2)}, u32[]{:S(2)}) collective-permute-start(bf16[160,128]{1,0:T(8,128)(2,1)S(1)} %get-tuple-element.160), channel_id=1, source_target_pairs={{0,6},{2,0},{4,2},{6,4},{1,7},{3,1},{5,3},{7,5},{8,14},{10,8},{12,... | collective-permute-start | bytes 122888 | tf_op jit(solution)/shard_map/ppermute | solution.py:713
  244.2 7.9 %collective-permute-start.39 = (bf16[160,128]{1,0:T(8,128)(2,1)S(1)}, bf16[160,128]{1,0:T(8,128)(2,1)S(1)}, u32[]{:S(2)}, u32[]{:S(2)}) collective-permute-start(bf16[160,128]{1,0:T(8,128)(2,1)S(1)} %get-tuple-element.161), channel_id=1, source_target_pairs={{0,4},{2,6},{4,0},{6,2},{1,5},{3,7},{5,1},{7,3},{8,12},{10,14},{12... | collective-permute-start | bytes 122888 | tf_op jit(solution)/shard_map/ppermute | solution.py:713
  253.0 7.9 %collective-permute-start.43 = (bf16[160,128]{1,0:T(8,128)(2,1)S(1)}, bf16[160,128]{1,0:T(8,128)(2,1)S(1)}, u32[]{:S(2)}, u32[]{:S(2)}) collective-permute-start(bf16[160,128]{1,0:T(8,128)(2,1)S(1)} %fusion.30), channel_id=1, source_target_pairs={{0,6},{2,0},{4,2},{6,4},{1,7},{3,1},{5,3},{7,5},{8,14},{10,8},{12,... | collective-permute-start | bytes 122888 | tf_op jit(solution)/shard_map/ppermute | solution.py:713
  257.1 5.7 collective-permute-start.42
  257.1 6.3 collective-permute-start.41
  264.1 5.5 collective-permute-start.44
  270.5 7.1 collective-permute-start.45
  281.4 44.5 %all-to-all-start.2 = ((bf16[8,3,256,128]{3,2,1,0:T(8,128)(2,1)}), bf16[8,3,256,128]{3,2,1,0:T(8,128)(2,1)S(1)}, u32[]{:S(2)}, u32[]{:S(2)}) async-start(bf16[8,3,256,128]{3,2,1,0:T(8,128)(2,1)} %tied.19), calls=%async_computation.2 | async-start | bytes 3145728 | tf_op jit(solution)/shard_map/all_to_all | solution.py:814
  289.2 438.7 %reduce-scatter.2.cloned.1.call-start = ((), (), s32[]{:S(2)}) async-start(), calls=%async_computation.7 | async-start | bytes 17301504 | tf_op jit(solution)/shard_map/reduce_scatter | solution.py:1042
  374.3 76.0 %all-to-all-start.3 = ((bf16[8,256,384]{2,1,0:T(8,128)(2,1)}), bf16[8,256,384]{2,1,0:T(8,128)(2,1)S(1)}, u32[]{:S(2)}, u32[]{:S(2)}) async-start(bf16[8,256,384]{2,1,0:T(8,128)(2,1)} %copy-done.19), calls=%async_computation.4 | async-start | bytes 3145728 | tf_op jit(solution)/shard_map/all_to_all | solution.py:814
  456.3 16.5 %collective-permute-start.48 = (bf16[2,4,160,128]{3,2,1,0:T(8,128)(2,1)S(1)}, bf16[2,4,160,128]{3,2,1,0:T(8,128)(2,1)S(1)}, u32[]{:S(2)}, u32[]{:S(2)}) collective-permute-start(bf16[2,4,160,128]{3,2,1,0:T(8,128)(2,1)S(1)} %fusion.22), channel_id=1, source_target_pairs={{0,16},{16,0},{1,17},{17,1},{2,18},{18,2},{3,19},{19,3},{4,20},{20... | collective-permute-start | bytes 983048 | tf_op jit(solution)/shard_map/ppermute | solution.py:871
  473.5 6.5 collective-permute-start.49
  480.1 7.9 %collective-permute-start.50 = (bf16[160,128]{1,0:T(8,128)(2,1)S(1)}, bf16[160,128]{1,0:T(8,128)(2,1)S(1)}, u32[]{:S(2)}, u32[]{:S(2)}) collective-permute-start(bf16[160,128]{1,0:T(8,128)(2,1)S(1)} %get-tuple-element.154), channel_id=1, source_target_pairs={{0,2},{2,4},{4,6},{6,0},{1,3},{3,5},{5,7},{7,1},{8,10},{10,12},{12... | collective-permute-start | bytes 122888 | tf_op jit(solution)/shard_map/ppermute | solution.py:713
  481.6 9.4 %collective-permute-start.52 = (bf16[160,128]{1,0:T(8,128)(2,1)S(1)}, bf16[160,128]{1,0:T(8,128)(2,1)S(1)}, u32[]{:S(2)}, u32[]{:S(2)}) collective-permute-start(bf16[160,128]{1,0:T(8,128)(2,1)S(1)} %get-tuple-element.155), channel_id=1, source_target_pairs={{0,6},{2,0},{4,2},{6,4},{1,7},{3,1},{5,3},{7,5},{8,14},{10,8},{12,... | collective-permute-start | bytes 122888 | tf_op jit(solution)/shard_map/ppermute | solution.py:713
  484.2 8.7 %collective-permute-start.51 = (bf16[160,128]{1,0:T(8,128)(2,1)S(1)}, bf16[160,128]{1,0:T(8,128)(2,1)S(1)}, u32[]{:S(2)}, u32[]{:S(2)}) collective-permute-start(bf16[160,128]{1,0:T(8,128)(2,1)S(1)} %get-tuple-element.156), channel_id=1, source_target_pairs={{0,4},{2,6},{4,0},{6,2},{1,5},{3,7},{5,1},{7,3},{8,12},{10,14},{12... | collective-permute-start | bytes 122888 | tf_op jit(solution)/shard_map/ppermute | solution.py:713
  492.9 6.2 collective-permute-start.55
  494.9 6.2 collective-permute-start.54
  495.5 7.6 %collective-permute-start.53 = (bf16[160,128]{1,0:T(8,128)(2,1)S(1)}, bf16[160,128]{1,0:T(8,128)(2,1)S(1)}, u32[]{:S(2)}, u32[]{:S(2)}) collective-permute-start(bf16[160,128]{1,0:T(8,128)(2,1)S(1)} %fusion.27), channel_id=1, source_target_pairs={{0,2},{2,4},{4,6},{6,0},{1,3},{3,5},{5,7},{7,1},{8,10},{10,12},{12... | collective-permute-start | bytes 122888 | tf_op jit(solution)/shard_map/ppermute | solution.py:713
  503.8 5.4 collective-permute-start.56
  509.3 7.1 collective-permute-start.57
  518.1 14.2 %collective-permute-start.58 = (bf16[2,2,4,160,128]{4,3,2,1,0:T(8,128)(2,1)}, bf16[2,2,4,160,128]{4,3,2,1,0:T(8,128)(2,1)}, u32[]{:S(2)}, u32[]{:S(2)}) collective-permute-start(bf16[2,2,4,160,128]{4,3,2,1,0:T(8,128)(2,1)} %pad_maximum_fusion.3), channel_id=1, source_target_pairs={{0,1},{1,0},{2,3},{3,2},{4,5},{5,4},{6,7},{7,6},{8,9},{9,8},{10,11... | collective-permute-start | bytes 1966088 | tf_op jit(solution)/shard_map/ppermute | solution.py:888
  518.1 68.4 %all-to-all-start.4 = ((bf16[8,256,384]{2,1,0:T(8,128)(2,1)}), bf16[8,256,384]{2,1,0:T(8,128)(2,1)S(1)}, u32[]{:S(2)}, u32[]{:S(2)}) async-start(bf16[8,256,384]{2,1,0:T(8,128)(2,1)} %feature_grad.4.refs_1_), calls=%async_computation.5 | async-start | bytes 3145728 | tf_op jit(solution)/shard_map/all_to_all | solution.py:814
  583.9 21.6 %collective-permute-start.64 = (bf16[8,128,2048]{2,1,0:T(8,128)(2,1)}, bf16[8,128,2048]{2,1,0:T(8,128)(2,1)}, u32[]{:S(2)}, u32[]{:S(2)}) collective-permute-start(bf16[8,128,2048]{2,1,0:T(8,128)(2,1)} %get-tuple-element.70), channel_id=1, source_target_pairs={{0,1},{1,0},{2,3},{3,2},{4,5},{5,4},{6,7},{7,6},{8,9},{9,8},{10,11... | collective-permute-start | bytes 12582920 | tf_op jit(solution)/shard_map/ppermute | solution.py:717
  605.3 7.7 %collective-permute-start.59 = (bf16[8,128,2048]{2,1,0:T(8,128)(2,1)}, bf16[8,128,2048]{2,1,0:T(8,128)(2,1)S(1)}, u32[]{:S(2)}, u32[]{:S(2)}) collective-permute-start(bf16[8,128,2048]{2,1,0:T(8,128)(2,1)} %get-tuple-element.68), channel_id=1, source_target_pairs={{0,1},{1,0},{2,3},{3,2},{4,5},{5,4},{6,7},{7,6},{8,9},{9,8},{10,11... | collective-permute-start | bytes 12582920 | tf_op jit(solution)/shard_map/ppermute | solution.py:717
  608.1 26.1 %collective-permute-start.65 = (bf16[2,2,128,2048]{3,2,0,1:T(8,128)(2,1)S(1)}, bf16[2,2,128,2048]{3,2,0,1:T(8,128)(2,1)S(1)}, u32[]{:S(2)}, u32[]{:S(2)}) collective-permute-start(bf16[2,2,128,2048]{3,2,0,1:T(8,128)(2,1)S(1)} %add_convert_fusion), channel_id=1, source_target_pairs={{0,16},{1,9},{2,18},{3,11},{4,20},{5,13},{6,22},{7,15},{8,24},{9,1... | collective-permute-start | bytes 6291464 | tf_op jit(solution)/shard_map/ppermute | solution.py:733
  615.1 53.0 %collective-permute-start.60 = (bf16[2,2,128,2048]{3,2,0,1:T(8,128)(2,1)S(1)}, bf16[2,2,128,2048]{3,2,0,1:T(8,128)(2,1)}, u32[]{:S(2)}, u32[]{:S(2)}) collective-permute-start(bf16[2,2,128,2048]{3,2,0,1:T(8,128)(2,1)S(1)} %add_convert_fusion.1), channel_id=1, source_target_pairs={{0,16},{1,9},{2,18},{3,11},{4,20},{5,13},{6,22},{7,15},{8,24},{9,1... | collective-permute-start | bytes 6291464 | tf_op jit(solution)/shard_map/ppermute | solution.py:733
  637.8 32.8 %collective-permute-start.66 = (bf16[2,128,2048]{2,1,0:T(8,128)(2,1)}, bf16[2,128,2048]{2,1,0:T(8,128)(2,1)S(1)}, u32[]{:S(2)}, u32[]{:S(2)}) collective-permute-start(bf16[2,128,2048]{2,1,0:T(8,128)(2,1)} %fusion.13), channel_id=1, source_target_pairs={{0,8},{1,17},{2,10},{3,19},{4,12},{5,21},{6,14},{7,23},{8,0},{9,25... | collective-permute-start | bytes 3145736 | tf_op jit(solution)/shard_map/ppermute | solution.py:733
  637.8 58.4 %all-to-all-start.5 = ((bf16[8,256,384]{2,1,0:T(8,128)(2,1)}), bf16[8,256,384]{2,1,0:T(8,128)(2,1)}, u32[]{:S(2)}, u32[]{:S(2)}) async-start(bf16[8,256,384]{2,1,0:T(8,128)(2,1)} %feature_grad.5.refs_5_), calls=%async_computation.6 | async-start | bytes 3145728 | tf_op jit(solution)/shard_map/all_to_all | solution.py:814
  670.5 14.9 %collective-permute-start.61 = (bf16[2,128,2048]{2,1,0:T(8,128)(2,1)S(1)}, bf16[2,128,2048]{2,1,0:T(8,128)(2,1)S(1)}, u32[]{:S(2)}, u32[]{:S(2)}) collective-permute-start(bf16[2,128,2048]{2,1,0:T(8,128)(2,1)S(1)} %fusion.12), channel_id=1, source_target_pairs={{0,8},{1,17},{2,10},{3,19},{4,12},{5,21},{6,14},{7,23},{8,0},{9,25... | collective-permute-start | bytes 3145736 | tf_op jit(solution)/shard_map/ppermute | solution.py:733
  673.7 43.6 %collective-permute-start.67 = (bf16[128,2048]{1,0:T(8,128)(2,1)}, bf16[128,2048]{1,0:T(8,128)(2,1)}, u32[]{:S(2)}, u32[]{:S(2)}) collective-permute-start(bf16[128,2048]{1,0:T(8,128)(2,1)} %fusion.18), channel_id=1, source_target_pairs={{0,2},{2,4},{4,6},{6,0},{1,3},{3,5},{5,7},{7,1},{8,10},{10,12},{12... | collective-permute-start | bytes 1572872 | tf_op jit(solution)/shard_map/ppermute | solution.py:713
  689.2 28.1 %collective-permute-start.62 = (bf16[128,2048]{1,0:T(8,128)(2,1)}, bf16[128,2048]{1,0:T(8,128)(2,1)}, u32[]{:S(2)}, u32[]{:S(2)}) collective-permute-start(bf16[128,2048]{1,0:T(8,128)(2,1)} %get-tuple-element.144), channel_id=1, source_target_pairs={{0,6},{2,0},{4,2},{6,4},{1,7},{3,1},{5,3},{7,5},{8,14},{10,8},{12,... | collective-permute-start | bytes 1572872 | tf_op jit(solution)/shard_map/ppermute | solution.py:713
  692.3 33.4 %collective-permute-start.63 = (bf16[128,2048]{1,0:T(8,128)(2,1)}, bf16[128,2048]{1,0:T(8,128)(2,1)}, u32[]{:S(2)}, u32[]{:S(2)}) collective-permute-start(bf16[128,2048]{1,0:T(8,128)(2,1)} %get-tuple-element.145), channel_id=1, source_target_pairs={{0,4},{2,6},{4,0},{6,2},{1,5},{3,7},{5,1},{7,3},{8,12},{10,14},{12... | collective-permute-start | bytes 1572872 | tf_op jit(solution)/shard_map/ppermute | solution.py:713
  707.6 9.1 %collective-permute-start.69 = (f32[256]{0:T(256)S(1)}, f32[256]{0:T(256)S(1)}, u32[]{:S(2)}, u32[]{:S(2)}) collective-permute-start(f32[256]{0:T(256)S(1)} %add.540), channel_id=1, source_target_pairs={{0,8},{8,0},{1,9},{9,1},{2,10},{10,2},{3,11},{11,3},{4,12},{12,4},... | collective-permute-start | bytes 3080 | tf_op jit(solution)/shard_map/ppermute | solution.py:1101
  (129 other events, 894.4 us)
Sparse Core Ops, SparseCore 0:
  149.7 136.4 all-gather.2
  355.8 258.5 reduce-scatter.1
